TPU v7x, 32 devices: a whole 2x2x4 slice. The times are simulated.
32 devices in a mesh: energy: 8 (over z, x), mom: 4 (over y, core).
Axes of the slice: x: 2, y: 2, z: 4, core: 2. Of those that a mesh axis runs over, the one named last changes fastest.
Arguments:
- green: bfloat16 [4, 16, 16, 2048], P('mom', 'energy'), may hold values from -6 to 6
- coupling: float32 [4, 6, 9, 5, 16], P('mom'), may hold values from -0.12 to 0.12
- gradient: bfloat16 [5, 3, 16, 1024], replicated, may hold values from -1 to 1
- neighbours: int32 [16, 5], replicated, may hold values from 0 to 15, as said below
- offsets: int32 [3], replicated, may hold values from 1 to 4, as said below
Outputs:
- sigma: float32 [16, 16, 2048], P('energy', 'mom')
Inputs may be any that keep to these rules, and one draw needn't show every extreme that they name: `neighbours`: each row names 5 different atoms, none of them the row's own atom. `offsets`: one offset is at most 2 and one equals 4.
All inputs are finite; a program needn't handle non-finite values.
Results may differ from a plain program's by a relative error of at most 0.012.
Values may be sent and summed in bfloat16 or wider, within the bound.
No kernel may reach another device: no remote copies, remote signals or barrier semaphores. Data moves between devices by JAX's collectives and lax.ppermute only.
A program may use at most 64 MiB of HBM per device.

v0:
```python
import jax
import jax.numpy as jnp
from jax import lax
from jax.sharding import PartitionSpec as P

NO = 32
NB = 5
NW = 3


def shifted_2(array, axis, by):
    length = lax.axis_size(axis)
    pairs = [(i, i + by) for i in range(length) if 0 <= i + by < length]
    return lax.ppermute(array, axis, pairs)


def shifted_stack(window, offsets, count, margin):
    pieces = []
    for phonon in range(NW):
        for direction in (1, -1):
            start = margin - direction * offsets[phonon]
            pieces.append(lax.dynamic_slice_in_dim(window, start, count, 0))
    return jnp.stack(pieces, 0)


def sandwich(shifted, weights, gradient, neighbours):
    count = shifted.shape[1]
    natoms = shifted.shape[2]
    blocks = shifted.reshape(2 * NW, count, natoms, 2, NO, NO)

    def one_slot(total, slot):
        table = lax.dynamic_index_in_dim(weights, slot, 2, keepdims=False).reshape(
            2 * NW, 3, 3, natoms
        )
        derivs = lax.dynamic_index_in_dim(gradient, slot, 0, keepdims=False).reshape(
            3, natoms, NO, NO
        )
        kernel = jnp.einsum("sija,janl->aslin", table, derivs.astype(jnp.float32)).astype(
            jnp.bfloat16
        )
        column = lax.dynamic_index_in_dim(neighbours, slot, 1, keepdims=False)
        gathered = jnp.take(blocks, column, axis=2)
        middle = jnp.einsum(
            "seacml,aslin->aiecmn", gathered, kernel, preferred_element_type=jnp.float32
        ).astype(jnp.bfloat16)
        total = total + jnp.einsum(
            "iapm,aiecmn->eacpn", derivs, middle, preferred_element_type=jnp.float32
        )
        return (total, None)

    start_total = jnp.zeros((count, natoms, 2, NO, NO), jnp.float32)
    total, _ = lax.scan(one_slot, start_total, jnp.arange(NB, dtype=jnp.int32))
    return total


def body(green, coupling, gradient, neighbours, offsets):
    local_block = green[0]
    count = local_block.shape[0]
    natoms = local_block.shape[1]
    below_first = shifted_2(local_block, "energy", 1)
    below_second = shifted_2(local_block, "energy", 2)
    above_first = shifted_2(local_block, "energy", -1)
    above_second = shifted_2(local_block, "energy", -2)
    window = jnp.concatenate(
        [below_second, below_first, local_block, above_first, above_second], axis=0
    )
    shifted = shifted_stack(window, offsets, count, 2 * count)
    partial_terms = sandwich(shifted, coupling[0], gradient, neighbours).reshape(
        count, natoms, 2 * NO * NO
    )
    summed = lax.psum(partial_terms, "mom")
    share = natoms // lax.axis_size("mom")
    start = lax.axis_index("mom") * share
    return lax.dynamic_slice_in_dim(summed, start, share, 1)


def solution(mesh):
    in_specs = (P("mom", "energy", None, None), P("mom", None, None, None, None), P(), P(), P())
    out_specs = P("energy", "mom", None)
    return jax.shard_map(body, mesh=mesh, in_specs=in_specs, out_specs=out_specs, check_vma=False)
```

profile of v0, /device:TPU:0, one launch (start us, length us, event | category | flops | bytes accessed | tf_op | source)
XLA Modules:
  0.0 198.5 jit_solution(15541276946606975576)
XLA Ops:
  6.5 4.9 %collective-permute-start = (bf16[2,16,2048]{2,1,0:T(8,128)(2,1)}, bf16[2,16,2048]{2,1,0:T(8,128)(2,1)S(1)}, u32[]{:S(2)}, u32[]{:S(2)}) collective-permute-start(bf16[2,16,2048]{2,1,0:T(8,128)(2,1)} %bitcast.93), channel_id=1, source_target_pairs={{0,8},{4,12},{8,16},{12,20},{16,24},{20,28},{1,9},{5,13},{9,17},{1... | collective-permute-start | bytes 393224 | tf_op jit(solution)/shard_map/ppermute | solution.py:14
  11.5 3.4 %collective-permute-start.1 = (bf16[2,16,2048]{2,1,0:T(8,128)(2,1)}, bf16[2,16,2048]{2,1,0:T(8,128)(2,1)S(1)}, u32[]{:S(2)}, u32[]{:S(2)}) collective-permute-start(bf16[2,16,2048]{2,1,0:T(8,128)(2,1)} %bitcast.94), channel_id=1, source_target_pairs={{0,4},{4,8},{8,12},{12,16},{16,20},{20,24},{24,28},{1,5},{5,9},{9,... | collective-permute-start | bytes 393224 | tf_op jit(solution)/shard_map/ppermute | solution.py:14
  24.6 1.6 copy.63
  30.2 2.1 %stack.22 = bf16[1,2,16,2,32,32]{5,4,3,2,1,0:T(8,128)(2,1)} reshape(bf16[2,16,2048]{2,1,0:T(8,128)(2,1)} %get-tuple-element.94) | data formatting | bytes 262144 | tf_op jit(solution)/shard_map/stack | solution.py:23
  32.3 2.1 %stack.23 = bf16[1,2,16,2,32,32]{5,4,3,2,1,0:T(8,128)(2,1)} reshape(bf16[2,16,2048]{2,1,0:T(8,128)(2,1)} %get-tuple-element.93) | data formatting | bytes 262144 | tf_op jit(solution)/shard_map/stack | solution.py:23
  41.5 110.2 %while.11 = (s32[]{:T(128)}, f32[2,16,2,32,32]{3,4,2,0,1:T(8,128)}, s32[5]{0:T(128)S(1)}, bf16[5,3,16,1024]{3,2,1,0:T(8,128)(2,1)}, bf16[6,9,5,16]{3,0,2,1:T(8,1...) while((s32[]{:T(128)}, f32[2,16,2,32,32]{3,4,2,0,1:T(8,128)}, ...), condition=%wide.region_1.2_spmd.clone, body=%wide.region_0.1_spmd.clone.sunk | while | flops 90571880 | bytes 4666249 | solution.py:52
  49.6 3.5 %convert_bitcast_fusion.2 = bf16[16,6,32,3,32,1,1]{2,1,3,4,0,6,5:T(8,128)(2,1)} fusion(bf16[6,3,3,16,1]{0,2,1,4,3:T(4,128)(2,1)} %copy.73, bf16[3,16,32,32,1]{3,2,1,0,4:T(8,128)(2,1)S(1)} %bitcast.90), kind=kOutput, calls=%fused_computation.5.clone.1 | convolution fusion | flops 1769472 | bytes 689856 | tf_op jit(solution)/shard_map/while/body/eval_jaxpr/sija,janl->aslin/dot_general | solution.py:38
  53.8 2.6 %gather_fusion = bf16[16,6,2,2,32,32]{5,4,3,2,1,0:T(8,128)(2,1)} fusion(bf16[6,2,16,2,32,32]{5,4,3,2,1,0:T(8,128)(2,1)S(1)} %get-tuple-element.172, s32[1024]{0:T(1024)S(1)} %pad_clamp_fusion.2), kind=kCustom, calls=%fused_computation.clone.clone.1 | custom fusion | bytes 1572928 | tf_op jit(solution)/shard_map/while/body/eval_jaxpr/jit(_take)/gather | solution.py:42
  56.4 7.0 %fusion.43 = f32[2,16,2,32,32]{3,4,2,0,1:T(8,128)} fusion(bf16[16,6,32,3,32,1,1]{2,1,3,4,0,6,5:T(8,128)(2,1)} %convert_bitcast_fusion.2, f32[2,16,2,32,32]{3,4,2,0,1:T(8,128)} %get-tuple-element.157, pred[]{:T(512)S(6)} %compare.3, bf16[16,6,2,2,32,32]{5,4,3,2,1,0:T(8,128)(2,1)} %gather_fusion, pred[16]{0:T(512)(128)(4,1)S(1)} %get-tuple-element.145, ...), kind=kOutput, calls=%fused_computation.10.clone.1 | convolution fusion | flops 88801280 | bytes 1998865 | tf_op jit(solution)/shard_map/while/body/eval_jaxpr/iapm,aiecmn->eacpn/dot_general | solution.py:46
  71.5 3.5 %convert_bitcast_fusion.2 = bf16[16,6,32,3,32,1,1]{2,1,3,4,0,6,5:T(8,128)(2,1)} fusion(bf16[6,3,3,16,1]{0,2,1,4,3:T(4,128)(2,1)} %copy.73, bf16[3,16,32,32,1]{3,2,1,0,4:T(8,128)(2,1)S(1)} %bitcast.90), kind=kOutput, calls=%fused_computation.5.clone.1 | convolution fusion | flops 1769472 | bytes 689856 | tf_op jit(solution)/shard_map/while/body/eval_jaxpr/sija,janl->aslin/dot_general | solution.py:38
  75.7 2.6 %gather_fusion = bf16[16,6,2,2,32,32]{5,4,3,2,1,0:T(8,128)(2,1)} fusion(bf16[6,2,16,2,32,32]{5,4,3,2,1,0:T(8,128)(2,1)S(1)} %get-tuple-element.172, s32[1024]{0:T(1024)S(1)} %pad_clamp_fusion.2), kind=kCustom, calls=%fused_computation.clone.clone.1 | custom fusion | bytes 1572928 | tf_op jit(solution)/shard_map/while/body/eval_jaxpr/jit(_take)/gather | solution.py:42
  78.3 7.2 %fusion.43 = f32[2,16,2,32,32]{3,4,2,0,1:T(8,128)} fusion(bf16[16,6,32,3,32,1,1]{2,1,3,4,0,6,5:T(8,128)(2,1)} %convert_bitcast_fusion.2, f32[2,16,2,32,32]{3,4,2,0,1:T(8,128)} %get-tuple-element.157, pred[]{:T(512)S(6)} %compare.3, bf16[16,6,2,2,32,32]{5,4,3,2,1,0:T(8,128)(2,1)} %gather_fusion, pred[16]{0:T(512)(128)(4,1)S(1)} %get-tuple-element.145, ...), kind=kOutput, calls=%fused_computation.10.clone.1 | convolution fusion | flops 88801280 | bytes 1998865 | tf_op jit(solution)/shard_map/while/body/eval_jaxpr/iapm,aiecmn->eacpn/dot_general | solution.py:46
  93.6 3.5 %convert_bitcast_fusion.2 = bf16[16,6,32,3,32,1,1]{2,1,3,4,0,6,5:T(8,128)(2,1)} fusion(bf16[6,3,3,16,1]{0,2,1,4,3:T(4,128)(2,1)} %copy.73, bf16[3,16,32,32,1]{3,2,1,0,4:T(8,128)(2,1)S(1)} %bitcast.90), kind=kOutput, calls=%fused_computation.5.clone.1 | convolution fusion | flops 1769472 | bytes 689856 | tf_op jit(solution)/shard_map/while/body/eval_jaxpr/sija,janl->aslin/dot_general | solution.py:38
  97.7 2.6 %gather_fusion = bf16[16,6,2,2,32,32]{5,4,3,2,1,0:T(8,128)(2,1)} fusion(bf16[6,2,16,2,32,32]{5,4,3,2,1,0:T(8,128)(2,1)S(1)} %get-tuple-element.172, s32[1024]{0:T(1024)S(1)} %pad_clamp_fusion.2), kind=kCustom, calls=%fused_computation.clone.clone.1 | custom fusion | bytes 1572928 | tf_op jit(solution)/shard_map/while/body/eval_jaxpr/jit(_take)/gather | solution.py:42
  100.4 7.2 %fusion.43 = f32[2,16,2,32,32]{3,4,2,0,1:T(8,128)} fusion(bf16[16,6,32,3,32,1,1]{2,1,3,4,0,6,5:T(8,128)(2,1)} %convert_bitcast_fusion.2, f32[2,16,2,32,32]{3,4,2,0,1:T(8,128)} %get-tuple-element.157, pred[]{:T(512)S(6)} %compare.3, bf16[16,6,2,2,32,32]{5,4,3,2,1,0:T(8,128)(2,1)} %gather_fusion, pred[16]{0:T(512)(128)(4,1)S(1)} %get-tuple-element.145, ...), kind=kOutput, calls=%fused_computation.10.clone.1 | convolution fusion | flops 88801280 | bytes 1998865 | tf_op jit(solution)/shard_map/while/body/eval_jaxpr/iapm,aiecmn->eacpn/dot_general | solution.py:46
  115.7 3.5 %convert_bitcast_fusion.2 = bf16[16,6,32,3,32,1,1]{2,1,3,4,0,6,5:T(8,128)(2,1)} fusion(bf16[6,3,3,16,1]{0,2,1,4,3:T(4,128)(2,1)} %copy.73, bf16[3,16,32,32,1]{3,2,1,0,4:T(8,128)(2,1)S(1)} %bitcast.90), kind=kOutput, calls=%fused_computation.5.clone.1 | convolution fusion | flops 1769472 | bytes 689856 | tf_op jit(solution)/shard_map/while/body/eval_jaxpr/sija,janl->aslin/dot_general | solution.py:38
  119.8 2.6 %gather_fusion = bf16[16,6,2,2,32,32]{5,4,3,2,1,0:T(8,128)(2,1)} fusion(bf16[6,2,16,2,32,32]{5,4,3,2,1,0:T(8,128)(2,1)S(1)} %get-tuple-element.172, s32[1024]{0:T(1024)S(1)} %pad_clamp_fusion.2), kind=kCustom, calls=%fused_computation.clone.clone.1 | custom fusion | bytes 1572928 | tf_op jit(solution)/shard_map/while/body/eval_jaxpr/jit(_take)/gather | solution.py:42
  122.5 7.2 %fusion.43 = f32[2,16,2,32,32]{3,4,2,0,1:T(8,128)} fusion(bf16[16,6,32,3,32,1,1]{2,1,3,4,0,6,5:T(8,128)(2,1)} %convert_bitcast_fusion.2, f32[2,16,2,32,32]{3,4,2,0,1:T(8,128)} %get-tuple-element.157, pred[]{:T(512)S(6)} %compare.3, bf16[16,6,2,2,32,32]{5,4,3,2,1,0:T(8,128)(2,1)} %gather_fusion, pred[16]{0:T(512)(128)(4,1)S(1)} %get-tuple-element.145, ...), kind=kOutput, calls=%fused_computation.10.clone.1 | convolution fusion | flops 88801280 | bytes 1998865 | tf_op jit(solution)/shard_map/while/body/eval_jaxpr/iapm,aiecmn->eacpn/dot_general | solution.py:46
  137.7 3.5 %convert_bitcast_fusion.2 = bf16[16,6,32,3,32,1,1]{2,1,3,4,0,6,5:T(8,128)(2,1)} fusion(bf16[6,3,3,16,1]{0,2,1,4,3:T(4,128)(2,1)} %copy.73, bf16[3,16,32,32,1]{3,2,1,0,4:T(8,128)(2,1)S(1)} %bitcast.90), kind=kOutput, calls=%fused_computation.5.clone.1 | convolution fusion | flops 1769472 | bytes 689856 | tf_op jit(solution)/shard_map/while/body/eval_jaxpr/sija,janl->aslin/dot_general | solution.py:38
  141.9 2.6 %gather_fusion = bf16[16,6,2,2,32,32]{5,4,3,2,1,0:T(8,128)(2,1)} fusion(bf16[6,2,16,2,32,32]{5,4,3,2,1,0:T(8,128)(2,1)S(1)} %get-tuple-element.172, s32[1024]{0:T(1024)S(1)} %pad_clamp_fusion.2), kind=kCustom, calls=%fused_computation.clone.clone.1 | custom fusion | bytes 1572928 | tf_op jit(solution)/shard_map/while/body/eval_jaxpr/jit(_take)/gather | solution.py:42
  144.5 7.2 %fusion.43 = f32[2,16,2,32,32]{3,4,2,0,1:T(8,128)} fusion(bf16[16,6,32,3,32,1,1]{2,1,3,4,0,6,5:T(8,128)(2,1)} %convert_bitcast_fusion.2, f32[2,16,2,32,32]{3,4,2,0,1:T(8,128)} %get-tuple-element.157, pred[]{:T(512)S(6)} %compare.3, bf16[16,6,2,2,32,32]{5,4,3,2,1,0:T(8,128)(2,1)} %gather_fusion, pred[16]{0:T(512)(128)(4,1)S(1)} %get-tuple-element.145, ...), kind=kOutput, calls=%fused_computation.10.clone.1 | convolution fusion | flops 88801280 | bytes 1998865 | tf_op jit(solution)/shard_map/while/body/eval_jaxpr/iapm,aiecmn->eacpn/dot_general | solution.py:46
  151.7 1.6 copy.24
  154.5 35.6 %all-reduce.2.cloned.1.call-done = f32[2,16,2048]{2,1,0:T(8,128)} async-done(((f32[2,16,2048]{2,1,0:T(8,128)}), f32[2,16,2048]{2,1,0:T(8,128)}) %all-reduce.2.cloned.1.call-update) | async-done | bytes 262160 | tf_op jit(solution)/shard_map/psum | solution.py:71
  190.1 1.5 constant_dynamic-slice_fusion.3
  (67 shorter events, 50.5 us)
Async XLA Ops:
  6.5 183.6 %all-reduce.2.cloned.1.call-start = ((), (), s32[]{:S(2)}) async-start(), calls=%async_computation | async-start | bytes 524288 | tf_op jit(solution)/shard_map/psum | solution.py:71
  6.5 19.6 %collective-permute-start = (bf16[2,16,2048]{2,1,0:T(8,128)(2,1)}, bf16[2,16,2048]{2,1,0:T(8,128)(2,1)S(1)}, u32[]{:S(2)}, u32[]{:S(2)}) collective-permute-start(bf16[2,16,2048]{2,1,0:T(8,128)(2,1)} %bitcast.93), channel_id=1, source_target_pairs={{0,8},{4,12},{8,16},{12,20},{16,24},{20,28},{1,9},{5,13},{9,17},{1... | collective-permute-start | bytes 393224 | tf_op jit(solution)/shard_map/ppermute | solution.py:14
  11.5 14.7 %collective-permute-start.1 = (bf16[2,16,2048]{2,1,0:T(8,128)(2,1)}, bf16[2,16,2048]{2,1,0:T(8,128)(2,1)S(1)}, u32[]{:S(2)}, u32[]{:S(2)}) collective-permute-start(bf16[2,16,2048]{2,1,0:T(8,128)(2,1)} %bitcast.94), channel_id=1, source_target_pairs={{0,4},{4,8},{8,12},{12,16},{16,20},{20,24},{24,28},{1,5},{5,9},{9,... | collective-permute-start | bytes 393224 | tf_op jit(solution)/shard_map/ppermute | solution.py:14
  14.9 12.2 %collective-permute-start.2 = (bf16[2,16,2048]{2,1,0:T(8,128)(2,1)}, bf16[2,16,2048]{2,1,0:T(8,128)(2,1)S(1)}, u32[]{:S(2)}, u32[]{:S(2)}) collective-permute-start(bf16[2,16,2048]{2,1,0:T(8,128)(2,1)} %bitcast.95), channel_id=1, source_target_pairs={{4,0},{8,4},{12,8},{16,12},{20,16},{24,20},{28,24},{5,1},{9,5},{13... | collective-permute-start | bytes 393224 | tf_op jit(solution)/shard_map/ppermute | solution.py:14
  16.2 11.0 %collective-permute-start.3 = (bf16[2,16,2048]{2,1,0:T(8,128)(2,1)}, bf16[2,16,2048]{2,1,0:T(8,128)(2,1)S(1)}, u32[]{:S(2)}, u32[]{:S(2)}) collective-permute-start(bf16[2,16,2048]{2,1,0:T(8,128)(2,1)} %bitcast.96), channel_id=1, source_target_pairs={{8,0},{12,4},{16,8},{20,12},{24,16},{28,20},{9,1},{13,5},{17,9},{2... | collective-permute-start | bytes 393224 | tf_op jit(solution)/shard_map/ppermute | solution.py:14
  37.9 3.4 %copy-start = (bf16[1,2,16,2,32,32]{5,4,3,2,1,0:T(8,128)(2,1)S(1)}, bf16[1,2,16,2,32,32]{5,4,3,2,1,0:T(8,128)(2,1)}, u32[]{:S(2)}) copy-start(bf16[1,2,16,2,32,32]{5,4,3,2,1,0:T(8,128)(2,1)} %stack.25) | copy-start | bytes 393220
  37.9 3.5 %copy-start.1 = (bf16[1,2,16,2,32,32]{5,4,3,2,1,0:T(8,128)(2,1)S(1)}, bf16[1,2,16,2,32,32]{5,4,3,2,1,0:T(8,128)(2,1)}, u32[]{:S(2)}) copy-start(bf16[1,2,16,2,32,32]{5,4,3,2,1,0:T(8,128)(2,1)} %stack.26) | copy-start | bytes 393220
Sparse Core Ops, SparseCore 0:
  154.6 35.4 all-reduce.1
where the time goes:
time: 200 us; the launch traced here: 199 us
  local copies, waits for them, and re-layouts  66.4 us (33%)
  matrix products  53 us (26%)
  waiting for transfers between devices  35.6 us (18%)
  between operations  19.3 us (10%)
  starting transfers between devices  10.9 us (5%)
  loops' own time  9.8 us (5%)
  other arithmetic  3.51 us (2%)
    dot_general x5, matrix products, one_slot(): jnp.einsum('iapm,aiecmn->eacpn', derivs, middle, preferred_element_type=j...  35.7 us
    psum x1, waiting for transfers between devices, body(): summed = lax.psum(partial_terms, 'mom')  35.6 us
    dot_general x5, matrix products, one_slot(): jnp.einsum('sija,janl->aslin', table, derivs.astype(jnp.float32))  17.3 us
    gather x5, local copies, waits for them, and re-layouts, one_slot(): gathered = jnp.take(blocks, column, axis=2)  13.2 us
    ppermute x4, starting transfers between devices, shifted_2(): return lax.ppermute(array, axis, pairs)  10.9 us
    another operation x1, loops' own time, sandwich(): total, _ = lax.scan(one_slot, start_total, jnp.arange(NB, dtype=jnp.int32))  9.8 us
    another operation x7, local copies, waits for them, and re-layouts, shifted_stack(): return jnp.stack(pieces, 0)  8.95 us
    dynamic_slice x5, local copies, waits for them, and re-layouts, one_slot(): lax.dynamic_index_in_dim(gradient, slot, 0, keepdims=False)  7.71 us
  transfers between devices with their start and end apart: 5, of which 1 were waited for; matrix products, arithmetic and copies ran while one was open for 2% of the time, Pallas kernels for 0%

commit v1 on v0

v1 whole, which is shorter than its diff:
```python
import functools

import jax
import jax.numpy as jnp
from jax import lax
from jax.experimental import pallas as pl
from jax.experimental.pallas import tpu as pltpu
from jax.sharding import PartitionSpec as P

NO = 32
NB = 5
NW = 3
NS = 2 * NW
LANES = 128
COPIES = LANES // NO
HI = NO // COPIES
VMEM_LIMIT = 40 * 1024 * 1024

NT = (((1,), (1,)), ((), ()))


def fold_matrix():
    row = lax.broadcasted_iota(jnp.int32, (LANES, COPIES * LANES), 0)
    col = lax.broadcasted_iota(jnp.int32, (LANES, COPIES * LANES), 1)
    inner = col % NO
    source = (col // LANES) * NO + (inner % HI) * COPIES + inner // HI
    return jnp.where(row == source, 1.0, 0.0).astype(jnp.bfloat16)


def spread_rows(spread, at, stacked, fold):
    wide = jnp.dot(stacked, fold, preferred_element_type=jnp.float32)
    for q in range(COPIES):
        spread[q, at : at + stacked.shape[0], :] = wide[:, q * LANES : (q + 1) * LANES]


def tables_kernel(natoms, gradient, coupling, kernel_out, derivs_out, spread, rows):
    fold = fold_matrix()
    tiles = NO * NO // LANES
    block = natoms * tiles
    for slot in range(NB):
        for direction in range(3):
            flat = gradient[slot, direction]
            stacked = jnp.concatenate(
                [flat[:, t * LANES : (t + 1) * LANES] for t in range(tiles)], axis=0
            )
            at = (slot * 3 + direction) * block
            spread_rows(spread, at, stacked, fold)

    pairs = 9
    row = lax.broadcasted_iota(jnp.int32, (NS * pairs, pairs * 2 * LANES), 0)
    col = lax.broadcasted_iota(jnp.int32, (NS * pairs, pairs * 2 * LANES), 1)
    source = ((col % (2 * LANES)) // NO) * pairs + col // (2 * LANES)
    expand = jnp.where(
        (row == source) & ((col % (2 * LANES)) // NO < NS), 1.0, 0.0
    ).astype(jnp.float32)
    wide = lax.dot_general(
        coupling[...],
        expand,
        (((0,), (0,)), ((), ())),
        precision=lax.Precision.HIGHEST,
        preferred_element_type=jnp.float32,
    )
    for k in range(pairs * 2):
        rows[k] = wide[:, k * LANES : (k + 1) * LANES]

    for slot in range(NB):

        def one_atom(atom, carry):
            at = slot * natoms + atom
            derivs = [
                [
                    spread[
                        q, pl.ds((slot * 3 + j) * block + atom, tiles, stride=natoms), :
                    ]
                    for q in range(COPIES)
                ]
                for j in range(3)
            ]
            for j in range(3):
                derivs_out[at, j * NO : (j + 1) * NO, :] = jnp.concatenate(
                    derivs[j], axis=0
                ).astype(jnp.bfloat16)
            for i in range(3):
                for half in range(2):
                    total = None
                    for j in range(3):
                        weight = rows[(3 * i + j) * 2 + half, pl.ds(at, 1), :]
                        term = jnp.concatenate([d * weight for d in derivs[j]], axis=0)
                        total = term if total is None else total + term
                    kernel_out[
                        at, i * NO : (i + 1) * NO, half * LANES : (half + 1) * LANES
                    ] = total.astype(jnp.bfloat16)
            return carry

        lax.fori_loop(0, natoms, one_atom, 0)


def tables(gradient, coupling):
    natoms = gradient.shape[2]
    count = NB * natoms
    tiles = NO * NO // LANES
    return pl.pallas_call(
        functools.partial(tables_kernel, natoms),
        out_shape=(
            jax.ShapeDtypeStruct((count, 3 * NO, 2 * LANES), jnp.bfloat16),
            jax.ShapeDtypeStruct((count, 3 * NO, LANES), jnp.bfloat16),
        ),
        in_specs=[pl.BlockSpec(memory_space=pltpu.VMEM)] * 2,
        out_specs=[pl.BlockSpec(memory_space=pltpu.VMEM)] * 2,
        scratch_shapes=[
            pltpu.VMEM((COPIES, NB * 3 * tiles * natoms, LANES), jnp.float32),
            pltpu.VMEM((9 * 2, count, LANES), jnp.float32),
        ],
        compiler_params=pltpu.CompilerParams(vmem_limit_bytes=VMEM_LIMIT),
        cost_estimate=pl.CostEstimate(
            flops=200_000_000, bytes_accessed=6_000_000, transcendentals=0
        ),
        name="tables",
    )(gradient, coupling)


def sandwich_kernel(
    count, natoms, neighbours, offsets, below2, below1, local, above1, above2,
    kernel, derivs, out, spread, blocks, sums,
):
    fold = fold_matrix()
    tiles = 2 * NO * NO // LANES
    energy_rows = tiles * natoms
    for piece, ref in enumerate((below2, below1, local, above1, above2)):
        for e in range(count):
            flat = ref[e]
            stacked = jnp.concatenate(
                [flat[:, t * LANES : (t + 1) * LANES] for t in range(tiles)], axis=0
            )
            at = (piece * count + e) * energy_rows
            spread_rows(spread, at, stacked, fold)

    group = lax.broadcasted_iota(jnp.int32, (HI, LANES), 1) // NO
    starts = []
    for phonon in range(NW):
        for sign in (1, -1):
            starts.append((2 * count - sign * offsets[phonon]) * energy_rows)

    def build(atom, carry):
        for e in range(count):
            for c in range(2):
                for half in range(2):
                    pieces = []
                    for q in range(COPIES):
                        total = jnp.zeros((HI, LANES), jnp.float32)
                        for g in range(COPIES):
                            s = half * COPIES + g
                            if s < NS:
                                base = starts[s] + (e * tiles + c * HI) * natoms + atom
                                part = spread[q, pl.ds(base, HI, stride=natoms), :]
                                total = jnp.where(group == g, part, total)
                        pieces.append(total)
                    at = (e * 2 + c) * NO
                    blocks[atom, at : at + NO, half * LANES : (half + 1) * LANES] = (
                        jnp.concatenate(pieces, axis=0).astype(jnp.bfloat16)
                    )
        return carry

    lax.fori_loop(0, natoms, build, 0)

    groups = 2 * count
    wide = lax.broadcasted_iota(jnp.int32, (NO, LANES), 1) // NO
    masks = [jnp.where(wide == g, 1.0, 0.0).astype(jnp.bfloat16) for g in range(groups)]

    def one_atom(atom, carry):
        lefts = []
        rights = []
        for slot in range(NB):
            at = slot * natoms + atom
            middle = lax.dot_general(
                kernel[at], blocks[neighbours[slot, atom]], NT,
                preferred_element_type=jnp.float32,
            ).astype(jnp.bfloat16)
            for i in range(3):
                rights.append(middle[i * NO : (i + 1) * NO, :])
                block = derivs[at, i * NO : (i + 1) * NO, :]
                lefts.append(jnp.concatenate([block * mask for mask in masks], axis=0))
        sigma = lax.dot_general(
            jnp.concatenate(lefts, axis=1), jnp.concatenate(rights, axis=1), NT,
            preferred_element_type=jnp.float32,
        )
        for q in range(COPIES):
            part = jnp.concatenate(
                [sigma[g * NO + q * HI : g * NO + (q + 1) * HI, :] for g in range(groups)],
                axis=0,
            )
            sums[q, pl.ds(atom * groups * HI, groups * HI), :] = part.astype(jnp.bfloat16)
        return carry

    lax.fori_loop(0, natoms, one_atom, 0)

    row = lax.broadcasted_iota(jnp.int32, (NO, LANES), 0)
    col = lax.broadcasted_iota(jnp.int32, (NO, LANES), 1)
    placed = None
    for q in range(COPIES):
        place = jnp.where(
            (col // NO == q) & ((row % HI) * COPIES + row // HI == col % NO), 1.0, 0.0
        ).astype(jnp.bfloat16)
        term = jnp.dot(sums[q], place, preferred_element_type=jnp.float32)
        placed = term if placed is None else placed + term
    out[...] = placed.astype(jnp.bfloat16).reshape(out.shape)


def sandwich(window, kernel, derivs, neighbours, offsets, shares):
    count, natoms, _ = window[0].shape
    groups = 2 * count
    tiles = 2 * NO * NO // LANES
    rows = natoms * groups * HI
    return pl.pallas_call(
        functools.partial(sandwich_kernel, count, natoms),
        out_shape=jax.ShapeDtypeStruct((shares, rows // shares, LANES), jnp.bfloat16),
        in_specs=[pl.BlockSpec(memory_space=pltpu.SMEM)] * 2
        + [pl.BlockSpec(memory_space=pltpu.VMEM)] * 7,
        out_specs=pl.BlockSpec(memory_space=pltpu.VMEM),
        scratch_shapes=[
            pltpu.VMEM((COPIES, 5 * count * tiles * natoms, LANES), jnp.float32),
            pltpu.VMEM((natoms, groups * NO, 2 * LANES), jnp.bfloat16),
            pltpu.VMEM((COPIES, rows, NO), jnp.bfloat16),
        ],
        compiler_params=pltpu.CompilerParams(vmem_limit_bytes=VMEM_LIMIT),
        cost_estimate=pl.CostEstimate(
            flops=800_000_000, bytes_accessed=7_000_000, transcendentals=0
        ),
        name="sandwich",
    )(neighbours, offsets, *window, kernel, derivs)


def combine_kernel(parts, out, total):
    count, share, width = out.shape
    tiles = width // LANES
    summed = parts[0].astype(jnp.float32)
    for k in range(1, parts.shape[0]):
        summed = summed + parts[k].astype(jnp.float32)
    total[...] = summed
    for e in range(count):
        for t in range(tiles):
            out[e, :, t * LANES : (t + 1) * LANES] = total[
                pl.ds(e * tiles + t, share, stride=count * tiles), :
            ]


def combine(parts, count, share):
    return pl.pallas_call(
        combine_kernel,
        out_shape=jax.ShapeDtypeStruct((count, share, 2 * NO * NO), jnp.float32),
        in_specs=[pl.BlockSpec(memory_space=pltpu.VMEM)],
        out_specs=pl.BlockSpec(memory_space=pltpu.VMEM),
        scratch_shapes=[pltpu.VMEM(parts.shape[1:], jnp.float32)],
        name="combine",
    )(parts)


def shifted(array, axis, by):
    length = lax.axis_size(axis)
    pairs = [(i, i + by) for i in range(length) if 0 <= i + by < length]
    return lax.ppermute(array, axis, pairs)


def local_partial(window, coupling, gradient, neighbours, offsets, shares):
    kernel, derivs = tables(gradient, coupling.reshape(NS * 9, -1))
    return sandwich(window, kernel, derivs, neighbours.T, offsets, shares)


def body(green, coupling, gradient, neighbours, offsets):
    local_block = green[0]
    count, natoms, _ = local_block.shape
    shares = lax.axis_size("mom")
    window = (
        shifted(local_block, "energy", 2),
        shifted(local_block, "energy", 1),
        local_block,
        shifted(local_block, "energy", -1),
        shifted(local_block, "energy", -2),
    )
    partial_terms = local_partial(window, coupling[0], gradient, neighbours, offsets, shares)
    parts = lax.all_to_all(partial_terms, "mom", 0, 0, tiled=True)
    return combine(parts, count, natoms // shares)


def solution(mesh):
    in_specs = (P("mom", "energy", None, None), P("mom", None, None, None, None), P(), P(), P())
    out_specs = P("energy", "mom", None)
    return jax.shard_map(body, mesh=mesh, in_specs=in_specs, out_specs=out_specs, check_vma=False)
```

time: 200 us -> 45.9 us (0.23)
  local copies, waits for them, and re-layouts: 66.4 us -> 3.36 us
  matrix products: 53 us -> 0 us
  waiting for transfers between devices: 35.6 us -> 0.01 us
  Pallas kernels: 0 us -> 20.3 us
  between operations: 19.3 us -> 0.11 us
  loops' own time: 9.8 us -> 0 us
  blocking collectives: 0 us -> 7.77 us
  other arithmetic: 3.51 us -> 1.26 us
    dot_general x10 -> x0, matrix products: 53 us -> none  [the longest x5 35.7 us: one_slot(): jnp.einsum('iapm,aiecmn->eacpn', derivs, middle, preferred_element_type=j...]
    psum x1 -> x0, waiting for transfers between devices: 35.6 us -> none  [body(): summed = lax.psum(partial_terms, 'mom')]
    pallas_call x0 -> x3, Pallas kernels: none -> 20.3 us  [the longest x1 13.6 us: sandwich(): pl.pallas_call(functools.partial(sandwich_kernel, count, natoms), out_sha...]
    dynamic_slice x17 -> x0, local copies, waits for them, and re-layouts: 19.7 us -> none  [the longest x5 7.71 us: one_slot(): lax.dynamic_index_in_dim(gradient, slot, 0, keepdims=False)]
    reshape x11 -> x0, local copies, waits for them, and re-layouts: 14.6 us -> none  [the longest x5 7.41 us: one_slot(): lax.dynamic_index_in_dim(weights, slot, 2, keepdims=False)]
    gather x5 -> x0, local copies, waits for them, and re-layouts: 13.2 us -> none  [one_slot(): gathered = jnp.take(blocks, column, axis=2)]
    another operation x1 -> x0, loops' own time: 9.8 us -> none  [sandwich(): total, _ = lax.scan(one_slot, start_total, jnp.arange(NB, dtype=jnp.int32))]
    another operation x7 -> x1, local copies, waits for them, and re-layouts: 8.95 us -> 0.1 us  [local_partial(): kernel, derivs = tables(gradient, coupling.reshape(NS * 9, -1))]
  transfers between devices with their start and end apart: 5 -> 4, of which waited for: 1 -> 0; matrix products, arithmetic and copies ran while one was open for 2% -> 3% of each run, Pallas kernels for 0% -> 11%
where the time goes in v1:
time: 45.9 us; the launch traced here: 45.5 us
  Pallas kernels  20.3 us (44%)
  starting transfers between devices  12.7 us (28%)
  blocking collectives  7.77 us (17%)
  local copies, waits for them, and re-layouts  3.36 us (7%)
  other arithmetic  1.26 us (3%)
    pallas_call x1, Pallas kernels, sandwich(): pl.pallas_call(functools.partial(sandwich_kernel, count, natoms), out_sha...  13.6 us
    ppermute x4, starting transfers between devices, shifted(): return lax.ppermute(array, axis, pairs)  12.7 us
    all_to_all x1, blocking collectives, body(): parts = lax.all_to_all(partial_terms, 'mom', 0, 0, tiled=True)  7.77 us
    pallas_call x1, Pallas kernels, tables(): pl.pallas_call(functools.partial(tables_kernel, natoms), out_shape=(jax.S...  5.19 us
    unnamed x8, local copies, waits for them, and re-layouts  3.27 us
    pallas_call x1, Pallas kernels, combine(): pl.pallas_call(combine_kernel, out_shape=jax.ShapeDtypeStruct((count, sha...  1.6 us
    unnamed x1, other arithmetic  1.26 us
  transfers between devices with their start and end apart: 4, of which 0 were waited for; matrix products, arithmetic and copies ran while one was open for 3% of the time, Pallas kernels for 11%

profile of v1, /device:TPU:0, one launch (start us, length us, event | category | flops | bytes accessed | tf_op | source)
XLA Modules:
  0.0 45.5 jit_solution(8491258046182675502)
XLA Ops:
  0.0 1.3 %collective-permute-start.3 = (bf16[2,16,2048]{2,1,0:T(8,128)(2,1)}, bf16[2,16,2048]{2,1,0:T(8,128)(2,1)S(1)}, u32[]{:S(2)}, u32[]{:S(2)}) collective-permute-start(bf16[2,16,2048]{2,1,0:T(8,128)(2,1)} %bitcast.2), channel_id=1, source_target_pairs={{8,0},{12,4},{16,8},{20,12},{24,16},{28,20},{9,1},{13,5},{17,9},{2... | collective-permute-start | bytes 393224 | tf_op jit(solution)/shard_map/ppermute | solution.py:261
  1.3 1.3 %collective-permute-start.2 = (bf16[2,16,2048]{2,1,0:T(8,128)(2,1)}, bf16[2,16,2048]{2,1,0:T(8,128)(2,1)S(1)}, u32[]{:S(2)}, u32[]{:S(2)}) collective-permute-start(bf16[2,16,2048]{2,1,0:T(8,128)(2,1)} %bitcast.3), channel_id=1, source_target_pairs={{4,0},{8,4},{12,8},{16,12},{20,16},{24,20},{28,24},{5,1},{9,5},{13... | collective-permute-start | bytes 393224 | tf_op jit(solution)/shard_map/ppermute | solution.py:261
  2.6 5.5 %collective-permute-start.1 = (bf16[2,16,2048]{2,1,0:T(8,128)(2,1)}, bf16[2,16,2048]{2,1,0:T(8,128)(2,1)S(1)}, u32[]{:S(2)}, u32[]{:S(2)}) collective-permute-start(bf16[2,16,2048]{2,1,0:T(8,128)(2,1)} %bitcast.4), channel_id=1, source_target_pairs={{0,4},{4,8},{8,12},{12,16},{16,20},{20,24},{24,28},{1,5},{5,9},{9,... | collective-permute-start | bytes 393224 | tf_op jit(solution)/shard_map/ppermute | solution.py:261
  8.1 4.6 %collective-permute-start = (bf16[2,16,2048]{2,1,0:T(8,128)(2,1)}, bf16[2,16,2048]{2,1,0:T(8,128)(2,1)S(1)}, u32[]{:S(2)}, u32[]{:S(2)}) collective-permute-start(bf16[2,16,2048]{2,1,0:T(8,128)(2,1)} %bitcast.5), channel_id=1, source_target_pairs={{0,8},{4,12},{8,16},{12,20},{16,24},{20,28},{1,9},{5,13},{9,17},{1... | collective-permute-start | bytes 393224 | tf_op jit(solution)/shard_map/ppermute | solution.py:261
  12.7 1.3 %reduce = f32[6,9,5,16]{3,2,1,0:T(8,128)S(1)} reduce(f32[1,6,9,5,16]{4,0,3,2,1:T(1,128)} %param.6, f32[]{:T(128)} %constant.2), dimensions={0}, to_apply=%param.6.reduce_sub_computation | reduce | bytes 34564 | tf_op args[1]
  14.0 0.1 reshape_squeeze.3.coupling
  14.1 0.0 copy-start.3
  14.1 1.0 %copy-done.3 = bf16[5,3,16,1024]{3,2,1,0:T(8,128)(2,1)S(1)} copy-done((bf16[5,3,16,1024]{3,2,1,0:T(8,128)(2,1)S(1)}, bf16[5,3,16,1024]{3,2,1,0:T(8,128)(2,1)}, u32[]{:S(2)}) %copy-start.3) | copy-done | bytes 491544
  15.1 5.2 %tables.1 = (bf16[80,96,256]{2,1,0:T(8,128)(2,1)S(1)}, bf16[80,96,128]{2,1,0:T(8,128)(2,1)S(1)}) custom-call(bf16[5,3,16,1024]{3,2,1,0:T(8,128)(2,1)S(1)} %copy-done.3, f32[54,80]{1,0:T(8,128)S(1)} %reshape_squeeze.3.coupling), custom_call_target="tpu_custom_call" | custom-call | flops 200000000 | bytes 6000000 | tf_op jit(solution)/shard_map/tables/pallas_call | solution.py:102
  20.3 0.0 collective-permute-done.3.above2
  20.3 0.0 collective-permute-done.2.above1
  20.3 0.0 collective-permute-done.1.below1
  20.4 0.0 collective-permute-done.below2
  20.4 0.0 copy-start
  20.4 0.9 %copy-done = bf16[1,2,16,2048]{3,2,1,0:T(8,128)(2,1)S(1)} copy-done((bf16[1,2,16,2048]{3,2,1,0:T(8,128)(2,1)S(1)}, bf16[1,2,16,2048]{3,2,1,0:T(8,128)(2,1)}, u32[]{:S(2)}) %copy-start) | copy-done | bytes 131096
  21.3 0.0 copy-start.1
  21.3 0.7 %copy-done.1 = s32[16,5]{0,1:T(8,128)S(1)} copy-done((s32[16,5]{0,1:T(8,128)S(1)}, s32[16,5]{0,1:T(8,128)}, u32[]{:S(2)}) %copy-start.1) | copy-done | bytes 344
  22.0 0.0 copy-start.2
  22.0 0.7 %copy-done.2 = s32[3]{0:T(128)S(1)} copy-done((s32[3]{0:T(128)S(1)}, s32[3]{0:T(128)}, u32[]{:S(2)}) %copy-start.2) | copy-done | bytes 36
  22.6 13.6 %sandwich.1 = bf16[4,128,128]{2,1,0:T(8,128)(2,1)S(1)} custom-call(s32[5,16]{1,0:T(8,128)S(1)} %bitcast.7, s32[3]{0:T(128)S(1)} %copy-done.2, bf16[2,16,2048]{2,1,0:T(8,128)(2,1)S(1)} %collective-permute-done.below2, bf16[2,16,2048]{2,1,0:T(8,128)(2,1)S(1)} %collective-permute-done.1.below1, bf16[2,16,2048]{2,1,0:T(8,128)(2,1)S(1)} %bitcast.6, ...), custom_call_target="tpu_custom_call" | custom-call | flops 800000000 | bytes 7000000 | tf_op jit(solution)/shard_map/sandwich/pallas_call | solution.py:214
  36.2 7.8 %all_to_all.5.parts = bf16[4,128,128]{2,1,0:T(8,128)(2,1)} all-to-all(bf16[4,128,128]{2,1,0:T(8,128)(2,1)S(1)} %sandwich.1), channel_id=1, replica_groups=mesh['energy'=8,'mom'=4] {'mom'}, dimensions={0} | all-to-all | bytes 262144 | tf_op jit(solution)/shard_map/all_to_all | solution.py:281
  43.9 1.6 %combine.1 = f32[2,4,2048]{2,1,0:T(4,128)} custom-call(bf16[4,128,128]{2,1,0:T(8,128)(2,1)} %all_to_all.5.parts), custom_call_target="tpu_custom_call" | custom-call | tf_op jit(solution)/shard_map/combine/pallas_call | solution.py:248
Async XLA Ops:
  0.0 20.3 %collective-permute-start.3 = (bf16[2,16,2048]{2,1,0:T(8,128)(2,1)}, bf16[2,16,2048]{2,1,0:T(8,128)(2,1)S(1)}, u32[]{:S(2)}, u32[]{:S(2)}) collective-permute-start(bf16[2,16,2048]{2,1,0:T(8,128)(2,1)} %bitcast.2), channel_id=1, source_target_pairs={{8,0},{12,4},{16,8},{20,12},{24,16},{28,20},{9,1},{13,5},{17,9},{2... | collective-permute-start | bytes 393224 | tf_op jit(solution)/shard_map/ppermute | solution.py:261
  1.3 19.1 %collective-permute-start.2 = (bf16[2,16,2048]{2,1,0:T(8,128)(2,1)}, bf16[2,16,2048]{2,1,0:T(8,128)(2,1)S(1)}, u32[]{:S(2)}, u32[]{:S(2)}) collective-permute-start(bf16[2,16,2048]{2,1,0:T(8,128)(2,1)} %bitcast.3), channel_id=1, source_target_pairs={{4,0},{8,4},{12,8},{16,12},{20,16},{24,20},{28,24},{5,1},{9,5},{13... | collective-permute-start | bytes 393224 | tf_op jit(solution)/shard_map/ppermute | solution.py:261
  2.6 17.8 %collective-permute-start.1 = (bf16[2,16,2048]{2,1,0:T(8,128)(2,1)}, bf16[2,16,2048]{2,1,0:T(8,128)(2,1)S(1)}, u32[]{:S(2)}, u32[]{:S(2)}) collective-permute-start(bf16[2,16,2048]{2,1,0:T(8,128)(2,1)} %bitcast.4), channel_id=1, source_target_pairs={{0,4},{4,8},{8,12},{12,16},{16,20},{20,24},{24,28},{1,5},{5,9},{9,... | collective-permute-start | bytes 393224 | tf_op jit(solution)/shard_map/ppermute | solution.py:261
  8.1 12.3 %collective-permute-start = (bf16[2,16,2048]{2,1,0:T(8,128)(2,1)}, bf16[2,16,2048]{2,1,0:T(8,128)(2,1)S(1)}, u32[]{:S(2)}, u32[]{:S(2)}) collective-permute-start(bf16[2,16,2048]{2,1,0:T(8,128)(2,1)} %bitcast.5), channel_id=1, source_target_pairs={{0,8},{4,12},{8,16},{12,20},{16,24},{20,28},{1,9},{5,13},{9,17},{1... | collective-permute-start | bytes 393224 | tf_op jit(solution)/shard_map/ppermute | solution.py:261
  14.1 1.0 %copy-start.3 = (bf16[5,3,16,1024]{3,2,1,0:T(8,128)(2,1)S(1)}, bf16[5,3,16,1024]{3,2,1,0:T(8,128)(2,1)}, u32[]{:S(2)}) copy-start(bf16[5,3,16,1024]{3,2,1,0:T(8,128)(2,1)} %gradient.1) | copy-start | bytes 1474564
  20.4 0.9 %copy-start = (bf16[1,2,16,2048]{3,2,1,0:T(8,128)(2,1)S(1)}, bf16[1,2,16,2048]{3,2,1,0:T(8,128)(2,1)}, u32[]{:S(2)}) copy-start(bf16[1,2,16,2048]{3,2,1,0:T(8,128)(2,1)} %param.5) | copy-start | bytes 393220
  21.3 0.7 %copy-start.1 = (s32[16,5]{0,1:T(8,128)S(1)}, s32[16,5]{0,1:T(8,128)}, u32[]{:S(2)}) copy-start(s32[16,5]{0,1:T(8,128)} %param.8) | copy-start | bytes 964
  22.0 0.7 %copy-start.2 = (s32[3]{0:T(128)S(1)}, s32[3]{0:T(128)}, u32[]{:S(2)}) copy-start(s32[3]{0:T(128)} %offsets.1) | copy-start | bytes 40

commit v2 on v1

v2 whole, which is shorter than its diff:
```python
import functools

import jax
import jax.numpy as jnp
from jax import lax
from jax.experimental import pallas as pl
from jax.experimental.pallas import tpu as pltpu
from jax.sharding import PartitionSpec as P

NO = 32
NB = 5
NW = 3
NS = 2 * NW
ND = 3
LANES = 128
COPIES = LANES // NO
HI = NO // COPIES
VMEM_LIMIT = 40 * 1024 * 1024

NT = (((1,), (1,)), ((), ()))


def in_hbm(array):
    return pltpu.with_memory_space_constraint(array, pltpu.HBM)


def iota(shape, dim):
    return lax.broadcasted_iota(jnp.int32, shape, dim)


def ones_where(condition):
    return jnp.where(condition, 1.0, 0.0).astype(jnp.bfloat16)


def mixed(lane):
    return (lane % HI) * COPIES + lane // HI


def fold_matrix():
    shape = (LANES, COPIES * LANES)
    row, col = iota(shape, 0), iota(shape, 1)
    return ones_where(row == (col // LANES) * NO + mixed(col % NO))


def lane_matrix():
    row, col = iota((LANES, LANES), 0), iota((LANES, LANES), 1)
    return ones_where(row == (col // NO) * NO + mixed(col % NO))


def row_matrix(tiles, natoms):
    size = tiles * natoms
    row, col = iota((size, size), 0), iota((size, size), 1)
    return ones_where(col == (row % tiles) * natoms + row // tiles)


def stack_tiles(flat):
    return jnp.concatenate(
        [flat[:, t : t + LANES] for t in range(0, flat.shape[1], LANES)], axis=0
    )


def exact_dot(left, right):
    return jnp.dot(left, right, preferred_element_type=jnp.float32)


def tables_kernel(
    natoms, gradient_hbm, coupling_hbm, kernel_out, derivs_out,
    gradient, coupling, spread, rows, gradient_sems, coupling_sem,
):
    copy_coupling = pltpu.make_async_copy(coupling_hbm.at[:, 0, :], coupling, coupling_sem)
    copy_coupling.start()
    copies = [
        pltpu.make_async_copy(gradient_hbm.at[b], gradient.at[b], gradient_sems.at[b])
        for b in range(NB)
    ]
    for copy in copies:
        copy.start()

    tiles = NO * NO // LANES
    block = natoms * tiles
    pairs = ND * ND
    cells = pairs * NB
    width = -(-NS * cells // LANES) * LANES
    fold = fold_matrix()
    order = row_matrix(tiles, natoms)
    lane = iota((width, 2 * LANES), 0)
    widen = ones_where((lane < NS * cells) & (lane // cells == iota((width, 2 * LANES), 1) // NO))
    cell = iota((natoms, width), 1)
    cell = jnp.where(cell < NS * cells, cell % cells, -1)

    copy_coupling.wait()
    table = jnp.transpose(coupling[...])
    table = jnp.concatenate(
        [table, jnp.zeros((natoms, width - NS * cells), jnp.float32)], axis=1
    )
    high = table.astype(jnp.bfloat16)
    low = (table - high.astype(jnp.float32)).astype(jnp.bfloat16)
    for half in (high, low):
        half32 = half.astype(jnp.float32)
        left = jnp.concatenate(
            [jnp.where(cell == k, half32, 0.0) for k in range(cells)], axis=0
        ).astype(jnp.bfloat16)
        wide = exact_dot(left, widen)
        for k in range(2):
            part = wide[:, k * LANES : (k + 1) * LANES]
            rows[k] = part if half is high else rows[k] + part

    for slot in range(NB):
        copies[slot].wait()
        for j in range(ND):
            ordered = exact_dot(order, stack_tiles(gradient[slot, j])).astype(jnp.bfloat16)
            wide = exact_dot(ordered, fold)
            for q in range(COPIES):
                spread[q, (slot * ND + j) * block : (slot * ND + j + 1) * block, :] = wide[
                    :, q * LANES : (q + 1) * LANES
                ]

    for slot in range(NB):

        def one_atom(atom, carry):
            at = slot * natoms + atom
            derivs = [
                [
                    spread[
                        q,
                        pl.ds(pl.multiple_of((slot * ND + j) * block + atom * tiles, tiles), tiles),
                        :,
                    ]
                    for q in range(COPIES)
                ]
                for j in range(ND)
            ]
            for j in range(ND):
                derivs_out[at, j * NO : (j + 1) * NO, :] = jnp.concatenate(
                    derivs[j], axis=0
                ).astype(jnp.bfloat16)
            for i in range(ND):
                for half in range(2):
                    total = None
                    for j in range(ND):
                        weight = rows[
                            half, pl.ds(((ND * i + j) * NB + slot) * natoms + atom, 1), :
                        ]
                        term = jnp.concatenate([d * weight for d in derivs[j]], axis=0)
                        total = term if total is None else total + term
                    kernel_out[
                        at, i * NO : (i + 1) * NO, half * LANES : (half + 1) * LANES
                    ] = total.astype(jnp.bfloat16)
            return carry

        lax.fori_loop(0, natoms, one_atom, 0, unroll=2)


def tables(gradient, coupling):
    natoms = gradient.shape[2]
    count = NB * natoms
    tiles = NO * NO // LANES
    return pl.pallas_call(
        functools.partial(tables_kernel, natoms),
        out_shape=(
            jax.ShapeDtypeStruct((count, ND * NO, 2 * LANES), jnp.bfloat16),
            jax.ShapeDtypeStruct((count, ND * NO, LANES), jnp.bfloat16),
        ),
        in_specs=[pl.BlockSpec(memory_space=pltpu.HBM)] * 2,
        out_specs=[pl.BlockSpec(memory_space=pltpu.VMEM)] * 2,
        scratch_shapes=[
            pltpu.VMEM(gradient.shape, gradient.dtype),
            pltpu.VMEM((coupling.shape[0], natoms), jnp.float32),
            pltpu.VMEM((COPIES, count * ND * tiles, LANES), jnp.float32),
            pltpu.VMEM((2, ND * ND * count, LANES), jnp.float32),
            pltpu.SemaphoreType.DMA((NB,)),
            pltpu.SemaphoreType.DMA,
        ],
        compiler_params=pltpu.CompilerParams(vmem_limit_bytes=VMEM_LIMIT),
        cost_estimate=pl.CostEstimate(
            flops=200_000_000, bytes_accessed=6_000_000, transcendentals=0
        ),
        name="tables",
    )(in_hbm(gradient), in_hbm(coupling))


def sandwich_kernel(
    count, natoms, shares, neighbours_hbm, offsets_hbm, local_hbm, below2, below1, above1, above2,
    kernel, derivs, out, neighbours, offsets, local, planes, blocks, sums, sems,
):
    copies = [
        pltpu.make_async_copy(source, target, sems.at[k])
        for k, (source, target) in enumerate(
            ((local_hbm, local), (neighbours_hbm, neighbours), (offsets_hbm, offsets))
        )
    ]
    for copy in copies:
        copy.start()

    tiles = 2 * NO * NO // LANES
    size = tiles * natoms
    lanes = lane_matrix()
    order = row_matrix(tiles, natoms)
    for piece, ref in ((0, below2), (1, below1), (3, above1), (4, above2), (2, local)):
        if ref is local:
            copies[0].wait()
        mixes = [
            exact_dot(stack_tiles(ref[e]), lanes).astype(jnp.bfloat16) for e in range(count)
        ]
        ordered = exact_dot(order, jnp.concatenate(mixes, axis=1))
        for e in range(count):
            planes[piece * count + e] = ordered[:, e * LANES : (e + 1) * LANES]

    copies[1].wait()
    copies[2].wait()
    group = iota((HI, LANES), 1) // NO
    starts = []
    for phonon in range(NW):
        for sign in (1, -1):
            starts.append(2 * count - sign * offsets[phonon])

    def build(atom, carry):
        for e in range(count):
            turned = []
            for s in range(NS):
                part = planes[starts[s] + e, pl.ds(pl.multiple_of(atom * tiles, tiles), tiles), :]
                turned.append(
                    [part] + [pltpu.roll(part, r * NO, axis=1) for r in range(1, COPIES)]
                )
            for c in range(2):
                at = (e * 2 + c) * NO
                for half in range(2):
                    pieces = []
                    for q in range(COPIES):
                        total = None
                        for g in range(min(COPIES, NS - half * COPIES)):
                            part = turned[half * COPIES + g][(g - q) % COPIES][
                                c * HI : (c + 1) * HI
                            ]
                            total = part if total is None else jnp.where(group == g, part, total)
                        pieces.append(total)
                    blocks[atom, at : at + NO, half * LANES : (half + 1) * LANES] = (
                        jnp.concatenate(pieces, axis=0).astype(jnp.bfloat16)
                    )
        return carry

    lax.fori_loop(0, natoms, build, 0, unroll=2)

    groups = 2 * count
    wide = iota((NO, LANES), 1) // NO
    masks = [ones_where(wide == g) for g in range(groups)]
    share = natoms // shares

    def some_atoms(step, carry):
        middles = []
        for k in range(share):
            atom = step * share + k
            middles.append(
                [
                    lax.dot_general(
                        kernel[slot * natoms + atom], blocks[neighbours[slot, atom]], NT,
                        preferred_element_type=jnp.float32,
                    ).astype(jnp.bfloat16)
                    for slot in range(NB)
                ]
            )
        for k in range(share):
            atom = step * share + k
            lefts = []
            rights = []
            for slot in range(NB):
                for i in range(ND):
                    rights.append(middles[k][slot][i * NO : (i + 1) * NO, :])
                    block = derivs[slot * natoms + atom, i * NO : (i + 1) * NO, :]
                    lefts.append(jnp.concatenate([block * mask for mask in masks], axis=0))
            sigma = lax.dot_general(
                jnp.concatenate(lefts, axis=1), jnp.concatenate(rights, axis=1), NT,
                preferred_element_type=jnp.float32,
            )
            for q in range(COPIES):
                part = jnp.concatenate(
                    [sigma[g * NO + q * HI : g * NO + (q + 1) * HI, :] for g in range(groups)],
                    axis=0,
                )
                sums[q, pl.ds(pl.multiple_of(atom * groups * HI, groups * HI), groups * HI), :] = (
                    part.astype(jnp.bfloat16)
                )
        return carry

    lax.fori_loop(0, shares, some_atoms, 0)

    row, col = iota((NO, LANES), 0), iota((NO, LANES), 1)
    placed = None
    for q in range(COPIES):
        place = ones_where((col // NO == q) & (mixed(row) == col % NO))
        term = exact_dot(sums[q], place)
        placed = term if placed is None else placed + term
    out[...] = placed.astype(jnp.bfloat16).reshape(out.shape)


def sandwich(window, kernel, derivs, neighbours, offsets, shares):
    below2, below1, local, above1, above2 = window
    count, natoms, _ = local.shape
    groups = 2 * count
    tiles = 2 * NO * NO // LANES
    rows = natoms * groups * HI
    return pl.pallas_call(
        functools.partial(sandwich_kernel, count, natoms, shares),
        out_shape=jax.ShapeDtypeStruct((shares, rows // shares, LANES), jnp.bfloat16),
        in_specs=[pl.BlockSpec(memory_space=pltpu.HBM)] * 3
        + [pl.BlockSpec(memory_space=pltpu.VMEM)] * 6,
        out_specs=pl.BlockSpec(memory_space=pltpu.VMEM),
        scratch_shapes=[
            pltpu.SMEM(neighbours.shape, jnp.int32),
            pltpu.SMEM(offsets.shape, jnp.int32),
            pltpu.VMEM(local.shape, local.dtype),
            pltpu.VMEM((5 * count, tiles * natoms, LANES), jnp.float32),
            pltpu.VMEM((natoms, groups * NO, 2 * LANES), jnp.bfloat16),
            pltpu.VMEM((COPIES, rows, NO), jnp.bfloat16),
            pltpu.SemaphoreType.DMA((3,)),
        ],
        compiler_params=pltpu.CompilerParams(vmem_limit_bytes=VMEM_LIMIT),
        cost_estimate=pl.CostEstimate(
            flops=800_000_000, bytes_accessed=7_000_000, transcendentals=0
        ),
        name="sandwich",
    )(
        in_hbm(neighbours), in_hbm(offsets), in_hbm(local),
        below2, below1, above1, above2, kernel, derivs,
    )


def combine_kernel(parts, out, total):
    count, share, width = out.shape
    tiles = width // LANES
    summed = parts[0].astype(jnp.float32)
    for k in range(1, parts.shape[0]):
        summed = summed + parts[k].astype(jnp.float32)
    total[...] = summed
    for e in range(count):
        for t in range(tiles):
            out[e, :, t * LANES : (t + 1) * LANES] = total[
                pl.ds(e * tiles + t, share, stride=count * tiles), :
            ]


def combine(parts, count, share):
    return pl.pallas_call(
        combine_kernel,
        out_shape=jax.ShapeDtypeStruct((count, share, 2 * NO * NO), jnp.float32),
        in_specs=[pl.BlockSpec(memory_space=pltpu.VMEM)],
        out_specs=pl.BlockSpec(memory_space=pltpu.VMEM),
        scratch_shapes=[pltpu.VMEM(parts.shape[1:], jnp.float32)],
        name="combine",
    )(parts)


def shifted(array, axis, by):
    length = lax.axis_size(axis)
    pairs = [(i, i + by) for i in range(length) if 0 <= i + by < length]
    return lax.ppermute(array, axis, pairs)


def local_partial(window, coupling, gradient, neighbours, offsets, shares):
    kernel, derivs = tables(gradient, coupling.reshape(-1, 1, coupling.shape[-1]))
    return sandwich(window, kernel, derivs, neighbours.T, offsets, shares)


def body(green, coupling, gradient, neighbours, offsets):
    local_block = green[0]
    count, natoms, _ = local_block.shape
    shares = lax.axis_size("mom")
    window = (
        shifted(local_block, "energy", 2),
        shifted(local_block, "energy", 1),
        local_block,
        shifted(local_block, "energy", -1),
        shifted(local_block, "energy", -2),
    )
    partial_terms = local_partial(window, coupling[0], gradient, neighbours, offsets, shares)
    parts = lax.all_to_all(partial_terms, "mom", 0, 0, tiled=True)
    return combine(parts, count, natoms // shares)


def solution(mesh):
    in_specs = (P("mom", "energy", None, None), P("mom", None, None, None, None), P(), P(), P())
    out_specs = P("energy", "mom", None)
    return jax.shard_map(body, mesh=mesh, in_specs=in_specs, out_specs=out_specs, check_vma=False)
```

time: 45.9 us -> 37.3 us (0.81)
  Pallas kernels: 20.3 us -> 16.4 us
  local copies, waits for them, and re-layouts: 3.36 us -> 0 us
  other arithmetic: 1.26 us -> 0 us
    pallas_call x1, Pallas kernels: 13.6 us -> 7.47 us  [sandwich(): pl.pallas_call(functools.partial(sandwich_kernel, count, natoms, shares),...]
    unnamed x8 -> x0, local copies, waits for them, and re-layouts: 3.27 us -> none
    pallas_call x1, Pallas kernels: 5.19 us -> 7.37 us  [tables(): pl.pallas_call(functools.partial(tables_kernel, natoms), out_shape=(jax.S...]
    unnamed x1 -> x0, other arithmetic: 1.26 us -> none
  transfers between devices with their start and end apart: 4 -> 4, of which waited for: 0 -> 0; matrix products, arithmetic and copies ran while one was open for 3% -> 0% of each run, Pallas kernels for 11% -> 20%
where the time goes in v2:
time: 37.3 us; the launch traced here: 37 us
  Pallas kernels  16.4 us (44%)
  starting transfers between devices  12.7 us (34%)
  blocking collectives  7.77 us (21%)
    ppermute x4, starting transfers between devices, shifted(): return lax.ppermute(array, axis, pairs)  12.7 us
    all_to_all x1, blocking collectives, body(): parts = lax.all_to_all(partial_terms, 'mom', 0, 0, tiled=True)  7.77 us
    pallas_call x1, Pallas kernels, sandwich(): pl.pallas_call(functools.partial(sandwich_kernel, count, natoms, shares),...  7.47 us
    pallas_call x1, Pallas kernels, tables(): pl.pallas_call(functools.partial(tables_kernel, natoms), out_shape=(jax.S...  7.37 us
    pallas_call x1, Pallas kernels, combine(): pl.pallas_call(combine_kernel, out_shape=jax.ShapeDtypeStruct((count, sha...  1.6 us
  transfers between devices with their start and end apart: 4, of which 0 were waited for; matrix products, arithmetic and copies ran while one was open for 0% of the time, Pallas kernels for 20%

profile of v2, /device:TPU:0, one launch (start us, length us, event | category | flops | bytes accessed | tf_op | source)
XLA Modules:
  0.0 37.0 jit_solution(2260057820309644097)
XLA Ops:
  0.0 1.3 %collective-permute-start.3 = (bf16[2,16,2048]{2,1,0:T(8,128)(2,1)}, bf16[2,16,2048]{2,1,0:T(8,128)(2,1)S(1)}, u32[]{:S(2)}, u32[]{:S(2)}) collective-permute-start(bf16[2,16,2048]{2,1,0:T(8,128)(2,1)} %bitcast.3), channel_id=1, source_target_pairs={{8,0},{12,4},{16,8},{20,12},{24,16},{28,20},{9,1},{13,5},{17,9},{2... | collective-permute-start | bytes 393224 | tf_op jit(solution)/shard_map/ppermute | solution.py:356
  1.3 1.3 %collective-permute-start.2 = (bf16[2,16,2048]{2,1,0:T(8,128)(2,1)}, bf16[2,16,2048]{2,1,0:T(8,128)(2,1)S(1)}, u32[]{:S(2)}, u32[]{:S(2)}) collective-permute-start(bf16[2,16,2048]{2,1,0:T(8,128)(2,1)} %bitcast.4), channel_id=1, source_target_pairs={{4,0},{8,4},{12,8},{16,12},{20,16},{24,20},{28,24},{5,1},{9,5},{13... | collective-permute-start | bytes 393224 | tf_op jit(solution)/shard_map/ppermute | solution.py:356
  2.6 5.5 %collective-permute-start.1 = (bf16[2,16,2048]{2,1,0:T(8,128)(2,1)}, bf16[2,16,2048]{2,1,0:T(8,128)(2,1)S(1)}, u32[]{:S(2)}, u32[]{:S(2)}) collective-permute-start(bf16[2,16,2048]{2,1,0:T(8,128)(2,1)} %bitcast.5), channel_id=1, source_target_pairs={{0,4},{4,8},{8,12},{12,16},{16,20},{20,24},{24,28},{1,5},{5,9},{9,... | collective-permute-start | bytes 393224 | tf_op jit(solution)/shard_map/ppermute | solution.py:356
  8.1 4.6 %collective-permute-start = (bf16[2,16,2048]{2,1,0:T(8,128)(2,1)}, bf16[2,16,2048]{2,1,0:T(8,128)(2,1)S(1)}, u32[]{:S(2)}, u32[]{:S(2)}) collective-permute-start(bf16[2,16,2048]{2,1,0:T(8,128)(2,1)} %bitcast.6), channel_id=1, source_target_pairs={{0,8},{4,12},{8,16},{12,20},{16,24},{20,28},{1,9},{5,13},{9,17},{1... | collective-permute-start | bytes 393224 | tf_op jit(solution)/shard_map/ppermute | solution.py:356
  12.7 7.4 %tables.1 = (bf16[80,96,256]{2,1,0:T(8,128)(2,1)S(1)}, bf16[80,96,128]{2,1,0:T(8,128)(2,1)S(1)}) custom-call(bf16[5,3,16,1024]{3,2,1,0:T(8,128)(2,1)} %gradient_hbm.1, f32[270,1,16]{2,1,0:T(1,128)} %bitcast.9), custom_call_target="tpu_custom_call" | custom-call | flops 200000000 | bytes 6000000 | tf_op jit(solution)/shard_map/tables/pallas_call | solution.py:158
  20.1 0.0 collective-permute-done.3.above2
  20.1 0.0 collective-permute-done.2.above1
  20.1 0.0 collective-permute-done.1.below1
  20.1 0.0 collective-permute-done.below2
  20.2 7.5 %sandwich.1 = bf16[4,128,128]{2,1,0:T(8,128)(2,1)S(1)} custom-call(s32[5,16]{1,0:T(8,128)} %bitcast.8, s32[3]{0:T(128)} %offsets_hbm.1, bf16[2,16,2048]{2,1,0:T(8,128)(2,1)} %bitcast.7, bf16[2,16,2048]{2,1,0:T(8,128)(2,1)S(1)} %collective-permute-done.below2, bf16[2,16,2048]{2,1,0:T(8,128)(2,1)S(1)} %collective-permute-done.1.below1, ...), custom_call_target="tpu_custom_call" | custom-call | flops 800000000 | bytes 7000000 | tf_op jit(solution)/shard_map/sandwich/pallas_call | solution.py:302
  27.6 7.8 %all_to_all.5.parts = bf16[4,128,128]{2,1,0:T(8,128)(2,1)} all-to-all(bf16[4,128,128]{2,1,0:T(8,128)(2,1)S(1)} %sandwich.1), channel_id=1, replica_groups=mesh['energy'=8,'mom'=4] {'mom'}, dimensions={0} | all-to-all | bytes 262144 | tf_op jit(solution)/shard_map/all_to_all | solution.py:376
  35.4 1.6 %combine.1 = f32[2,4,2048]{2,1,0:T(4,128)} custom-call(bf16[4,128,128]{2,1,0:T(8,128)(2,1)} %all_to_all.5.parts), custom_call_target="tpu_custom_call" | custom-call | tf_op jit(solution)/shard_map/combine/pallas_call | solution.py:343
Async XLA Ops:
  0.0 20.1 %collective-permute-start.3 = (bf16[2,16,2048]{2,1,0:T(8,128)(2,1)}, bf16[2,16,2048]{2,1,0:T(8,128)(2,1)S(1)}, u32[]{:S(2)}, u32[]{:S(2)}) collective-permute-start(bf16[2,16,2048]{2,1,0:T(8,128)(2,1)} %bitcast.3), channel_id=1, source_target_pairs={{8,0},{12,4},{16,8},{20,12},{24,16},{28,20},{9,1},{13,5},{17,9},{2... | collective-permute-start | bytes 393224 | tf_op jit(solution)/shard_map/ppermute | solution.py:356
  1.3 18.8 %collective-permute-start.2 = (bf16[2,16,2048]{2,1,0:T(8,128)(2,1)}, bf16[2,16,2048]{2,1,0:T(8,128)(2,1)S(1)}, u32[]{:S(2)}, u32[]{:S(2)}) collective-permute-start(bf16[2,16,2048]{2,1,0:T(8,128)(2,1)} %bitcast.4), channel_id=1, source_target_pairs={{4,0},{8,4},{12,8},{16,12},{20,16},{24,20},{28,24},{5,1},{9,5},{13... | collective-permute-start | bytes 393224 | tf_op jit(solution)/shard_map/ppermute | solution.py:356
  2.6 17.5 %collective-permute-start.1 = (bf16[2,16,2048]{2,1,0:T(8,128)(2,1)}, bf16[2,16,2048]{2,1,0:T(8,128)(2,1)S(1)}, u32[]{:S(2)}, u32[]{:S(2)}) collective-permute-start(bf16[2,16,2048]{2,1,0:T(8,128)(2,1)} %bitcast.5), channel_id=1, source_target_pairs={{0,4},{4,8},{8,12},{12,16},{16,20},{20,24},{24,28},{1,5},{5,9},{9,... | collective-permute-start | bytes 393224 | tf_op jit(solution)/shard_map/ppermute | solution.py:356
  8.1 12.1 %collective-permute-start = (bf16[2,16,2048]{2,1,0:T(8,128)(2,1)}, bf16[2,16,2048]{2,1,0:T(8,128)(2,1)S(1)}, u32[]{:S(2)}, u32[]{:S(2)}) collective-permute-start(bf16[2,16,2048]{2,1,0:T(8,128)(2,1)} %bitcast.6), channel_id=1, source_target_pairs={{0,8},{4,12},{8,16},{12,20},{16,24},{20,28},{1,9},{5,13},{9,17},{1... | collective-permute-start | bytes 393224 | tf_op jit(solution)/shard_map/ppermute | solution.py:356

commit v3 on v2

--- a/solution.py
+++ b/solution.py
@@ -65,96 +65,78 @@
 
 def tables_kernel(
     natoms, gradient_hbm, coupling_hbm, kernel_out, derivs_out,
-    gradient, coupling, spread, rows, gradient_sems, coupling_sem,
+    gradient, coupling, rows, sems,
 ):
-    copy_coupling = pltpu.make_async_copy(coupling_hbm.at[:, 0, :], coupling, coupling_sem)
-    copy_coupling.start()
     copies = [
-        pltpu.make_async_copy(gradient_hbm.at[b], gradient.at[b], gradient_sems.at[b])
-        for b in range(NB)
+        pltpu.make_async_copy(coupling_hbm.at[:, 0, :], coupling, sems.at[0]),
+        pltpu.make_async_copy(gradient_hbm, gradient, sems.at[1]),
     ]
     for copy in copies:
         copy.start()
 
     tiles = NO * NO // LANES
     block = natoms * tiles
-    pairs = ND * ND
-    cells = pairs * NB
+    cells = ND * ND * NB
+    depth = rows.shape[2]
     width = -(-NS * cells // LANES) * LANES
     fold = fold_matrix()
     order = row_matrix(tiles, natoms)
     lane = iota((width, 2 * LANES), 0)
     widen = ones_where((lane < NS * cells) & (lane // cells == iota((width, 2 * LANES), 1) // NO))
-    cell = iota((natoms, width), 1)
-    cell = jnp.where(cell < NS * cells, cell % cells, -1)
-
-    copy_coupling.wait()
+    line, lane = iota((NB * depth, width), 0), iota((NB * depth, width), 1)
+    chosen = (lane < NS * cells) & (lane % cells == (line % depth) * NB + line // depth)
+
+    copies[0].wait()
     table = jnp.transpose(coupling[...])
     table = jnp.concatenate(
         [table, jnp.zeros((natoms, width - NS * cells), jnp.float32)], axis=1
     )
-    high = table.astype(jnp.bfloat16)
-    low = (table - high.astype(jnp.float32)).astype(jnp.bfloat16)
-    for half in (high, low):
-        half32 = half.astype(jnp.float32)
-        left = jnp.concatenate(
-            [jnp.where(cell == k, half32, 0.0) for k in range(cells)], axis=0
-        ).astype(jnp.bfloat16)
+    for atom in range(natoms):
+        left = jnp.where(chosen, table[atom : atom + 1, :], 0.0).astype(jnp.bfloat16)
         wide = exact_dot(left, widen)
-        for k in range(2):
-            part = wide[:, k * LANES : (k + 1) * LANES]
-            rows[k] = part if half is high else rows[k] + part
-
+        for slot in range(NB):
+            for half in range(2):
+                rows[atom * NB + slot, half] = wide[
+                    slot * depth : (slot + 1) * depth, half * LANES : (half + 1) * LANES
+                ]
+
+    copies[1].wait()
+    flats = [stack_tiles(gradient[slot, j]) for slot in range(NB) for j in range(ND)]
+    ordered = exact_dot(order, jnp.concatenate(flats, axis=1)).astype(jnp.bfloat16)
     for slot in range(NB):
-        copies[slot].wait()
         for j in range(ND):
-            ordered = exact_dot(order, stack_tiles(gradient[slot, j])).astype(jnp.bfloat16)
-            wide = exact_dot(ordered, fold)
-            for q in range(COPIES):
-                spread[q, (slot * ND + j) * block : (slot * ND + j + 1) * block, :] = wide[
-                    :, q * LANES : (q + 1) * LANES
-                ]
-
-    for slot in range(NB):
-
-        def one_atom(atom, carry):
-            at = slot * natoms + atom
-            derivs = [
-                [
-                    spread[
-                        q,
-                        pl.ds(pl.multiple_of((slot * ND + j) * block + atom * tiles, tiles), tiles),
-                        :,
-                    ]
-                    for q in range(COPIES)
-                ]
-                for j in range(ND)
-            ]
-            for j in range(ND):
-                derivs_out[at, j * NO : (j + 1) * NO, :] = jnp.concatenate(
-                    derivs[j], axis=0
+            at = (slot * ND + j) * LANES
+            wide = exact_dot(ordered[:, at : at + LANES], fold)
+            for atom in range(natoms):
+                derivs_out[atom * NB + slot, j * NO : (j + 1) * NO, :] = jnp.concatenate(
+                    [
+                        wide[atom * tiles : (atom + 1) * tiles, q * LANES : (q + 1) * LANES]
+                        for q in range(COPIES)
+                    ],
+                    axis=0,
                 ).astype(jnp.bfloat16)
-            for i in range(ND):
-                for half in range(2):
-                    total = None
-                    for j in range(ND):
-                        weight = rows[
-                            half, pl.ds(((ND * i + j) * NB + slot) * natoms + atom, 1), :
-                        ]
-                        term = jnp.concatenate([d * weight for d in derivs[j]], axis=0)
-                        total = term if total is None else total + term
-                    kernel_out[
-                        at, i * NO : (i + 1) * NO, half * LANES : (half + 1) * LANES
-                    ] = total.astype(jnp.bfloat16)
-            return carry
-
-        lax.fori_loop(0, natoms, one_atom, 0, unroll=2)
+
+    def one_cell(at, carry):
+        derivs = [
+            derivs_out[at, j * NO : (j + 1) * NO, :].astype(jnp.float32) for j in range(ND)
+        ]
+        for i in range(ND):
+            for half in range(2):
+                total = None
+                for j in range(ND):
+                    term = derivs[j] * rows[at, half, ND * i + j : ND * i + j + 1, :]
+                    total = term if total is None else total + term
+                kernel_out[at, i * NO : (i + 1) * NO, half * LANES : (half + 1) * LANES] = (
+                    total.astype(jnp.bfloat16)
+                )
+        return carry
+
+    lax.fori_loop(0, natoms * NB, one_cell, 0, unroll=4)
 
 
 def tables(gradient, coupling):
     natoms = gradient.shape[2]
     count = NB * natoms
-    tiles = NO * NO // LANES
     return pl.pallas_call(
         functools.partial(tables_kernel, natoms),
         out_shape=(
@@ -166,10 +148,8 @@
         scratch_shapes=[
             pltpu.VMEM(gradient.shape, gradient.dtype),
             pltpu.VMEM((coupling.shape[0], natoms), jnp.float32),
-            pltpu.VMEM((COPIES, count * ND * tiles, LANES), jnp.float32),
-            pltpu.VMEM((2, ND * ND * count, LANES), jnp.float32),
-            pltpu.SemaphoreType.DMA((NB,)),
-            pltpu.SemaphoreType.DMA,
+            pltpu.VMEM((count, 2, 2 * HI, LANES), jnp.float32),
+            pltpu.SemaphoreType.DMA((2,)),
         ],
         compiler_params=pltpu.CompilerParams(vmem_limit_bytes=VMEM_LIMIT),
         cost_estimate=pl.CostEstimate(
@@ -253,7 +233,7 @@
             middles.append(
                 [
                     lax.dot_general(
-                        kernel[slot * natoms + atom], blocks[neighbours[slot, atom]], NT,
+                        kernel[atom * NB + slot], blocks[neighbours[slot, atom]], NT,
                         preferred_element_type=jnp.float32,
                     ).astype(jnp.bfloat16)
                     for slot in range(NB)
@@ -266,7 +246,7 @@
             for slot in range(NB):
                 for i in range(ND):
                     rights.append(middles[k][slot][i * NO : (i + 1) * NO, :])
-                    block = derivs[slot * natoms + atom, i * NO : (i + 1) * NO, :]
+                    block = derivs[atom * NB + slot, i * NO : (i + 1) * NO, :]
                     lefts.append(jnp.concatenate([block * mask for mask in masks], axis=0))
             sigma = lax.dot_general(
                 jnp.concatenate(lefts, axis=1), jnp.concatenate(rights, axis=1), NT,

time: 37.3 us -> 34.2 us (0.917)
  Pallas kernels: 16.4 us -> 13.3 us
    pallas_call x1, Pallas kernels: 7.37 us -> 4.27 us  [tables(): pl.pallas_call(functools.partial(tables_kernel, natoms), out_shape=(jax.S...]
  transfers between devices with their start and end apart: 4 -> 4, of which waited for: 0 -> 0; matrix products, arithmetic and copies ran while one was open for 0% -> 0% of each run, Pallas kernels for 20% -> 13%
where the time goes in v3:
time: 34.2 us; the launch traced here: 33.9 us
  Pallas kernels  13.3 us (39%)
  starting transfers between devices  12.7 us (37%)
  blocking collectives  7.77 us (23%)
    ppermute x4, starting transfers between devices, shifted(): return lax.ppermute(array, axis, pairs)  12.7 us
    all_to_all x1, blocking collectives, body(): parts = lax.all_to_all(partial_terms, 'mom', 0, 0, tiled=True)  7.77 us
    pallas_call x1, Pallas kernels, sandwich(): pl.pallas_call(functools.partial(sandwich_kernel, count, natoms, shares),...  7.47 us
    pallas_call x1, Pallas kernels, tables(): pl.pallas_call(functools.partial(tables_kernel, natoms), out_shape=(jax.S...  4.27 us
    pallas_call x1, Pallas kernels, combine(): pl.pallas_call(combine_kernel, out_shape=jax.ShapeDtypeStruct((count, sha...  1.6 us
  transfers between devices with their start and end apart: 4, of which 0 were waited for; matrix products, arithmetic and copies ran while one was open for 0% of the time, Pallas kernels for 13%

profile of v3, /device:TPU:0, one launch (start us, length us, event | category | flops | bytes accessed | tf_op | source)
XLA Modules:
  0.0 33.9 jit_solution(4497443460263914610)
XLA Ops:
  0.0 1.3 %collective-permute-start.3 = (bf16[2,16,2048]{2,1,0:T(8,128)(2,1)}, bf16[2,16,2048]{2,1,0:T(8,128)(2,1)S(1)}, u32[]{:S(2)}, u32[]{:S(2)}) collective-permute-start(bf16[2,16,2048]{2,1,0:T(8,128)(2,1)} %bitcast.3), channel_id=1, source_target_pairs={{8,0},{12,4},{16,8},{20,12},{24,16},{28,20},{9,1},{13,5},{17,9},{2... | collective-permute-start | bytes 393224 | tf_op jit(solution)/shard_map/ppermute | solution.py:336
  1.3 1.3 %collective-permute-start.2 = (bf16[2,16,2048]{2,1,0:T(8,128)(2,1)}, bf16[2,16,2048]{2,1,0:T(8,128)(2,1)S(1)}, u32[]{:S(2)}, u32[]{:S(2)}) collective-permute-start(bf16[2,16,2048]{2,1,0:T(8,128)(2,1)} %bitcast.4), channel_id=1, source_target_pairs={{4,0},{8,4},{12,8},{16,12},{20,16},{24,20},{28,24},{5,1},{9,5},{13... | collective-permute-start | bytes 393224 | tf_op jit(solution)/shard_map/ppermute | solution.py:336
  2.6 5.5 %collective-permute-start.1 = (bf16[2,16,2048]{2,1,0:T(8,128)(2,1)}, bf16[2,16,2048]{2,1,0:T(8,128)(2,1)S(1)}, u32[]{:S(2)}, u32[]{:S(2)}) collective-permute-start(bf16[2,16,2048]{2,1,0:T(8,128)(2,1)} %bitcast.5), channel_id=1, source_target_pairs={{0,4},{4,8},{8,12},{12,16},{16,20},{20,24},{24,28},{1,5},{5,9},{9,... | collective-permute-start | bytes 393224 | tf_op jit(solution)/shard_map/ppermute | solution.py:336
  8.1 4.6 %collective-permute-start = (bf16[2,16,2048]{2,1,0:T(8,128)(2,1)}, bf16[2,16,2048]{2,1,0:T(8,128)(2,1)S(1)}, u32[]{:S(2)}, u32[]{:S(2)}) collective-permute-start(bf16[2,16,2048]{2,1,0:T(8,128)(2,1)} %bitcast.6), channel_id=1, source_target_pairs={{0,8},{4,12},{8,16},{12,20},{16,24},{20,28},{1,9},{5,13},{9,17},{1... | collective-permute-start | bytes 393224 | tf_op jit(solution)/shard_map/ppermute | solution.py:336
  12.7 4.3 %tables.1 = (bf16[80,96,256]{2,1,0:T(8,128)(2,1)S(1)}, bf16[80,96,128]{2,1,0:T(8,128)(2,1)S(1)}) custom-call(bf16[5,3,16,1024]{3,2,1,0:T(8,128)(2,1)} %gradient_hbm.1, f32[270,1,16]{2,1,0:T(1,128)} %bitcast.9), custom_call_target="tpu_custom_call" | custom-call | flops 200000000 | bytes 6000000 | tf_op jit(solution)/shard_map/tables/pallas_call | solution.py:140
  17.0 0.0 collective-permute-done.3.above2
  17.0 0.0 collective-permute-done.2.above1
  17.0 0.0 collective-permute-done.1.below1
  17.0 0.0 collective-permute-done.below2
  17.1 7.5 %sandwich.1 = bf16[4,128,128]{2,1,0:T(8,128)(2,1)S(1)} custom-call(s32[5,16]{1,0:T(8,128)} %bitcast.8, s32[3]{0:T(128)} %offsets_hbm.1, bf16[2,16,2048]{2,1,0:T(8,128)(2,1)} %bitcast.7, bf16[2,16,2048]{2,1,0:T(8,128)(2,1)S(1)} %collective-permute-done.below2, bf16[2,16,2048]{2,1,0:T(8,128)(2,1)S(1)} %collective-permute-done.1.below1, ...), custom_call_target="tpu_custom_call" | custom-call | flops 800000000 | bytes 7000000 | tf_op jit(solution)/shard_map/sandwich/pallas_call | solution.py:282
  24.5 7.8 %all_to_all.5.parts = bf16[4,128,128]{2,1,0:T(8,128)(2,1)} all-to-all(bf16[4,128,128]{2,1,0:T(8,128)(2,1)S(1)} %sandwich.1), channel_id=1, replica_groups=mesh['energy'=8,'mom'=4] {'mom'}, dimensions={0} | all-to-all | bytes 262144 | tf_op jit(solution)/shard_map/all_to_all | solution.py:356
  32.3 1.6 %combine.1 = f32[2,4,2048]{2,1,0:T(4,128)} custom-call(bf16[4,128,128]{2,1,0:T(8,128)(2,1)} %all_to_all.5.parts), custom_call_target="tpu_custom_call" | custom-call | tf_op jit(solution)/shard_map/combine/pallas_call | solution.py:323
Async XLA Ops:
  0.0 17.0 %collective-permute-start.3 = (bf16[2,16,2048]{2,1,0:T(8,128)(2,1)}, bf16[2,16,2048]{2,1,0:T(8,128)(2,1)S(1)}, u32[]{:S(2)}, u32[]{:S(2)}) collective-permute-start(bf16[2,16,2048]{2,1,0:T(8,128)(2,1)} %bitcast.3), channel_id=1, source_target_pairs={{8,0},{12,4},{16,8},{20,12},{24,16},{28,20},{9,1},{13,5},{17,9},{2... | collective-permute-start | bytes 393224 | tf_op jit(solution)/shard_map/ppermute | solution.py:336
  1.3 15.7 %collective-permute-start.2 = (bf16[2,16,2048]{2,1,0:T(8,128)(2,1)}, bf16[2,16,2048]{2,1,0:T(8,128)(2,1)S(1)}, u32[]{:S(2)}, u32[]{:S(2)}) collective-permute-start(bf16[2,16,2048]{2,1,0:T(8,128)(2,1)} %bitcast.4), channel_id=1, source_target_pairs={{4,0},{8,4},{12,8},{16,12},{20,16},{24,20},{28,24},{5,1},{9,5},{13... | collective-permute-start | bytes 393224 | tf_op jit(solution)/shard_map/ppermute | solution.py:336
  2.6 14.4 %collective-permute-start.1 = (bf16[2,16,2048]{2,1,0:T(8,128)(2,1)}, bf16[2,16,2048]{2,1,0:T(8,128)(2,1)S(1)}, u32[]{:S(2)}, u32[]{:S(2)}) collective-permute-start(bf16[2,16,2048]{2,1,0:T(8,128)(2,1)} %bitcast.5), channel_id=1, source_target_pairs={{0,4},{4,8},{8,12},{12,16},{16,20},{20,24},{24,28},{1,5},{5,9},{9,... | collective-permute-start | bytes 393224 | tf_op jit(solution)/shard_map/ppermute | solution.py:336
  8.1 9.0 %collective-permute-start = (bf16[2,16,2048]{2,1,0:T(8,128)(2,1)}, bf16[2,16,2048]{2,1,0:T(8,128)(2,1)S(1)}, u32[]{:S(2)}, u32[]{:S(2)}) collective-permute-start(bf16[2,16,2048]{2,1,0:T(8,128)(2,1)} %bitcast.6), channel_id=1, source_target_pairs={{0,8},{4,12},{8,16},{12,20},{16,24},{20,28},{1,9},{5,13},{9,17},{1... | collective-permute-start | bytes 393224 | tf_op jit(solution)/shard_map/ppermute | solution.py:336

commit v4 on v3

--- a/solution.py
+++ b/solution.py
@@ -63,13 +63,27 @@
     return jnp.dot(left, right, preferred_element_type=jnp.float32)
 
 
+def make_planes(block, planes, at):
+    count, natoms, size = block.shape
+    mixes = [
+        exact_dot(stack_tiles(block[e]), lane_matrix()).astype(jnp.bfloat16)
+        for e in range(count)
+    ]
+    ordered = exact_dot(
+        row_matrix(size // LANES, natoms), jnp.concatenate(mixes, axis=1)
+    )
+    for e in range(count):
+        planes[at + e] = ordered[:, e * LANES : (e + 1) * LANES]
+
+
 def tables_kernel(
-    natoms, gradient_hbm, coupling_hbm, kernel_out, derivs_out,
-    gradient, coupling, rows, sems,
+    natoms, local_hbm, gradient_hbm, coupling_hbm, kernel_out, derivs_out, planes_out,
+    local, gradient, coupling, rows, sems,
 ):
     copies = [
         pltpu.make_async_copy(coupling_hbm.at[:, 0, :], coupling, sems.at[0]),
         pltpu.make_async_copy(gradient_hbm, gradient, sems.at[1]),
+        pltpu.make_async_copy(local_hbm, local, sems.at[2]),
     ]
     for copy in copies:
         copy.start()
@@ -116,6 +130,9 @@
                     axis=0,
                 ).astype(jnp.bfloat16)
 
+    copies[2].wait()
+    make_planes(local, planes_out, 0)
+
     def one_cell(at, carry):
         derivs = [
             derivs_out[at, j * NO : (j + 1) * NO, :].astype(jnp.float32) for j in range(ND)
@@ -134,60 +151,51 @@
     lax.fori_loop(0, natoms * NB, one_cell, 0, unroll=4)
 
 
-def tables(gradient, coupling):
-    natoms = gradient.shape[2]
+def tables(local, gradient, coupling):
+    energies, natoms, size = local.shape
     count = NB * natoms
     return pl.pallas_call(
         functools.partial(tables_kernel, natoms),
         out_shape=(
             jax.ShapeDtypeStruct((count, ND * NO, 2 * LANES), jnp.bfloat16),
             jax.ShapeDtypeStruct((count, ND * NO, LANES), jnp.bfloat16),
+            jax.ShapeDtypeStruct((energies, natoms * size // LANES, LANES), jnp.float32),
         ),
-        in_specs=[pl.BlockSpec(memory_space=pltpu.HBM)] * 2,
-        out_specs=[pl.BlockSpec(memory_space=pltpu.VMEM)] * 2,
+        in_specs=[pl.BlockSpec(memory_space=pltpu.HBM)] * 3,
+        out_specs=[pl.BlockSpec(memory_space=pltpu.VMEM)] * 3,
         scratch_shapes=[
+            pltpu.VMEM(local.shape, local.dtype),
             pltpu.VMEM(gradient.shape, gradient.dtype),
             pltpu.VMEM((coupling.shape[0], natoms), jnp.float32),
             pltpu.VMEM((count, 2, 2 * HI, LANES), jnp.float32),
-            pltpu.SemaphoreType.DMA((2,)),
+            pltpu.SemaphoreType.DMA((3,)),
         ],
         compiler_params=pltpu.CompilerParams(vmem_limit_bytes=VMEM_LIMIT),
         cost_estimate=pl.CostEstimate(
             flops=200_000_000, bytes_accessed=6_000_000, transcendentals=0
         ),
         name="tables",
-    )(in_hbm(gradient), in_hbm(coupling))
+    )(in_hbm(local), in_hbm(gradient), in_hbm(coupling))
 
 
 def sandwich_kernel(
-    count, natoms, shares, neighbours_hbm, offsets_hbm, local_hbm, below2, below1, above1, above2,
-    kernel, derivs, out, neighbours, offsets, local, planes, blocks, sums, sems,
+    count, natoms, neighbours_hbm, offsets_hbm, middle_planes, below2, below1, above1, above2,
+    kernel, derivs, out, neighbours, offsets, planes, blocks, sems,
 ):
     copies = [
-        pltpu.make_async_copy(source, target, sems.at[k])
-        for k, (source, target) in enumerate(
-            ((local_hbm, local), (neighbours_hbm, neighbours), (offsets_hbm, offsets))
-        )
+        pltpu.make_async_copy(neighbours_hbm, neighbours, sems.at[0]),
+        pltpu.make_async_copy(offsets_hbm, offsets, sems.at[1]),
     ]
     for copy in copies:
         copy.start()
 
     tiles = 2 * NO * NO // LANES
-    size = tiles * natoms
-    lanes = lane_matrix()
-    order = row_matrix(tiles, natoms)
-    for piece, ref in ((0, below2), (1, below1), (3, above1), (4, above2), (2, local)):
-        if ref is local:
-            copies[0].wait()
-        mixes = [
-            exact_dot(stack_tiles(ref[e]), lanes).astype(jnp.bfloat16) for e in range(count)
-        ]
-        ordered = exact_dot(order, jnp.concatenate(mixes, axis=1))
-        for e in range(count):
-            planes[piece * count + e] = ordered[:, e * LANES : (e + 1) * LANES]
-
-    copies[1].wait()
-    copies[2].wait()
+    for piece, ref in ((0, below2), (1, below1), (3, above1), (4, above2)):
+        make_planes(ref, planes, piece * count)
+    planes[2 * count : 3 * count] = middle_planes[...]
+
+    for copy in copies:
+        copy.wait()
     group = iota((HI, LANES), 1) // NO
     starts = []
     for phonon in range(NW):
@@ -219,80 +227,96 @@
                     )
         return carry
 
-    lax.fori_loop(0, natoms, build, 0, unroll=2)
+    lax.fori_loop(0, natoms, build, 0, unroll=4)
 
     groups = 2 * count
     wide = iota((NO, LANES), 1) // NO
     masks = [ones_where(wide == g) for g in range(groups)]
-    share = natoms // shares
-
-    def some_atoms(step, carry):
-        middles = []
-        for k in range(share):
-            atom = step * share + k
-            middles.append(
-                [
-                    lax.dot_general(
-                        kernel[atom * NB + slot], blocks[neighbours[slot, atom]], NT,
-                        preferred_element_type=jnp.float32,
-                    ).astype(jnp.bfloat16)
-                    for slot in range(NB)
-                ]
-            )
-        for k in range(share):
-            atom = step * share + k
-            lefts = []
-            rights = []
-            for slot in range(NB):
-                for i in range(ND):
-                    rights.append(middles[k][slot][i * NO : (i + 1) * NO, :])
-                    block = derivs[atom * NB + slot, i * NO : (i + 1) * NO, :]
-                    lefts.append(jnp.concatenate([block * mask for mask in masks], axis=0))
-            sigma = lax.dot_general(
-                jnp.concatenate(lefts, axis=1), jnp.concatenate(rights, axis=1), NT,
+
+    def middles(pair):
+        parts = [[] for _ in pair]
+        for slot in range(NB):
+            wide = lax.dot_general(
+                jnp.concatenate([kernel[atom * NB + slot] for atom in pair], axis=0),
+                jnp.concatenate([blocks[neighbours[slot, atom]] for atom in pair], axis=0),
+                NT,
                 preferred_element_type=jnp.float32,
             )
-            for q in range(COPIES):
-                part = jnp.concatenate(
-                    [sigma[g * NO + q * HI : g * NO + (q + 1) * HI, :] for g in range(groups)],
-                    axis=0,
+            for k in range(len(pair)):
+                own = wide[
+                    k * ND * NO : (k + 1) * ND * NO, k * groups * NO : (k + 1) * groups * NO
+                ].astype(jnp.bfloat16)
+                for i in range(ND):
+                    block = own[i * NO : (i + 1) * NO, :]
+                    parts[k].append(jnp.concatenate([block * mask for mask in masks], axis=0))
+        return jnp.concatenate([jnp.concatenate(part, axis=1) for part in parts], axis=0)
+
+    def sigmas(pair, right):
+        left = jnp.concatenate(
+            [
+                jnp.concatenate(
+                    [
+                        derivs[atom * NB + slot, i * NO : (i + 1) * NO, :]
+                        for slot in range(NB)
+                        for i in range(ND)
+                    ],
+                    axis=1,
                 )
-                sums[q, pl.ds(pl.multiple_of(atom * groups * HI, groups * HI), groups * HI), :] = (
-                    part.astype(jnp.bfloat16)
-                )
-        return carry
-
-    lax.fori_loop(0, shares, some_atoms, 0)
-
-    row, col = iota((NO, LANES), 0), iota((NO, LANES), 1)
-    placed = None
-    for q in range(COPIES):
-        place = ones_where((col // NO == q) & (mixed(row) == col % NO))
-        term = exact_dot(sums[q], place)
-        placed = term if placed is None else placed + term
-    out[...] = placed.astype(jnp.bfloat16).reshape(out.shape)
-
-
-def sandwich(window, kernel, derivs, neighbours, offsets, shares):
-    below2, below1, local, above1, above2 = window
-    count, natoms, _ = local.shape
+                for atom in pair
+            ],
+            axis=0,
+        )
+        wide = lax.dot_general(left, right, NT, preferred_element_type=jnp.float32)
+        placed = []
+        for k in range(len(pair)):
+            own = wide[k * NO : (k + 1) * NO, k * groups * NO : (k + 1) * groups * NO]
+            rows = [own[q * HI : (q + 1) * HI, :] for q in range(COPIES)]
+            for g in range(groups):
+                total = None
+                for q in range(COPIES):
+                    shift = (q - g) % COPIES * NO
+                    part = pltpu.roll(rows[q], shift, axis=1) if shift else rows[q]
+                    total = part if total is None else jnp.where(group == q, part, total)
+                placed.append(total)
+        return placed
+
+    row, col = iota((LANES, LANES), 0), iota((LANES, LANES), 1)
+    unmix = ones_where((row // NO == col // NO) & (mixed(row % NO) == col % NO))
+    shares = out.shape[0]
+    share = natoms // shares
+    pairs = [tuple(range(a, min(a + 2, natoms))) for a in range(0, natoms, 2)]
+    placed = []
+    step = 0
+    ready = middles(pairs[0])
+    for at, pair in enumerate(pairs):
+        later = middles(pairs[at + 1]) if at + 1 < len(pairs) else None
+        placed.extend(sigmas(pair, ready))
+        ready = later
+        while len(placed) >= share * groups:
+            mine, placed = placed[: share * groups], placed[share * groups :]
+            out[step] = exact_dot(
+                jnp.concatenate(mine, axis=0).astype(jnp.bfloat16), unmix
+            ).astype(jnp.bfloat16)
+            step += 1
+
+
+def sandwich(window, middle_planes, kernel, derivs, neighbours, offsets, shares):
+    below2, below1, above1, above2 = window
+    count, natoms, size = below2.shape
     groups = 2 * count
-    tiles = 2 * NO * NO // LANES
     rows = natoms * groups * HI
     return pl.pallas_call(
-        functools.partial(sandwich_kernel, count, natoms, shares),
+        functools.partial(sandwich_kernel, count, natoms),
         out_shape=jax.ShapeDtypeStruct((shares, rows // shares, LANES), jnp.bfloat16),
-        in_specs=[pl.BlockSpec(memory_space=pltpu.HBM)] * 3
-        + [pl.BlockSpec(memory_space=pltpu.VMEM)] * 6,
+        in_specs=[pl.BlockSpec(memory_space=pltpu.HBM)] * 2
+        + [pl.BlockSpec(memory_space=pltpu.VMEM)] * 7,
         out_specs=pl.BlockSpec(memory_space=pltpu.VMEM),
         scratch_shapes=[
             pltpu.SMEM(neighbours.shape, jnp.int32),
             pltpu.SMEM(offsets.shape, jnp.int32),
-            pltpu.VMEM(local.shape, local.dtype),
-            pltpu.VMEM((5 * count, tiles * natoms, LANES), jnp.float32),
+            pltpu.VMEM((5 * count, natoms * size // LANES, LANES), jnp.float32),
             pltpu.VMEM((natoms, groups * NO, 2 * LANES), jnp.bfloat16),
-            pltpu.VMEM((COPIES, rows, NO), jnp.bfloat16),
-            pltpu.SemaphoreType.DMA((3,)),
+            pltpu.SemaphoreType.DMA((2,)),
         ],
         compiler_params=pltpu.CompilerParams(vmem_limit_bytes=VMEM_LIMIT),
         cost_estimate=pl.CostEstimate(
@@ -300,8 +324,8 @@
         ),
         name="sandwich",
     )(
-        in_hbm(neighbours), in_hbm(offsets), in_hbm(local),
-        below2, below1, above1, above2, kernel, derivs,
+        in_hbm(neighbours), in_hbm(offsets),
+        middle_planes, below2, below1, above1, above2, kernel, derivs,
     )
 
 
@@ -337,8 +361,12 @@
 
 
 def local_partial(window, coupling, gradient, neighbours, offsets, shares):
-    kernel, derivs = tables(gradient, coupling.reshape(-1, 1, coupling.shape[-1]))
-    return sandwich(window, kernel, derivs, neighbours.T, offsets, shares)
+    below2, below1, local, above1, above2 = window
+    kernel, derivs, planes = tables(
+        local, gradient, coupling.reshape(-1, 1, coupling.shape[-1])
+    )
+    remote = (below2, below1, above1, above2)
+    return sandwich(remote, planes, kernel, derivs, neighbours.T, offsets, shares)
 
 
 def body(green, coupling, gradient, neighbours, offsets):

time: 34.2 us -> 34.1 us (level)
  no operation moved by 1% of the time
where the time goes in v4:
time: 34.1 us; the launch traced here: 33.8 us
  Pallas kernels  13.3 us (39%)
  starting transfers between devices  12.7 us (37%)
  blocking collectives  7.77 us (23%)
    ppermute x4, starting transfers between devices, shifted(): return lax.ppermute(array, axis, pairs)  12.7 us
    all_to_all x1, blocking collectives, body(): parts = lax.all_to_all(partial_terms, 'mom', 0, 0, tiled=True)  7.77 us
    pallas_call x1, Pallas kernels, sandwich(): pl.pallas_call(functools.partial(sandwich_kernel, count, natoms), out_sha...  7.17 us
    pallas_call x1, Pallas kernels, tables(): pl.pallas_call(functools.partial(tables_kernel, natoms), out_shape=(jax.S...  4.54 us
    pallas_call x1, Pallas kernels, combine(): pl.pallas_call(combine_kernel, out_shape=jax.ShapeDtypeStruct((count, sha...  1.6 us
  transfers between devices with their start and end apart: 4, of which 0 were waited for; matrix products, arithmetic and copies ran while one was open for 0% of the time, Pallas kernels for 13%

profile of v4, /device:TPU:0, one launch (start us, length us, event | category | flops | bytes accessed | tf_op | source)
XLA Modules:
  0.0 33.8 jit_solution(16422321916368390940)
XLA Ops:
  0.0 1.3 %collective-permute-start.3 = (bf16[2,16,2048]{2,1,0:T(8,128)(2,1)}, bf16[2,16,2048]{2,1,0:T(8,128)(2,1)S(1)}, u32[]{:S(2)}, u32[]{:S(2)}) collective-permute-start(bf16[2,16,2048]{2,1,0:T(8,128)(2,1)} %bitcast.4), channel_id=1, source_target_pairs={{8,0},{12,4},{16,8},{20,12},{24,16},{28,20},{9,1},{13,5},{17,9},{2... | collective-permute-start | bytes 393224 | tf_op jit(solution)/shard_map/ppermute | solution.py:360
  1.3 1.3 %collective-permute-start.2 = (bf16[2,16,2048]{2,1,0:T(8,128)(2,1)}, bf16[2,16,2048]{2,1,0:T(8,128)(2,1)S(1)}, u32[]{:S(2)}, u32[]{:S(2)}) collective-permute-start(bf16[2,16,2048]{2,1,0:T(8,128)(2,1)} %bitcast.5), channel_id=1, source_target_pairs={{4,0},{8,4},{12,8},{16,12},{20,16},{24,20},{28,24},{5,1},{9,5},{13... | collective-permute-start | bytes 393224 | tf_op jit(solution)/shard_map/ppermute | solution.py:360
  2.6 5.5 %collective-permute-start.1 = (bf16[2,16,2048]{2,1,0:T(8,128)(2,1)}, bf16[2,16,2048]{2,1,0:T(8,128)(2,1)S(1)}, u32[]{:S(2)}, u32[]{:S(2)}) collective-permute-start(bf16[2,16,2048]{2,1,0:T(8,128)(2,1)} %bitcast.6), channel_id=1, source_target_pairs={{0,4},{4,8},{8,12},{12,16},{16,20},{20,24},{24,28},{1,5},{5,9},{9,... | collective-permute-start | bytes 393224 | tf_op jit(solution)/shard_map/ppermute | solution.py:360
  8.1 4.6 %collective-permute-start = (bf16[2,16,2048]{2,1,0:T(8,128)(2,1)}, bf16[2,16,2048]{2,1,0:T(8,128)(2,1)S(1)}, u32[]{:S(2)}, u32[]{:S(2)}) collective-permute-start(bf16[2,16,2048]{2,1,0:T(8,128)(2,1)} %bitcast.7), channel_id=1, source_target_pairs={{0,8},{4,12},{8,16},{12,20},{16,24},{20,28},{1,9},{5,13},{9,17},{1... | collective-permute-start | bytes 393224 | tf_op jit(solution)/shard_map/ppermute | solution.py:360
  12.7 4.5 %tables.1 = (bf16[80,96,256]{2,1,0:T(8,128)(2,1)S(1)}, bf16[80,96,128]{2,1,0:T(8,128)(2,1)S(1)}, f32[2,256,128]{2,1,0:T(8,128)S(1)}) custom-call(bf16[2,16,2048]{2,1,0:T(8,128)(2,1)} %bitcast.8, bf16[5,3,16,1024]{3,2,1,0:T(8,128)(2,1)} %gradient_hbm.1, f32[270,1,16]{2,1,0:T(1,128)} %bitcast.3), custom_call_target="tpu_custom_call" | custom-call | flops 200000000 | bytes 6000000 | tf_op jit(solution)/shard_map/tables/pallas_call | solution.py:157
  17.3 0.0 collective-permute-done.3.above2
  17.3 0.0 collective-permute-done.2.above1
  17.3 0.0 collective-permute-done.1.below1
  17.3 0.0 collective-permute-done.below2
  17.3 7.2 %sandwich.1 = bf16[4,128,128]{2,1,0:T(8,128)(2,1)S(1)} custom-call(s32[5,16]{1,0:T(8,128)} %bitcast.9, s32[3]{0:T(128)} %offsets_hbm.1, f32[2,256,128]{2,1,0:T(8,128)S(1)} %get-tuple-element.8.middle_planes, bf16[2,16,2048]{2,1,0:T(8,128)(2,1)S(1)} %collective-permute-done.below2, bf16[2,16,2048]{2,1,0:T(8,128)(2,1)S(1)} %collective-permute-done.1.below1, ...), custom_call_target="tpu_custom_call" | custom-call | flops 800000000 | bytes 7000000 | tf_op jit(solution)/shard_map/sandwich/pallas_call | solution.py:308
  24.5 7.8 %all_to_all.5.parts = bf16[4,128,128]{2,1,0:T(8,128)(2,1)} all-to-all(bf16[4,128,128]{2,1,0:T(8,128)(2,1)S(1)} %sandwich.1), channel_id=1, replica_groups=mesh['energy'=8,'mom'=4] {'mom'}, dimensions={0} | all-to-all | bytes 262144 | tf_op jit(solution)/shard_map/all_to_all | solution.py:384
  32.3 1.6 %combine.1 = f32[2,4,2048]{2,1,0:T(4,128)} custom-call(bf16[4,128,128]{2,1,0:T(8,128)(2,1)} %all_to_all.5.parts), custom_call_target="tpu_custom_call" | custom-call | tf_op jit(solution)/shard_map/combine/pallas_call | solution.py:347
Async XLA Ops:
  0.0 17.3 %collective-permute-start.3 = (bf16[2,16,2048]{2,1,0:T(8,128)(2,1)}, bf16[2,16,2048]{2,1,0:T(8,128)(2,1)S(1)}, u32[]{:S(2)}, u32[]{:S(2)}) collective-permute-start(bf16[2,16,2048]{2,1,0:T(8,128)(2,1)} %bitcast.4), channel_id=1, source_target_pairs={{8,0},{12,4},{16,8},{20,12},{24,16},{28,20},{9,1},{13,5},{17,9},{2... | collective-permute-start | bytes 393224 | tf_op jit(solution)/shard_map/ppermute | solution.py:360
  1.3 16.0 %collective-permute-start.2 = (bf16[2,16,2048]{2,1,0:T(8,128)(2,1)}, bf16[2,16,2048]{2,1,0:T(8,128)(2,1)S(1)}, u32[]{:S(2)}, u32[]{:S(2)}) collective-permute-start(bf16[2,16,2048]{2,1,0:T(8,128)(2,1)} %bitcast.5), channel_id=1, source_target_pairs={{4,0},{8,4},{12,8},{16,12},{20,16},{24,20},{28,24},{5,1},{9,5},{13... | collective-permute-start | bytes 393224 | tf_op jit(solution)/shard_map/ppermute | solution.py:360
  2.6 14.7 %collective-permute-start.1 = (bf16[2,16,2048]{2,1,0:T(8,128)(2,1)}, bf16[2,16,2048]{2,1,0:T(8,128)(2,1)S(1)}, u32[]{:S(2)}, u32[]{:S(2)}) collective-permute-start(bf16[2,16,2048]{2,1,0:T(8,128)(2,1)} %bitcast.6), channel_id=1, source_target_pairs={{0,4},{4,8},{8,12},{12,16},{16,20},{20,24},{24,28},{1,5},{5,9},{9,... | collective-permute-start | bytes 393224 | tf_op jit(solution)/shard_map/ppermute | solution.py:360
  8.1 9.2 %collective-permute-start = (bf16[2,16,2048]{2,1,0:T(8,128)(2,1)}, bf16[2,16,2048]{2,1,0:T(8,128)(2,1)S(1)}, u32[]{:S(2)}, u32[]{:S(2)}) collective-permute-start(bf16[2,16,2048]{2,1,0:T(8,128)(2,1)} %bitcast.7), channel_id=1, source_target_pairs={{0,8},{4,12},{8,16},{12,20},{16,24},{20,28},{1,9},{5,13},{9,17},{1... | collective-permute-start | bytes 393224 | tf_op jit(solution)/shard_map/ppermute | solution.py:360

commit v5 on v4

--- a/solution.py
+++ b/solution.py
@@ -32,25 +32,33 @@
     return jnp.where(condition, 1.0, 0.0).astype(jnp.bfloat16)
 
 
+def over(value, size):
+    return value >> (size.bit_length() - 1) if size & (size - 1) == 0 else value // size
+
+
+def rest(value, size):
+    return value & (size - 1) if size & (size - 1) == 0 else value % size
+
+
 def mixed(lane):
-    return (lane % HI) * COPIES + lane // HI
+    return rest(lane, HI) * COPIES + over(lane, HI)
 
 
 def fold_matrix():
     shape = (LANES, COPIES * LANES)
     row, col = iota(shape, 0), iota(shape, 1)
-    return ones_where(row == (col // LANES) * NO + mixed(col % NO))
+    return ones_where(row == over(col, LANES) * NO + mixed(rest(col, NO)))
 
 
 def lane_matrix():
     row, col = iota((LANES, LANES), 0), iota((LANES, LANES), 1)
-    return ones_where(row == (col // NO) * NO + mixed(col % NO))
+    return ones_where(row == (col - rest(col, NO)) + mixed(rest(col, NO)))
 
 
 def row_matrix(tiles, natoms):
     size = tiles * natoms
     row, col = iota((size, size), 0), iota((size, size), 1)
-    return ones_where(col == (row % tiles) * natoms + row // tiles)
+    return ones_where(col == rest(row, tiles) * natoms + over(row, tiles))
 
 
 def stack_tiles(flat):
@@ -63,15 +71,12 @@
     return jnp.dot(left, right, preferred_element_type=jnp.float32)
 
 
-def make_planes(block, planes, at):
-    count, natoms, size = block.shape
+def make_planes(block, planes, at, lanes, order):
+    count = block.shape[0]
     mixes = [
-        exact_dot(stack_tiles(block[e]), lane_matrix()).astype(jnp.bfloat16)
-        for e in range(count)
+        exact_dot(stack_tiles(block[e]), lanes).astype(jnp.bfloat16) for e in range(count)
     ]
-    ordered = exact_dot(
-        row_matrix(size // LANES, natoms), jnp.concatenate(mixes, axis=1)
-    )
+    ordered = exact_dot(order, jnp.concatenate(mixes, axis=1))
     for e in range(count):
         planes[at + e] = ordered[:, e * LANES : (e + 1) * LANES]
 
@@ -95,10 +100,14 @@
     width = -(-NS * cells // LANES) * LANES
     fold = fold_matrix()
     order = row_matrix(tiles, natoms)
-    lane = iota((width, 2 * LANES), 0)
-    widen = ones_where((lane < NS * cells) & (lane // cells == iota((width, 2 * LANES), 1) // NO))
+    branch = over(iota((width, 2 * LANES), 1), NO)
+    lane = iota((width, 2 * LANES), 0) - branch * cells
+    widen = ones_where((lane >= 0) & (lane < cells) & (branch < NS))
     line, lane = iota((NB * depth, width), 0), iota((NB * depth, width), 1)
-    chosen = (lane < NS * cells) & (lane % cells == (line % depth) * NB + line // depth)
+    lane = lane - (rest(line, depth) * NB + over(line, depth))
+    chosen = lane == 0
+    for s in range(1, NS):
+        chosen = chosen | (lane == s * cells)
 
     copies[0].wait()
     table = jnp.transpose(coupling[...])
@@ -131,7 +140,7 @@
                 ).astype(jnp.bfloat16)
 
     copies[2].wait()
-    make_planes(local, planes_out, 0)
+    make_planes(local, planes_out, 0, lane_matrix(), row_matrix(2 * tiles, natoms))
 
     def one_cell(at, carry):
         derivs = [
@@ -190,13 +199,15 @@
         copy.start()
 
     tiles = 2 * NO * NO // LANES
+    lanes = lane_matrix()
+    order = row_matrix(tiles, natoms)
     for piece, ref in ((0, below2), (1, below1), (3, above1), (4, above2)):
-        make_planes(ref, planes, piece * count)
+        make_planes(ref, planes, piece * count, lanes, order)
     planes[2 * count : 3 * count] = middle_planes[...]
 
     for copy in copies:
         copy.wait()
-    group = iota((HI, LANES), 1) // NO
+    group = over(iota((HI, LANES), 1), NO)
     starts = []
     for phonon in range(NW):
         for sign in (1, -1):
@@ -230,7 +241,7 @@
     lax.fori_loop(0, natoms, build, 0, unroll=4)
 
     groups = 2 * count
-    wide = iota((NO, LANES), 1) // NO
+    wide = over(iota((NO, LANES), 1), NO)
     masks = [ones_where(wide == g) for g in range(groups)]
 
     def middles(pair):
@@ -281,7 +292,7 @@
         return placed
 
     row, col = iota((LANES, LANES), 0), iota((LANES, LANES), 1)
-    unmix = ones_where((row // NO == col // NO) & (mixed(row % NO) == col % NO))
+    unmix = ones_where(col == (row - rest(row, NO)) + mixed(rest(row, NO)))
     shares = out.shape[0]
     share = natoms // shares
     pairs = [tuple(range(a, min(a + 2, natoms))) for a in range(0, natoms, 2)]

time: 34.1 us -> 34.2 us (level)
  transfers between devices with their start and end apart: 4 -> 4, of which waited for: 0 -> 0; matrix products, arithmetic and copies ran while one was open for 0% -> 0% of each run, Pallas kernels for 13% -> 14%
where the time goes in v5:
time: 34.2 us; the launch traced here: 33.9 us
  Pallas kernels  13.4 us (39%)
  starting transfers between devices  12.7 us (37%)
  blocking collectives  7.76 us (23%)
    ppermute x4, starting transfers between devices, shifted(): return lax.ppermute(array, axis, pairs)  12.7 us
    all_to_all x1, blocking collectives, body(): parts = lax.all_to_all(partial_terms, 'mom', 0, 0, tiled=True)  7.76 us
    pallas_call x1, Pallas kernels, sandwich(): pl.pallas_call(functools.partial(sandwich_kernel, count, natoms), out_sha...  7.18 us
    pallas_call x1, Pallas kernels, tables(): pl.pallas_call(functools.partial(tables_kernel, natoms), out_shape=(jax.S...  4.58 us
    pallas_call x1, Pallas kernels, combine(): pl.pallas_call(combine_kernel, out_shape=jax.ShapeDtypeStruct((count, sha...  1.6 us
  transfers between devices with their start and end apart: 4, of which 0 were waited for; matrix products, arithmetic and copies ran while one was open for 0% of the time, Pallas kernels for 14%

profile of v5, /device:TPU:0, one launch (start us, length us, event | category | flops | bytes accessed | tf_op | source)
XLA Modules:
  0.0 33.9 jit_solution(7682054538853483426)
XLA Ops:
  0.0 1.3 %collective-permute-start.3 = (bf16[2,16,2048]{2,1,0:T(8,128)(2,1)}, bf16[2,16,2048]{2,1,0:T(8,128)(2,1)S(1)}, u32[]{:S(2)}, u32[]{:S(2)}) collective-permute-start(bf16[2,16,2048]{2,1,0:T(8,128)(2,1)} %bitcast.4), channel_id=1, source_target_pairs={{8,0},{12,4},{16,8},{20,12},{24,16},{28,20},{9,1},{13,5},{17,9},{2... | collective-permute-start | bytes 393224 | tf_op jit(solution)/shard_map/ppermute | solution.py:371
  1.3 1.3 %collective-permute-start.2 = (bf16[2,16,2048]{2,1,0:T(8,128)(2,1)}, bf16[2,16,2048]{2,1,0:T(8,128)(2,1)S(1)}, u32[]{:S(2)}, u32[]{:S(2)}) collective-permute-start(bf16[2,16,2048]{2,1,0:T(8,128)(2,1)} %bitcast.5), channel_id=1, source_target_pairs={{4,0},{8,4},{12,8},{16,12},{20,16},{24,20},{28,24},{5,1},{9,5},{13... | collective-permute-start | bytes 393224 | tf_op jit(solution)/shard_map/ppermute | solution.py:371
  2.6 5.5 %collective-permute-start.1 = (bf16[2,16,2048]{2,1,0:T(8,128)(2,1)}, bf16[2,16,2048]{2,1,0:T(8,128)(2,1)S(1)}, u32[]{:S(2)}, u32[]{:S(2)}) collective-permute-start(bf16[2,16,2048]{2,1,0:T(8,128)(2,1)} %bitcast.6), channel_id=1, source_target_pairs={{0,4},{4,8},{8,12},{12,16},{16,20},{20,24},{24,28},{1,5},{5,9},{9,... | collective-permute-start | bytes 393224 | tf_op jit(solution)/shard_map/ppermute | solution.py:371
  8.1 4.6 %collective-permute-start = (bf16[2,16,2048]{2,1,0:T(8,128)(2,1)}, bf16[2,16,2048]{2,1,0:T(8,128)(2,1)S(1)}, u32[]{:S(2)}, u32[]{:S(2)}) collective-permute-start(bf16[2,16,2048]{2,1,0:T(8,128)(2,1)} %bitcast.7), channel_id=1, source_target_pairs={{0,8},{4,12},{8,16},{12,20},{16,24},{20,28},{1,9},{5,13},{9,17},{1... | collective-permute-start | bytes 393224 | tf_op jit(solution)/shard_map/ppermute | solution.py:371
  12.7 4.6 %tables.1 = (bf16[80,96,256]{2,1,0:T(8,128)(2,1)S(1)}, bf16[80,96,128]{2,1,0:T(8,128)(2,1)S(1)}, f32[2,256,128]{2,1,0:T(8,128)S(1)}) custom-call(bf16[2,16,2048]{2,1,0:T(8,128)(2,1)} %bitcast.8, bf16[5,3,16,1024]{3,2,1,0:T(8,128)(2,1)} %gradient_hbm.1, f32[270,1,16]{2,1,0:T(1,128)} %bitcast.3), custom_call_target="tpu_custom_call" | custom-call | flops 200000000 | bytes 6000000 | tf_op jit(solution)/shard_map/tables/pallas_call | solution.py:166
  17.3 0.0 collective-permute-done.3.above2
  17.3 0.0 collective-permute-done.2.above1
  17.3 0.0 collective-permute-done.1.below1
  17.3 0.0 collective-permute-done.below2
  17.3 7.2 %sandwich.1 = bf16[4,128,128]{2,1,0:T(8,128)(2,1)S(1)} custom-call(s32[5,16]{1,0:T(8,128)} %bitcast.9, s32[3]{0:T(128)} %offsets_hbm.1, f32[2,256,128]{2,1,0:T(8,128)S(1)} %get-tuple-element.8.middle_planes, bf16[2,16,2048]{2,1,0:T(8,128)(2,1)S(1)} %collective-permute-done.below2, bf16[2,16,2048]{2,1,0:T(8,128)(2,1)S(1)} %collective-permute-done.1.below1, ...), custom_call_target="tpu_custom_call" | custom-call | flops 800000000 | bytes 7000000 | tf_op jit(solution)/shard_map/sandwich/pallas_call | solution.py:319
  24.5 7.8 %all_to_all.5.parts = bf16[4,128,128]{2,1,0:T(8,128)(2,1)} all-to-all(bf16[4,128,128]{2,1,0:T(8,128)(2,1)S(1)} %sandwich.1), channel_id=1, replica_groups=mesh['energy'=8,'mom'=4] {'mom'}, dimensions={0} | all-to-all | bytes 262144 | tf_op jit(solution)/shard_map/all_to_all | solution.py:395
  32.3 1.6 %combine.1 = f32[2,4,2048]{2,1,0:T(4,128)} custom-call(bf16[4,128,128]{2,1,0:T(8,128)(2,1)} %all_to_all.5.parts), custom_call_target="tpu_custom_call" | custom-call | tf_op jit(solution)/shard_map/combine/pallas_call | solution.py:358
Async XLA Ops:
  0.0 17.3 %collective-permute-start.3 = (bf16[2,16,2048]{2,1,0:T(8,128)(2,1)}, bf16[2,16,2048]{2,1,0:T(8,128)(2,1)S(1)}, u32[]{:S(2)}, u32[]{:S(2)}) collective-permute-start(bf16[2,16,2048]{2,1,0:T(8,128)(2,1)} %bitcast.4), channel_id=1, source_target_pairs={{8,0},{12,4},{16,8},{20,12},{24,16},{28,20},{9,1},{13,5},{17,9},{2... | collective-permute-start | bytes 393224 | tf_op jit(solution)/shard_map/ppermute | solution.py:371
  1.3 16.0 %collective-permute-start.2 = (bf16[2,16,2048]{2,1,0:T(8,128)(2,1)}, bf16[2,16,2048]{2,1,0:T(8,128)(2,1)S(1)}, u32[]{:S(2)}, u32[]{:S(2)}) collective-permute-start(bf16[2,16,2048]{2,1,0:T(8,128)(2,1)} %bitcast.5), channel_id=1, source_target_pairs={{4,0},{8,4},{12,8},{16,12},{20,16},{24,20},{28,24},{5,1},{9,5},{13... | collective-permute-start | bytes 393224 | tf_op jit(solution)/shard_map/ppermute | solution.py:371
  2.6 14.7 %collective-permute-start.1 = (bf16[2,16,2048]{2,1,0:T(8,128)(2,1)}, bf16[2,16,2048]{2,1,0:T(8,128)(2,1)S(1)}, u32[]{:S(2)}, u32[]{:S(2)}) collective-permute-start(bf16[2,16,2048]{2,1,0:T(8,128)(2,1)} %bitcast.6), channel_id=1, source_target_pairs={{0,4},{4,8},{8,12},{12,16},{16,20},{20,24},{24,28},{1,5},{5,9},{9,... | collective-permute-start | bytes 393224 | tf_op jit(solution)/shard_map/ppermute | solution.py:371
  8.1 9.3 %collective-permute-start = (bf16[2,16,2048]{2,1,0:T(8,128)(2,1)}, bf16[2,16,2048]{2,1,0:T(8,128)(2,1)S(1)}, u32[]{:S(2)}, u32[]{:S(2)}) collective-permute-start(bf16[2,16,2048]{2,1,0:T(8,128)(2,1)} %bitcast.7), channel_id=1, source_target_pairs={{0,8},{4,12},{8,16},{12,20},{16,24},{20,28},{1,9},{5,13},{9,17},{1... | collective-permute-start | bytes 393224 | tf_op jit(solution)/shard_map/ppermute | solution.py:371

commit v6 on v5

--- a/solution.py
+++ b/solution.py
@@ -44,15 +44,18 @@
     return rest(lane, HI) * COPIES + over(lane, HI)
 
 
+def group_of(lane):
+    return over(lane, 2 * NO) * 2 + rest(over(lane, HI), 2)
+
+
+def orbital_of(lane):
+    return rest(lane, HI) * COPIES + rest(over(lane, 2 * HI), COPIES)
+
+
 def fold_matrix():
     shape = (LANES, COPIES * LANES)
     row, col = iota(shape, 0), iota(shape, 1)
-    return ones_where(row == over(col, LANES) * NO + mixed(rest(col, NO)))
-
-
-def lane_matrix():
-    row, col = iota((LANES, LANES), 0), iota((LANES, LANES), 1)
-    return ones_where(row == (col - rest(col, NO)) + mixed(rest(col, NO)))
+    return ones_where(row == over(col, LANES) * NO + orbital_of(rest(col, LANES)))
 
 
 def row_matrix(tiles, natoms):
@@ -71,12 +74,11 @@
     return jnp.dot(left, right, preferred_element_type=jnp.float32)
 
 
-def make_planes(block, planes, at, lanes, order):
+def make_planes(block, planes, at, order):
     count = block.shape[0]
-    mixes = [
-        exact_dot(stack_tiles(block[e]), lanes).astype(jnp.bfloat16) for e in range(count)
-    ]
-    ordered = exact_dot(order, jnp.concatenate(mixes, axis=1))
+    ordered = exact_dot(
+        order, jnp.concatenate([stack_tiles(block[e]) for e in range(count)], axis=1)
+    ).astype(jnp.bfloat16)
     for e in range(count):
         planes[at + e] = ordered[:, e * LANES : (e + 1) * LANES]
 
@@ -100,7 +102,8 @@
     width = -(-NS * cells // LANES) * LANES
     fold = fold_matrix()
     order = row_matrix(tiles, natoms)
-    branch = over(iota((width, 2 * LANES), 1), NO)
+    lane = iota((width, 2 * LANES), 1)
+    branch = over(lane, LANES) * COPIES + group_of(rest(lane, LANES))
     lane = iota((width, 2 * LANES), 0) - branch * cells
     widen = ones_where((lane >= 0) & (lane < cells) & (branch < NS))
     line, lane = iota((NB * depth, width), 0), iota((NB * depth, width), 1)
@@ -140,7 +143,7 @@
                 ).astype(jnp.bfloat16)
 
     copies[2].wait()
-    make_planes(local, planes_out, 0, lane_matrix(), row_matrix(2 * tiles, natoms))
+    make_planes(local, planes_out, 0, row_matrix(2 * tiles, natoms))
 
     def one_cell(at, carry):
         derivs = [
@@ -168,7 +171,7 @@
         out_shape=(
             jax.ShapeDtypeStruct((count, ND * NO, 2 * LANES), jnp.bfloat16),
             jax.ShapeDtypeStruct((count, ND * NO, LANES), jnp.bfloat16),
-            jax.ShapeDtypeStruct((energies, natoms * size // LANES, LANES), jnp.float32),
+            jax.ShapeDtypeStruct((energies, natoms * size // LANES, LANES), jnp.bfloat16),
         ),
         in_specs=[pl.BlockSpec(memory_space=pltpu.HBM)] * 3,
         out_specs=[pl.BlockSpec(memory_space=pltpu.VMEM)] * 3,
@@ -199,50 +202,37 @@
         copy.start()
 
     tiles = 2 * NO * NO // LANES
-    lanes = lane_matrix()
+    groups = 2 * count
     order = row_matrix(tiles, natoms)
     for piece, ref in ((0, below2), (1, below1), (3, above1), (4, above2)):
-        make_planes(ref, planes, piece * count, lanes, order)
+        make_planes(ref, planes, piece * count, order)
     planes[2 * count : 3 * count] = middle_planes[...]
 
+    fold = fold_matrix()
+    group = group_of(rest(iota(fold.shape, 1), LANES))
+    places = [fold * ones_where(group == g) for g in range(COPIES)]
     for copy in copies:
         copy.wait()
+    for e in range(count):
+        for half in range(2):
+            branches = range(half * COPIES, min(NS, (half + 1) * COPIES))
+            shifted_planes = [
+                planes[2 * count + e - (1 - 2 * (s % 2)) * offsets[s // 2]] for s in branches
+            ]
+            wide = exact_dot(
+                jnp.concatenate(shifted_planes, axis=1),
+                jnp.concatenate(places[: len(branches)], axis=0),
+            ).astype(jnp.bfloat16)
+            for atom in range(natoms):
+                for q in range(COPIES):
+                    at = (e * COPIES + q) * tiles
+                    blocks[atom, at : at + tiles, half * LANES : (half + 1) * LANES] = wide[
+                        atom * tiles : (atom + 1) * tiles, q * LANES : (q + 1) * LANES
+                    ]
+
+    lane_group = group_of(iota((NO, LANES), 1))
+    masks = [ones_where(lane_group == g) for g in range(groups)]
     group = over(iota((HI, LANES), 1), NO)
-    starts = []
-    for phonon in range(NW):
-        for sign in (1, -1):
-            starts.append(2 * count - sign * offsets[phonon])
-
-    def build(atom, carry):
-        for e in range(count):
-            turned = []
-            for s in range(NS):
-                part = planes[starts[s] + e, pl.ds(pl.multiple_of(atom * tiles, tiles), tiles), :]
-                turned.append(
-                    [part] + [pltpu.roll(part, r * NO, axis=1) for r in range(1, COPIES)]
-                )
-            for c in range(2):
-                at = (e * 2 + c) * NO
-                for half in range(2):
-                    pieces = []
-                    for q in range(COPIES):
-                        total = None
-                        for g in range(min(COPIES, NS - half * COPIES)):
-                            part = turned[half * COPIES + g][(g - q) % COPIES][
-                                c * HI : (c + 1) * HI
-                            ]
-                            total = part if total is None else jnp.where(group == g, part, total)
-                        pieces.append(total)
-                    blocks[atom, at : at + NO, half * LANES : (half + 1) * LANES] = (
-                        jnp.concatenate(pieces, axis=0).astype(jnp.bfloat16)
-                    )
-        return carry
-
-    lax.fori_loop(0, natoms, build, 0, unroll=4)
-
-    groups = 2 * count
-    wide = over(iota((NO, LANES), 1), NO)
-    masks = [ones_where(wide == g) for g in range(groups)]
 
     def middles(pair):
         parts = [[] for _ in pair]
@@ -325,7 +315,7 @@
         scratch_shapes=[
             pltpu.SMEM(neighbours.shape, jnp.int32),
             pltpu.SMEM(offsets.shape, jnp.int32),
-            pltpu.VMEM((5 * count, natoms * size // LANES, LANES), jnp.float32),
+            pltpu.VMEM((5 * count, natoms * size // LANES, LANES), jnp.bfloat16),
             pltpu.VMEM((natoms, groups * NO, 2 * LANES), jnp.bfloat16),
             pltpu.SemaphoreType.DMA((2,)),
         ],

time: 34.2 us -> 33.8 us (0.988)
  Pallas kernels: 13.4 us -> 13 us
  transfers between devices with their start and end apart: 4 -> 4, of which waited for: 0 -> 0; matrix products, arithmetic and copies ran while one was open for 0% -> 0% of each run, Pallas kernels for 14% -> 13%
where the time goes in v6:
time: 33.8 us; the launch traced here: 33.5 us
  Pallas kernels  13 us (38%)
  starting transfers between devices  12.7 us (38%)
  blocking collectives  7.75 us (23%)
    ppermute x4, starting transfers between devices, shifted(): return lax.ppermute(array, axis, pairs)  12.7 us
    all_to_all x1, blocking collectives, body(): parts = lax.all_to_all(partial_terms, 'mom', 0, 0, tiled=True)  7.75 us
    pallas_call x1, Pallas kernels, sandwich(): pl.pallas_call(functools.partial(sandwich_kernel, count, natoms), out_sha...  6.98 us
    pallas_call x1, Pallas kernels, tables(): pl.pallas_call(functools.partial(tables_kernel, natoms), out_shape=(jax.S...  4.44 us
    pallas_call x1, Pallas kernels, combine(): pl.pallas_call(combine_kernel, out_shape=jax.ShapeDtypeStruct((count, sha...  1.6 us
  transfers between devices with their start and end apart: 4, of which 0 were waited for; matrix products, arithmetic and copies ran while one was open for 0% of the time, Pallas kernels for 13%

profile of v6, /device:TPU:0, one launch (start us, length us, event | category | flops | bytes accessed | tf_op | source)
XLA Modules:
  0.0 33.5 jit_solution(2835790780551211852)
XLA Ops:
  0.0 1.3 %collective-permute-start.3 = (bf16[2,16,2048]{2,1,0:T(8,128)(2,1)}, bf16[2,16,2048]{2,1,0:T(8,128)(2,1)S(1)}, u32[]{:S(2)}, u32[]{:S(2)}) collective-permute-start(bf16[2,16,2048]{2,1,0:T(8,128)(2,1)} %bitcast.4), channel_id=1, source_target_pairs={{8,0},{12,4},{16,8},{20,12},{24,16},{28,20},{9,1},{13,5},{17,9},{2... | collective-permute-start | bytes 393224 | tf_op jit(solution)/shard_map/ppermute | solution.py:361
  1.3 1.3 %collective-permute-start.2 = (bf16[2,16,2048]{2,1,0:T(8,128)(2,1)}, bf16[2,16,2048]{2,1,0:T(8,128)(2,1)S(1)}, u32[]{:S(2)}, u32[]{:S(2)}) collective-permute-start(bf16[2,16,2048]{2,1,0:T(8,128)(2,1)} %bitcast.5), channel_id=1, source_target_pairs={{4,0},{8,4},{12,8},{16,12},{20,16},{24,20},{28,24},{5,1},{9,5},{13... | collective-permute-start | bytes 393224 | tf_op jit(solution)/shard_map/ppermute | solution.py:361
  2.6 5.5 %collective-permute-start.1 = (bf16[2,16,2048]{2,1,0:T(8,128)(2,1)}, bf16[2,16,2048]{2,1,0:T(8,128)(2,1)S(1)}, u32[]{:S(2)}, u32[]{:S(2)}) collective-permute-start(bf16[2,16,2048]{2,1,0:T(8,128)(2,1)} %bitcast.6), channel_id=1, source_target_pairs={{0,4},{4,8},{8,12},{12,16},{16,20},{20,24},{24,28},{1,5},{5,9},{9,... | collective-permute-start | bytes 393224 | tf_op jit(solution)/shard_map/ppermute | solution.py:361
  8.1 4.6 %collective-permute-start = (bf16[2,16,2048]{2,1,0:T(8,128)(2,1)}, bf16[2,16,2048]{2,1,0:T(8,128)(2,1)S(1)}, u32[]{:S(2)}, u32[]{:S(2)}) collective-permute-start(bf16[2,16,2048]{2,1,0:T(8,128)(2,1)} %bitcast.7), channel_id=1, source_target_pairs={{0,8},{4,12},{8,16},{12,20},{16,24},{20,28},{1,9},{5,13},{9,17},{1... | collective-permute-start | bytes 393224 | tf_op jit(solution)/shard_map/ppermute | solution.py:361
  12.7 4.4 %tables.1 = (bf16[80,96,256]{2,1,0:T(8,128)(2,1)S(1)}, bf16[80,96,128]{2,1,0:T(8,128)(2,1)S(1)}, bf16[2,256,128]{2,1,0:T(8,128)(2,1)S(1)}) custom-call(bf16[2,16,2048]{2,1,0:T(8,128)(2,1)} %bitcast.8, bf16[5,3,16,1024]{3,2,1,0:T(8,128)(2,1)} %gradient_hbm.1, f32[270,1,16]{2,1,0:T(1,128)} %bitcast.3), custom_call_target="tpu_custom_call" | custom-call | flops 200000000 | bytes 6000000 | tf_op jit(solution)/shard_map/tables/pallas_call | solution.py:169
  17.2 0.0 collective-permute-done.3.above2
  17.2 0.0 collective-permute-done.2.above1
  17.2 0.0 collective-permute-done.1.below1
  17.2 0.0 collective-permute-done.below2
  17.2 7.0 %sandwich.1 = bf16[4,128,128]{2,1,0:T(8,128)(2,1)S(1)} custom-call(s32[5,16]{1,0:T(8,128)} %bitcast.9, s32[3]{0:T(128)} %offsets_hbm.1, bf16[2,256,128]{2,1,0:T(8,128)(2,1)S(1)} %get-tuple-element.8.middle_planes, bf16[2,16,2048]{2,1,0:T(8,128)(2,1)S(1)} %collective-permute-done.below2, bf16[2,16,2048]{2,1,0:T(8,128)(2,1)S(1)} %collective-permute-done.1.below1, ...), custom_call_target="tpu_custom_call" | custom-call | flops 800000000 | bytes 7000000 | tf_op jit(solution)/shard_map/sandwich/pallas_call | solution.py:309
  24.2 7.7 %all_to_all.5.parts = bf16[4,128,128]{2,1,0:T(8,128)(2,1)} all-to-all(bf16[4,128,128]{2,1,0:T(8,128)(2,1)S(1)} %sandwich.1), channel_id=1, replica_groups=mesh['energy'=8,'mom'=4] {'mom'}, dimensions={0} | all-to-all | bytes 262144 | tf_op jit(solution)/shard_map/all_to_all | solution.py:385
  31.9 1.6 %combine.1 = f32[2,4,2048]{2,1,0:T(4,128)} custom-call(bf16[4,128,128]{2,1,0:T(8,128)(2,1)} %all_to_all.5.parts), custom_call_target="tpu_custom_call" | custom-call | tf_op jit(solution)/shard_map/combine/pallas_call | solution.py:348
Async XLA Ops:
  0.0 17.2 %collective-permute-start.3 = (bf16[2,16,2048]{2,1,0:T(8,128)(2,1)}, bf16[2,16,2048]{2,1,0:T(8,128)(2,1)S(1)}, u32[]{:S(2)}, u32[]{:S(2)}) collective-permute-start(bf16[2,16,2048]{2,1,0:T(8,128)(2,1)} %bitcast.4), channel_id=1, source_target_pairs={{8,0},{12,4},{16,8},{20,12},{24,16},{28,20},{9,1},{13,5},{17,9},{2... | collective-permute-start | bytes 393224 | tf_op jit(solution)/shard_map/ppermute | solution.py:361
  1.3 15.9 %collective-permute-start.2 = (bf16[2,16,2048]{2,1,0:T(8,128)(2,1)}, bf16[2,16,2048]{2,1,0:T(8,128)(2,1)S(1)}, u32[]{:S(2)}, u32[]{:S(2)}) collective-permute-start(bf16[2,16,2048]{2,1,0:T(8,128)(2,1)} %bitcast.5), channel_id=1, source_target_pairs={{4,0},{8,4},{12,8},{16,12},{20,16},{24,20},{28,24},{5,1},{9,5},{13... | collective-permute-start | bytes 393224 | tf_op jit(solution)/shard_map/ppermute | solution.py:361
  2.6 14.6 %collective-permute-start.1 = (bf16[2,16,2048]{2,1,0:T(8,128)(2,1)}, bf16[2,16,2048]{2,1,0:T(8,128)(2,1)S(1)}, u32[]{:S(2)}, u32[]{:S(2)}) collective-permute-start(bf16[2,16,2048]{2,1,0:T(8,128)(2,1)} %bitcast.6), channel_id=1, source_target_pairs={{0,4},{4,8},{8,12},{12,16},{16,20},{20,24},{24,28},{1,5},{5,9},{9,... | collective-permute-start | bytes 393224 | tf_op jit(solution)/shard_map/ppermute | solution.py:361
  8.1 9.1 %collective-permute-start = (bf16[2,16,2048]{2,1,0:T(8,128)(2,1)}, bf16[2,16,2048]{2,1,0:T(8,128)(2,1)S(1)}, u32[]{:S(2)}, u32[]{:S(2)}) collective-permute-start(bf16[2,16,2048]{2,1,0:T(8,128)(2,1)} %bitcast.7), channel_id=1, source_target_pairs={{0,8},{4,12},{8,16},{12,20},{16,24},{20,28},{1,9},{5,13},{9,17},{1... | collective-permute-start | bytes 393224 | tf_op jit(solution)/shard_map/ppermute | solution.py:361

commit v7 on v6

--- a/solution.py
+++ b/solution.py
@@ -285,20 +285,19 @@
     unmix = ones_where(col == (row - rest(row, NO)) + mixed(rest(row, NO)))
     shares = out.shape[0]
     share = natoms // shares
-    pairs = [tuple(range(a, min(a + 2, natoms))) for a in range(0, natoms, 2)]
-    placed = []
-    step = 0
-    ready = middles(pairs[0])
-    for at, pair in enumerate(pairs):
-        later = middles(pairs[at + 1]) if at + 1 < len(pairs) else None
-        placed.extend(sigmas(pair, ready))
-        ready = later
-        while len(placed) >= share * groups:
-            mine, placed = placed[: share * groups], placed[share * groups :]
-            out[step] = exact_dot(
-                jnp.concatenate(mine, axis=0).astype(jnp.bfloat16), unmix
-            ).astype(jnp.bfloat16)
-            step += 1
+
+    def one_share(step, carry):
+        atoms = [step * share + k for k in range(share)]
+        pairs = [atoms[k : k + 2] for k in range(0, share, 2)]
+        placed = []
+        for pair, right in zip(pairs, [middles(pair) for pair in pairs]):
+            placed.extend(sigmas(pair, right))
+        out[step] = exact_dot(
+            jnp.concatenate(placed, axis=0).astype(jnp.bfloat16), unmix
+        ).astype(jnp.bfloat16)
+        return carry
+
+    lax.fori_loop(0, shares, one_share, 0)
 
 
 def sandwich(window, middle_planes, kernel, derivs, neighbours, offsets, shares):

time: 33.8 us -> 33.6 us (level)
  no operation moved by 1% of the time
where the time goes in v7:
time: 33.6 us; the launch traced here: 33.3 us
  Pallas kernels  12.8 us (38%)
  starting transfers between devices  12.7 us (38%)
  blocking collectives  7.76 us (23%)
    ppermute x4, starting transfers between devices, shifted(): return lax.ppermute(array, axis, pairs)  12.7 us
    all_to_all x1, blocking collectives, body(): parts = lax.all_to_all(partial_terms, 'mom', 0, 0, tiled=True)  7.76 us
    pallas_call x1, Pallas kernels, sandwich(): pl.pallas_call(functools.partial(sandwich_kernel, count, natoms), out_sha...  6.78 us
    pallas_call x1, Pallas kernels, tables(): pl.pallas_call(functools.partial(tables_kernel, natoms), out_shape=(jax.S...  4.44 us
    pallas_call x1, Pallas kernels, combine(): pl.pallas_call(combine_kernel, out_shape=jax.ShapeDtypeStruct((count, sha...  1.6 us
  transfers between devices with their start and end apart: 4, of which 0 were waited for; matrix products, arithmetic and copies ran while one was open for 0% of the time, Pallas kernels for 13%

profile of v7, /device:TPU:0, one launch (start us, length us, event | category | flops | bytes accessed | tf_op | source)
XLA Modules:
  0.0 33.3 jit_solution(3586074301563848634)
XLA Ops:
  0.0 1.3 %collective-permute-start.3 = (bf16[2,16,2048]{2,1,0:T(8,128)(2,1)}, bf16[2,16,2048]{2,1,0:T(8,128)(2,1)S(1)}, u32[]{:S(2)}, u32[]{:S(2)}) collective-permute-start(bf16[2,16,2048]{2,1,0:T(8,128)(2,1)} %bitcast.4), channel_id=1, source_target_pairs={{8,0},{12,4},{16,8},{20,12},{24,16},{28,20},{9,1},{13,5},{17,9},{2... | collective-permute-start | bytes 393224 | tf_op jit(solution)/shard_map/ppermute | solution.py:360
  1.3 1.3 %collective-permute-start.2 = (bf16[2,16,2048]{2,1,0:T(8,128)(2,1)}, bf16[2,16,2048]{2,1,0:T(8,128)(2,1)S(1)}, u32[]{:S(2)}, u32[]{:S(2)}) collective-permute-start(bf16[2,16,2048]{2,1,0:T(8,128)(2,1)} %bitcast.5), channel_id=1, source_target_pairs={{4,0},{8,4},{12,8},{16,12},{20,16},{24,20},{28,24},{5,1},{9,5},{13... | collective-permute-start | bytes 393224 | tf_op jit(solution)/shard_map/ppermute | solution.py:360
  2.6 5.5 %collective-permute-start.1 = (bf16[2,16,2048]{2,1,0:T(8,128)(2,1)}, bf16[2,16,2048]{2,1,0:T(8,128)(2,1)S(1)}, u32[]{:S(2)}, u32[]{:S(2)}) collective-permute-start(bf16[2,16,2048]{2,1,0:T(8,128)(2,1)} %bitcast.6), channel_id=1, source_target_pairs={{0,4},{4,8},{8,12},{12,16},{16,20},{20,24},{24,28},{1,5},{5,9},{9,... | collective-permute-start | bytes 393224 | tf_op jit(solution)/shard_map/ppermute | solution.py:360
  8.1 4.6 %collective-permute-start = (bf16[2,16,2048]{2,1,0:T(8,128)(2,1)}, bf16[2,16,2048]{2,1,0:T(8,128)(2,1)S(1)}, u32[]{:S(2)}, u32[]{:S(2)}) collective-permute-start(bf16[2,16,2048]{2,1,0:T(8,128)(2,1)} %bitcast.7), channel_id=1, source_target_pairs={{0,8},{4,12},{8,16},{12,20},{16,24},{20,28},{1,9},{5,13},{9,17},{1... | collective-permute-start | bytes 393224 | tf_op jit(solution)/shard_map/ppermute | solution.py:360
  12.7 4.4 %tables.1 = (bf16[80,96,256]{2,1,0:T(8,128)(2,1)S(1)}, bf16[80,96,128]{2,1,0:T(8,128)(2,1)S(1)}, bf16[2,256,128]{2,1,0:T(8,128)(2,1)S(1)}) custom-call(bf16[2,16,2048]{2,1,0:T(8,128)(2,1)} %bitcast.8, bf16[5,3,16,1024]{3,2,1,0:T(8,128)(2,1)} %gradient_hbm.1, f32[270,1,16]{2,1,0:T(1,128)} %bitcast.3), custom_call_target="tpu_custom_call" | custom-call | flops 200000000 | bytes 6000000 | tf_op jit(solution)/shard_map/tables/pallas_call | solution.py:169
  17.2 0.0 collective-permute-done.3.above2
  17.2 0.0 collective-permute-done.2.above1
  17.2 0.0 collective-permute-done.1.below1
  17.2 0.0 collective-permute-done.below2
  17.2 6.8 %sandwich.1 = bf16[4,128,128]{2,1,0:T(8,128)(2,1)S(1)} custom-call(s32[5,16]{1,0:T(8,128)} %bitcast.9, s32[3]{0:T(128)} %offsets_hbm.1, bf16[2,256,128]{2,1,0:T(8,128)(2,1)S(1)} %get-tuple-element.8.middle_planes, bf16[2,16,2048]{2,1,0:T(8,128)(2,1)S(1)} %collective-permute-done.below2, bf16[2,16,2048]{2,1,0:T(8,128)(2,1)S(1)} %collective-permute-done.1.below1, ...), custom_call_target="tpu_custom_call" | custom-call | flops 800000000 | bytes 7000000 | tf_op jit(solution)/shard_map/sandwich/pallas_call | solution.py:308
  24.0 7.8 %all_to_all.5.parts = bf16[4,128,128]{2,1,0:T(8,128)(2,1)} all-to-all(bf16[4,128,128]{2,1,0:T(8,128)(2,1)S(1)} %sandwich.1), channel_id=1, replica_groups=mesh['energy'=8,'mom'=4] {'mom'}, dimensions={0} | all-to-all | bytes 262144 | tf_op jit(solution)/shard_map/all_to_all | solution.py:384
  31.7 1.6 %combine.1 = f32[2,4,2048]{2,1,0:T(4,128)} custom-call(bf16[4,128,128]{2,1,0:T(8,128)(2,1)} %all_to_all.5.parts), custom_call_target="tpu_custom_call" | custom-call | tf_op jit(solution)/shard_map/combine/pallas_call | solution.py:347
Async XLA Ops:
  0.0 17.2 %collective-permute-start.3 = (bf16[2,16,2048]{2,1,0:T(8,128)(2,1)}, bf16[2,16,2048]{2,1,0:T(8,128)(2,1)S(1)}, u32[]{:S(2)}, u32[]{:S(2)}) collective-permute-start(bf16[2,16,2048]{2,1,0:T(8,128)(2,1)} %bitcast.4), channel_id=1, source_target_pairs={{8,0},{12,4},{16,8},{20,12},{24,16},{28,20},{9,1},{13,5},{17,9},{2... | collective-permute-start | bytes 393224 | tf_op jit(solution)/shard_map/ppermute | solution.py:360
  1.3 15.9 %collective-permute-start.2 = (bf16[2,16,2048]{2,1,0:T(8,128)(2,1)}, bf16[2,16,2048]{2,1,0:T(8,128)(2,1)S(1)}, u32[]{:S(2)}, u32[]{:S(2)}) collective-permute-start(bf16[2,16,2048]{2,1,0:T(8,128)(2,1)} %bitcast.5), channel_id=1, source_target_pairs={{4,0},{8,4},{12,8},{16,12},{20,16},{24,20},{28,24},{5,1},{9,5},{13... | collective-permute-start | bytes 393224 | tf_op jit(solution)/shard_map/ppermute | solution.py:360
  2.6 14.6 %collective-permute-start.1 = (bf16[2,16,2048]{2,1,0:T(8,128)(2,1)}, bf16[2,16,2048]{2,1,0:T(8,128)(2,1)S(1)}, u32[]{:S(2)}, u32[]{:S(2)}) collective-permute-start(bf16[2,16,2048]{2,1,0:T(8,128)(2,1)} %bitcast.6), channel_id=1, source_target_pairs={{0,4},{4,8},{8,12},{12,16},{16,20},{20,24},{24,28},{1,5},{5,9},{9,... | collective-permute-start | bytes 393224 | tf_op jit(solution)/shard_map/ppermute | solution.py:360
  8.1 9.1 %collective-permute-start = (bf16[2,16,2048]{2,1,0:T(8,128)(2,1)}, bf16[2,16,2048]{2,1,0:T(8,128)(2,1)S(1)}, u32[]{:S(2)}, u32[]{:S(2)}) collective-permute-start(bf16[2,16,2048]{2,1,0:T(8,128)(2,1)} %bitcast.7), channel_id=1, source_target_pairs={{0,8},{4,12},{8,16},{12,20},{16,24},{20,28},{1,9},{5,13},{9,17},{1... | collective-permute-start | bytes 393224 | tf_op jit(solution)/shard_map/ppermute | solution.py:360

commit v8 on v7

--- a/solution.py
+++ b/solution.py
@@ -70,13 +70,13 @@
     )
 
 
-def exact_dot(left, right):
+def dot(left, right):
     return jnp.dot(left, right, preferred_element_type=jnp.float32)
 
 
 def make_planes(block, planes, at, order):
     count = block.shape[0]
-    ordered = exact_dot(
+    ordered = dot(
         order, jnp.concatenate([stack_tiles(block[e]) for e in range(count)], axis=1)
     ).astype(jnp.bfloat16)
     for e in range(count):
@@ -119,7 +119,7 @@
     )
     for atom in range(natoms):
         left = jnp.where(chosen, table[atom : atom + 1, :], 0.0).astype(jnp.bfloat16)
-        wide = exact_dot(left, widen)
+        wide = dot(left, widen)
         for slot in range(NB):
             for half in range(2):
                 rows[atom * NB + slot, half] = wide[
@@ -128,11 +128,11 @@
 
     copies[1].wait()
     flats = [stack_tiles(gradient[slot, j]) for slot in range(NB) for j in range(ND)]
-    ordered = exact_dot(order, jnp.concatenate(flats, axis=1)).astype(jnp.bfloat16)
+    ordered = dot(order, jnp.concatenate(flats, axis=1)).astype(jnp.bfloat16)
     for slot in range(NB):
         for j in range(ND):
             at = (slot * ND + j) * LANES
-            wide = exact_dot(ordered[:, at : at + LANES], fold)
+            wide = dot(ordered[:, at : at + LANES], fold)
             for atom in range(natoms):
                 derivs_out[atom * NB + slot, j * NO : (j + 1) * NO, :] = jnp.concatenate(
                     [
@@ -219,7 +219,7 @@
             shifted_planes = [
                 planes[2 * count + e - (1 - 2 * (s % 2)) * offsets[s // 2]] for s in branches
             ]
-            wide = exact_dot(
+            wide = dot(
                 jnp.concatenate(shifted_planes, axis=1),
                 jnp.concatenate(places[: len(branches)], axis=0),
             ).astype(jnp.bfloat16)
@@ -231,54 +231,68 @@
                     ]
 
     lane_group = group_of(iota((NO, LANES), 1))
-    masks = [ones_where(lane_group == g) for g in range(groups)]
-    group = over(iota((HI, LANES), 1), NO)
-
-    def middles(pair):
-        parts = [[] for _ in pair]
+    masks = [ones_where(lane_group == g) for g in range(COPIES)]
+    group = over(iota((NO, LANES), 1), NO)
+    row_group = over(iota((HI, LANES), 1), NO)
+    spans = -(-NB * ND // COPIES)
+
+    def middles(atom):
+        blocked = []
         for slot in range(NB):
             wide = lax.dot_general(
-                jnp.concatenate([kernel[atom * NB + slot] for atom in pair], axis=0),
-                jnp.concatenate([blocks[neighbours[slot, atom]] for atom in pair], axis=0),
-                NT,
+                blocks[neighbours[slot, atom]], kernel[atom * NB + slot], NT,
                 preferred_element_type=jnp.float32,
             )
-            for k in range(len(pair)):
-                own = wide[
-                    k * ND * NO : (k + 1) * ND * NO, k * groups * NO : (k + 1) * groups * NO
-                ].astype(jnp.bfloat16)
-                for i in range(ND):
-                    block = own[i * NO : (i + 1) * NO, :]
-                    parts[k].append(jnp.concatenate([block * mask for mask in masks], axis=0))
-        return jnp.concatenate([jnp.concatenate(part, axis=1) for part in parts], axis=0)
-
-    def sigmas(pair, right):
-        left = jnp.concatenate(
-            [
-                jnp.concatenate(
-                    [
-                        derivs[atom * NB + slot, i * NO : (i + 1) * NO, :]
-                        for slot in range(NB)
-                        for i in range(ND)
-                    ],
-                    axis=1,
-                )
-                for atom in pair
-            ],
-            axis=0,
-        )
-        wide = lax.dot_general(left, right, NT, preferred_element_type=jnp.float32)
+            wide = jnp.concatenate(
+                [wide, jnp.zeros((groups * NO, LANES - ND * NO), jnp.float32)], axis=1
+            )
+            rows = []
+            for g in range(groups):
+                starts = [((g // 2) * COPIES + q) * tiles + (g % 2) * HI for q in range(COPIES)]
+                rows.append(jnp.concatenate([wide[at : at + HI] for at in starts], axis=0))
+            turned = []
+            for d in range(COPIES):
+                total = rows[-d % COPIES]
+                for lane in range(1, COPIES):
+                    total = jnp.where(group == lane, rows[(lane - d) % COPIES], total)
+                turned.append(pltpu.roll(total, (COPIES - d) * NO, axis=1) if d else total)
+            for i in range(ND):
+                total = turned[i]
+                for g in range(1, groups):
+                    total = jnp.where(group == g, turned[(i - g) % COPIES], total)
+                blocked.append(total)
+        blocked.extend([jnp.zeros((NO, LANES), jnp.float32)] * (spans * COPIES - len(blocked)))
+        pieces = []
+        for span in range(spans):
+            for u in range(COPIES // 2):
+                for q in range(COPIES):
+                    for v in range(2):
+                        pieces.append(
+                            blocked[span * COPIES + 2 * u + v][q * HI : (q + 1) * HI]
+                        )
+        return jnp.concatenate(pieces, axis=0).astype(jnp.bfloat16)
+
+    def sigmas(atom, right):
+        left = []
+        for span in range(spans):
+            total = None
+            for g in range(COPIES):
+                k = span * COPIES + g
+                if k < NB * ND:
+                    at = (k % ND) * NO
+                    part = derivs[atom * NB + k // ND, at : at + NO, :] * masks[g]
+                    total = part if total is None else total + part
+            left.append(total)
+        own = dot(jnp.concatenate(left, axis=1), right)
+        rows = [own[q * HI : (q + 1) * HI, :] for q in range(COPIES)]
         placed = []
-        for k in range(len(pair)):
-            own = wide[k * NO : (k + 1) * NO, k * groups * NO : (k + 1) * groups * NO]
-            rows = [own[q * HI : (q + 1) * HI, :] for q in range(COPIES)]
-            for g in range(groups):
-                total = None
-                for q in range(COPIES):
-                    shift = (q - g) % COPIES * NO
-                    part = pltpu.roll(rows[q], shift, axis=1) if shift else rows[q]
-                    total = part if total is None else jnp.where(group == q, part, total)
-                placed.append(total)
+        for g in range(groups):
+            total = None
+            for q in range(COPIES):
+                shift = (q - g) % COPIES * NO
+                part = pltpu.roll(rows[q], shift, axis=1) if shift else rows[q]
+                total = part if total is None else jnp.where(row_group == q, part, total)
+            placed.append(total)
         return placed
 
     row, col = iota((LANES, LANES), 0), iota((LANES, LANES), 1)
@@ -288,11 +302,10 @@
 
     def one_share(step, carry):
         atoms = [step * share + k for k in range(share)]
-        pairs = [atoms[k : k + 2] for k in range(0, share, 2)]
         placed = []
-        for pair, right in zip(pairs, [middles(pair) for pair in pairs]):
-            placed.extend(sigmas(pair, right))
-        out[step] = exact_dot(
+        for atom, right in zip(atoms, [middles(atom) for atom in atoms]):
+            placed.extend(sigmas(atom, right))
+        out[step] = dot(
             jnp.concatenate(placed, axis=0).astype(jnp.bfloat16), unmix
         ).astype(jnp.bfloat16)
         return carry

time: 33.6 us -> 32.1 us (0.955)
  Pallas kernels: 12.8 us -> 11.3 us
    pallas_call x1, Pallas kernels: 6.78 us -> 5.29 us  [sandwich(): pl.pallas_call(functools.partial(sandwich_kernel, count, natoms), out_sha...]
  transfers between devices with their start and end apart: 4 -> 4, of which waited for: 0 -> 0; matrix products, arithmetic and copies ran while one was open for 0% -> 0% of each run, Pallas kernels for 13% -> 14%
where the time goes in v8:
time: 32.1 us; the launch traced here: 31.9 us
  starting transfers between devices  12.7 us (40%)
  Pallas kernels  11.3 us (35%)
  blocking collectives  7.76 us (24%)
    ppermute x4, starting transfers between devices, shifted(): return lax.ppermute(array, axis, pairs)  12.7 us
    all_to_all x1, blocking collectives, body(): parts = lax.all_to_all(partial_terms, 'mom', 0, 0, tiled=True)  7.76 us
    pallas_call x1, Pallas kernels, sandwich(): pl.pallas_call(functools.partial(sandwich_kernel, count, natoms), out_sha...  5.29 us
    pallas_call x1, Pallas kernels, tables(): pl.pallas_call(functools.partial(tables_kernel, natoms), out_shape=(jax.S...  4.44 us
    pallas_call x1, Pallas kernels, combine(): pl.pallas_call(combine_kernel, out_shape=jax.ShapeDtypeStruct((count, sha...  1.6 us
  transfers between devices with their start and end apart: 4, of which 0 were waited for; matrix products, arithmetic and copies ran while one was open for 0% of the time, Pallas kernels for 14%

profile of v8, /device:TPU:0, one launch (start us, length us, event | category | flops | bytes accessed | tf_op | source)
XLA Modules:
  0.0 31.9 jit_solution(2197638041898212200)
XLA Ops:
  0.0 1.3 %collective-permute-start.3 = (bf16[2,16,2048]{2,1,0:T(8,128)(2,1)}, bf16[2,16,2048]{2,1,0:T(8,128)(2,1)S(1)}, u32[]{:S(2)}, u32[]{:S(2)}) collective-permute-start(bf16[2,16,2048]{2,1,0:T(8,128)(2,1)} %bitcast.4), channel_id=1, source_target_pairs={{8,0},{12,4},{16,8},{20,12},{24,16},{28,20},{9,1},{13,5},{17,9},{2... | collective-permute-start | bytes 393224 | tf_op jit(solution)/shard_map/ppermute | solution.py:373
  1.3 1.3 %collective-permute-start.2 = (bf16[2,16,2048]{2,1,0:T(8,128)(2,1)}, bf16[2,16,2048]{2,1,0:T(8,128)(2,1)S(1)}, u32[]{:S(2)}, u32[]{:S(2)}) collective-permute-start(bf16[2,16,2048]{2,1,0:T(8,128)(2,1)} %bitcast.5), channel_id=1, source_target_pairs={{4,0},{8,4},{12,8},{16,12},{20,16},{24,20},{28,24},{5,1},{9,5},{13... | collective-permute-start | bytes 393224 | tf_op jit(solution)/shard_map/ppermute | solution.py:373
  2.6 5.5 %collective-permute-start.1 = (bf16[2,16,2048]{2,1,0:T(8,128)(2,1)}, bf16[2,16,2048]{2,1,0:T(8,128)(2,1)S(1)}, u32[]{:S(2)}, u32[]{:S(2)}) collective-permute-start(bf16[2,16,2048]{2,1,0:T(8,128)(2,1)} %bitcast.6), channel_id=1, source_target_pairs={{0,4},{4,8},{8,12},{12,16},{16,20},{20,24},{24,28},{1,5},{5,9},{9,... | collective-permute-start | bytes 393224 | tf_op jit(solution)/shard_map/ppermute | solution.py:373
  8.1 4.6 %collective-permute-start = (bf16[2,16,2048]{2,1,0:T(8,128)(2,1)}, bf16[2,16,2048]{2,1,0:T(8,128)(2,1)S(1)}, u32[]{:S(2)}, u32[]{:S(2)}) collective-permute-start(bf16[2,16,2048]{2,1,0:T(8,128)(2,1)} %bitcast.7), channel_id=1, source_target_pairs={{0,8},{4,12},{8,16},{12,20},{16,24},{20,28},{1,9},{5,13},{9,17},{1... | collective-permute-start | bytes 393224 | tf_op jit(solution)/shard_map/ppermute | solution.py:373
  12.7 4.4 %tables.1 = (bf16[80,96,256]{2,1,0:T(8,128)(2,1)S(1)}, bf16[80,96,128]{2,1,0:T(8,128)(2,1)S(1)}, bf16[2,256,128]{2,1,0:T(8,128)(2,1)S(1)}) custom-call(bf16[2,16,2048]{2,1,0:T(8,128)(2,1)} %bitcast.8, bf16[5,3,16,1024]{3,2,1,0:T(8,128)(2,1)} %gradient_hbm.1, f32[270,1,16]{2,1,0:T(1,128)} %bitcast.3), custom_call_target="tpu_custom_call" | custom-call | flops 200000000 | bytes 6000000 | tf_op jit(solution)/shard_map/tables/pallas_call | solution.py:169
  17.2 0.0 collective-permute-done.3.above2
  17.2 0.0 collective-permute-done.2.above1
  17.2 0.0 collective-permute-done.1.below1
  17.2 0.0 collective-permute-done.below2
  17.2 5.3 %sandwich.1 = bf16[4,128,128]{2,1,0:T(8,128)(2,1)S(1)} custom-call(s32[5,16]{1,0:T(8,128)} %bitcast.9, s32[3]{0:T(128)} %offsets_hbm.1, bf16[2,256,128]{2,1,0:T(8,128)(2,1)S(1)} %get-tuple-element.8.middle_planes, bf16[2,16,2048]{2,1,0:T(8,128)(2,1)S(1)} %collective-permute-done.below2, bf16[2,16,2048]{2,1,0:T(8,128)(2,1)S(1)} %collective-permute-done.1.below1, ...), custom_call_target="tpu_custom_call" | custom-call | flops 800000000 | bytes 7000000 | tf_op jit(solution)/shard_map/sandwich/pallas_call | solution.py:321
  22.5 7.8 %all_to_all.5.parts = bf16[4,128,128]{2,1,0:T(8,128)(2,1)} all-to-all(bf16[4,128,128]{2,1,0:T(8,128)(2,1)S(1)} %sandwich.1), channel_id=1, replica_groups=mesh['energy'=8,'mom'=4] {'mom'}, dimensions={0} | all-to-all | bytes 262144 | tf_op jit(solution)/shard_map/all_to_all | solution.py:397
  30.3 1.6 %combine.1 = f32[2,4,2048]{2,1,0:T(4,128)} custom-call(bf16[4,128,128]{2,1,0:T(8,128)(2,1)} %all_to_all.5.parts), custom_call_target="tpu_custom_call" | custom-call | tf_op jit(solution)/shard_map/combine/pallas_call | solution.py:360
Async XLA Ops:
  0.0 17.2 %collective-permute-start.3 = (bf16[2,16,2048]{2,1,0:T(8,128)(2,1)}, bf16[2,16,2048]{2,1,0:T(8,128)(2,1)S(1)}, u32[]{:S(2)}, u32[]{:S(2)}) collective-permute-start(bf16[2,16,2048]{2,1,0:T(8,128)(2,1)} %bitcast.4), channel_id=1, source_target_pairs={{8,0},{12,4},{16,8},{20,12},{24,16},{28,20},{9,1},{13,5},{17,9},{2... | collective-permute-start | bytes 393224 | tf_op jit(solution)/shard_map/ppermute | solution.py:373
  1.3 15.9 %collective-permute-start.2 = (bf16[2,16,2048]{2,1,0:T(8,128)(2,1)}, bf16[2,16,2048]{2,1,0:T(8,128)(2,1)S(1)}, u32[]{:S(2)}, u32[]{:S(2)}) collective-permute-start(bf16[2,16,2048]{2,1,0:T(8,128)(2,1)} %bitcast.5), channel_id=1, source_target_pairs={{4,0},{8,4},{12,8},{16,12},{20,16},{24,20},{28,24},{5,1},{9,5},{13... | collective-permute-start | bytes 393224 | tf_op jit(solution)/shard_map/ppermute | solution.py:373
  2.6 14.6 %collective-permute-start.1 = (bf16[2,16,2048]{2,1,0:T(8,128)(2,1)}, bf16[2,16,2048]{2,1,0:T(8,128)(2,1)S(1)}, u32[]{:S(2)}, u32[]{:S(2)}) collective-permute-start(bf16[2,16,2048]{2,1,0:T(8,128)(2,1)} %bitcast.6), channel_id=1, source_target_pairs={{0,4},{4,8},{8,12},{12,16},{16,20},{20,24},{24,28},{1,5},{5,9},{9,... | collective-permute-start | bytes 393224 | tf_op jit(solution)/shard_map/ppermute | solution.py:373
  8.1 9.1 %collective-permute-start = (bf16[2,16,2048]{2,1,0:T(8,128)(2,1)}, bf16[2,16,2048]{2,1,0:T(8,128)(2,1)S(1)}, u32[]{:S(2)}, u32[]{:S(2)}) collective-permute-start(bf16[2,16,2048]{2,1,0:T(8,128)(2,1)} %bitcast.7), channel_id=1, source_target_pairs={{0,8},{4,12},{8,16},{12,20},{16,24},{20,28},{1,9},{5,13},{9,17},{1... | collective-permute-start | bytes 393224 | tf_op jit(solution)/shard_map/ppermute | solution.py:373

commit v9 on v8

--- a/solution.py
+++ b/solution.py
@@ -117,26 +117,29 @@
     table = jnp.concatenate(
         [table, jnp.zeros((natoms, width - NS * cells), jnp.float32)], axis=1
     )
-    for atom in range(natoms):
-        left = jnp.where(chosen, table[atom : atom + 1, :], 0.0).astype(jnp.bfloat16)
-        wide = dot(left, widen)
-        for slot in range(NB):
-            for half in range(2):
-                rows[atom * NB + slot, half] = wide[
-                    slot * depth : (slot + 1) * depth, half * LANES : (half + 1) * LANES
-                ]
+    lefts = [
+        jnp.where(chosen, table[atom : atom + 1, :], 0.0).astype(jnp.bfloat16)
+        for atom in range(natoms)
+    ]
+    wide = dot(jnp.concatenate(lefts, axis=0), widen)
+    for at in range(natoms * NB):
+        for half in range(2):
+            rows[at, half] = wide[
+                at * depth : (at + 1) * depth, half * LANES : (half + 1) * LANES
+            ]
 
     copies[1].wait()
     flats = [stack_tiles(gradient[slot, j]) for slot in range(NB) for j in range(ND)]
     ordered = dot(order, jnp.concatenate(flats, axis=1)).astype(jnp.bfloat16)
+    stacked = [ordered[:, at : at + LANES] for at in range(0, NB * ND * LANES, LANES)]
+    wide = dot(jnp.concatenate(stacked, axis=0), fold)
     for slot in range(NB):
         for j in range(ND):
-            at = (slot * ND + j) * LANES
-            wide = dot(ordered[:, at : at + LANES], fold)
             for atom in range(natoms):
+                at = (slot * ND + j) * block + atom * tiles
                 derivs_out[atom * NB + slot, j * NO : (j + 1) * NO, :] = jnp.concatenate(
                     [
-                        wide[atom * tiles : (atom + 1) * tiles, q * LANES : (q + 1) * LANES]
+                        wide[at : at + tiles, q * LANES : (q + 1) * LANES]
                         for q in range(COPIES)
                     ],
                     axis=0,
@@ -213,21 +216,29 @@
     places = [fold * ones_where(group == g) for g in range(COPIES)]
     for copy in copies:
         copy.wait()
-    for e in range(count):
-        for half in range(2):
-            branches = range(half * COPIES, min(NS, (half + 1) * COPIES))
-            shifted_planes = [
-                planes[2 * count + e - (1 - 2 * (s % 2)) * offsets[s // 2]] for s in branches
-            ]
-            wide = dot(
-                jnp.concatenate(shifted_planes, axis=1),
-                jnp.concatenate(places[: len(branches)], axis=0),
-            ).astype(jnp.bfloat16)
+    for half in range(2):
+        branches = range(half * COPIES, min(NS, (half + 1) * COPIES))
+        shifted_planes = [
+            jnp.concatenate(
+                [
+                    planes[2 * count + e - (1 - 2 * (s % 2)) * offsets[s // 2]]
+                    for e in range(count)
+                ],
+                axis=0,
+            )
+            for s in branches
+        ]
+        wide = dot(
+            jnp.concatenate(shifted_planes, axis=1),
+            jnp.concatenate(places[: len(branches)], axis=0),
+        ).astype(jnp.bfloat16)
+        for e in range(count):
             for atom in range(natoms):
                 for q in range(COPIES):
                     at = (e * COPIES + q) * tiles
+                    start = (e * natoms + atom) * tiles
                     blocks[atom, at : at + tiles, half * LANES : (half + 1) * LANES] = wide[
-                        atom * tiles : (atom + 1) * tiles, q * LANES : (q + 1) * LANES
+                        start : start + tiles, q * LANES : (q + 1) * LANES
                     ]
 
     lane_group = group_of(iota((NO, LANES), 1))

time: 32.1 us -> 32.2 us (level)
  no operation moved by 1% of the time
where the time goes in v9:
time: 32.2 us; the launch traced here: 31.9 us
  starting transfers between devices  12.7 us (39%)
  Pallas kernels  11.4 us (35%)
  blocking collectives  7.77 us (24%)
    ppermute x4, starting transfers between devices, shifted(): return lax.ppermute(array, axis, pairs)  12.7 us
    all_to_all x1, blocking collectives, body(): parts = lax.all_to_all(partial_terms, 'mom', 0, 0, tiled=True)  7.77 us
    pallas_call x1, Pallas kernels, sandwich(): pl.pallas_call(functools.partial(sandwich_kernel, count, natoms), out_sha...  5.27 us
    pallas_call x1, Pallas kernels, tables(): pl.pallas_call(functools.partial(tables_kernel, natoms), out_shape=(jax.S...  4.49 us
    pallas_call x1, Pallas kernels, combine(): pl.pallas_call(combine_kernel, out_shape=jax.ShapeDtypeStruct((count, sha...  1.6 us
  transfers between devices with their start and end apart: 4, of which 0 were waited for; matrix products, arithmetic and copies ran while one was open for 0% of the time, Pallas kernels for 14%

profile of v9, /device:TPU:0, one launch (start us, length us, event | category | flops | bytes accessed | tf_op | source)
XLA Modules:
  0.0 31.9 jit_solution(14496762588220817284)
XLA Ops:
  0.0 1.3 %collective-permute-start.3 = (bf16[2,16,2048]{2,1,0:T(8,128)(2,1)}, bf16[2,16,2048]{2,1,0:T(8,128)(2,1)S(1)}, u32[]{:S(2)}, u32[]{:S(2)}) collective-permute-start(bf16[2,16,2048]{2,1,0:T(8,128)(2,1)} %bitcast.4), channel_id=1, source_target_pairs={{8,0},{12,4},{16,8},{20,12},{24,16},{28,20},{9,1},{13,5},{17,9},{2... | collective-permute-start | bytes 393224 | tf_op jit(solution)/shard_map/ppermute | solution.py:384
  1.3 1.3 %collective-permute-start.2 = (bf16[2,16,2048]{2,1,0:T(8,128)(2,1)}, bf16[2,16,2048]{2,1,0:T(8,128)(2,1)S(1)}, u32[]{:S(2)}, u32[]{:S(2)}) collective-permute-start(bf16[2,16,2048]{2,1,0:T(8,128)(2,1)} %bitcast.5), channel_id=1, source_target_pairs={{4,0},{8,4},{12,8},{16,12},{20,16},{24,20},{28,24},{5,1},{9,5},{13... | collective-permute-start | bytes 393224 | tf_op jit(solution)/shard_map/ppermute | solution.py:384
  2.6 5.5 %collective-permute-start.1 = (bf16[2,16,2048]{2,1,0:T(8,128)(2,1)}, bf16[2,16,2048]{2,1,0:T(8,128)(2,1)S(1)}, u32[]{:S(2)}, u32[]{:S(2)}) collective-permute-start(bf16[2,16,2048]{2,1,0:T(8,128)(2,1)} %bitcast.6), channel_id=1, source_target_pairs={{0,4},{4,8},{8,12},{12,16},{16,20},{20,24},{24,28},{1,5},{5,9},{9,... | collective-permute-start | bytes 393224 | tf_op jit(solution)/shard_map/ppermute | solution.py:384
  8.1 4.6 %collective-permute-start = (bf16[2,16,2048]{2,1,0:T(8,128)(2,1)}, bf16[2,16,2048]{2,1,0:T(8,128)(2,1)S(1)}, u32[]{:S(2)}, u32[]{:S(2)}) collective-permute-start(bf16[2,16,2048]{2,1,0:T(8,128)(2,1)} %bitcast.7), channel_id=1, source_target_pairs={{0,8},{4,12},{8,16},{12,20},{16,24},{20,28},{1,9},{5,13},{9,17},{1... | collective-permute-start | bytes 393224 | tf_op jit(solution)/shard_map/ppermute | solution.py:384
  12.7 4.5 %tables.1 = (bf16[80,96,256]{2,1,0:T(8,128)(2,1)S(1)}, bf16[80,96,128]{2,1,0:T(8,128)(2,1)S(1)}, bf16[2,256,128]{2,1,0:T(8,128)(2,1)S(1)}) custom-call(bf16[2,16,2048]{2,1,0:T(8,128)(2,1)} %bitcast.8, bf16[5,3,16,1024]{3,2,1,0:T(8,128)(2,1)} %gradient_hbm.1, f32[270,1,16]{2,1,0:T(1,128)} %bitcast.3), custom_call_target="tpu_custom_call" | custom-call | flops 200000000 | bytes 6000000 | tf_op jit(solution)/shard_map/tables/pallas_call | solution.py:172
  17.2 0.0 collective-permute-done.3.above2
  17.2 0.0 collective-permute-done.2.above1
  17.2 0.0 collective-permute-done.1.below1
  17.2 0.0 collective-permute-done.below2
  17.3 5.3 %sandwich.1 = bf16[4,128,128]{2,1,0:T(8,128)(2,1)S(1)} custom-call(s32[5,16]{1,0:T(8,128)} %bitcast.9, s32[3]{0:T(128)} %offsets_hbm.1, bf16[2,256,128]{2,1,0:T(8,128)(2,1)S(1)} %get-tuple-element.8.middle_planes, bf16[2,16,2048]{2,1,0:T(8,128)(2,1)S(1)} %collective-permute-done.below2, bf16[2,16,2048]{2,1,0:T(8,128)(2,1)S(1)} %collective-permute-done.1.below1, ...), custom_call_target="tpu_custom_call" | custom-call | flops 800000000 | bytes 7000000 | tf_op jit(solution)/shard_map/sandwich/pallas_call | solution.py:332
  22.5 7.8 %all_to_all.5.parts = bf16[4,128,128]{2,1,0:T(8,128)(2,1)} all-to-all(bf16[4,128,128]{2,1,0:T(8,128)(2,1)S(1)} %sandwich.1), channel_id=1, replica_groups=mesh['energy'=8,'mom'=4] {'mom'}, dimensions={0} | all-to-all | bytes 262144 | tf_op jit(solution)/shard_map/all_to_all | solution.py:408
  30.3 1.6 %combine.1 = f32[2,4,2048]{2,1,0:T(4,128)} custom-call(bf16[4,128,128]{2,1,0:T(8,128)(2,1)} %all_to_all.5.parts), custom_call_target="tpu_custom_call" | custom-call | tf_op jit(solution)/shard_map/combine/pallas_call | solution.py:371
Async XLA Ops:
  0.0 17.2 %collective-permute-start.3 = (bf16[2,16,2048]{2,1,0:T(8,128)(2,1)}, bf16[2,16,2048]{2,1,0:T(8,128)(2,1)S(1)}, u32[]{:S(2)}, u32[]{:S(2)}) collective-permute-start(bf16[2,16,2048]{2,1,0:T(8,128)(2,1)} %bitcast.4), channel_id=1, source_target_pairs={{8,0},{12,4},{16,8},{20,12},{24,16},{28,20},{9,1},{13,5},{17,9},{2... | collective-permute-start | bytes 393224 | tf_op jit(solution)/shard_map/ppermute | solution.py:384
  1.3 15.9 %collective-permute-start.2 = (bf16[2,16,2048]{2,1,0:T(8,128)(2,1)}, bf16[2,16,2048]{2,1,0:T(8,128)(2,1)S(1)}, u32[]{:S(2)}, u32[]{:S(2)}) collective-permute-start(bf16[2,16,2048]{2,1,0:T(8,128)(2,1)} %bitcast.5), channel_id=1, source_target_pairs={{4,0},{8,4},{12,8},{16,12},{20,16},{24,20},{28,24},{5,1},{9,5},{13... | collective-permute-start | bytes 393224 | tf_op jit(solution)/shard_map/ppermute | solution.py:384
  2.6 14.6 %collective-permute-start.1 = (bf16[2,16,2048]{2,1,0:T(8,128)(2,1)}, bf16[2,16,2048]{2,1,0:T(8,128)(2,1)S(1)}, u32[]{:S(2)}, u32[]{:S(2)}) collective-permute-start(bf16[2,16,2048]{2,1,0:T(8,128)(2,1)} %bitcast.6), channel_id=1, source_target_pairs={{0,4},{4,8},{8,12},{12,16},{16,20},{20,24},{24,28},{1,5},{5,9},{9,... | collective-permute-start | bytes 393224 | tf_op jit(solution)/shard_map/ppermute | solution.py:384
  8.1 9.2 %collective-permute-start = (bf16[2,16,2048]{2,1,0:T(8,128)(2,1)}, bf16[2,16,2048]{2,1,0:T(8,128)(2,1)S(1)}, u32[]{:S(2)}, u32[]{:S(2)}) collective-permute-start(bf16[2,16,2048]{2,1,0:T(8,128)(2,1)} %bitcast.7), channel_id=1, source_target_pairs={{0,8},{4,12},{8,16},{12,20},{16,24},{20,28},{1,9},{5,13},{9,17},{1... | collective-permute-start | bytes 393224 | tf_op jit(solution)/shard_map/ppermute | solution.py:384

commit v10 on v8

--- a/solution.py
+++ b/solution.py
@@ -117,26 +117,29 @@
     table = jnp.concatenate(
         [table, jnp.zeros((natoms, width - NS * cells), jnp.float32)], axis=1
     )
-    for atom in range(natoms):
-        left = jnp.where(chosen, table[atom : atom + 1, :], 0.0).astype(jnp.bfloat16)
-        wide = dot(left, widen)
-        for slot in range(NB):
-            for half in range(2):
-                rows[atom * NB + slot, half] = wide[
-                    slot * depth : (slot + 1) * depth, half * LANES : (half + 1) * LANES
-                ]
+    lefts = [
+        jnp.where(chosen, table[atom : atom + 1, :], 0.0).astype(jnp.bfloat16)
+        for atom in range(natoms)
+    ]
+    wide = dot(jnp.concatenate(lefts, axis=0), widen)
+    for at in range(natoms * NB):
+        for half in range(2):
+            rows[at, half] = wide[
+                at * depth : (at + 1) * depth, half * LANES : (half + 1) * LANES
+            ]
 
     copies[1].wait()
     flats = [stack_tiles(gradient[slot, j]) for slot in range(NB) for j in range(ND)]
     ordered = dot(order, jnp.concatenate(flats, axis=1)).astype(jnp.bfloat16)
+    stacked = [ordered[:, at : at + LANES] for at in range(0, NB * ND * LANES, LANES)]
+    wide = dot(jnp.concatenate(stacked, axis=0), fold)
     for slot in range(NB):
         for j in range(ND):
-            at = (slot * ND + j) * LANES
-            wide = dot(ordered[:, at : at + LANES], fold)
             for atom in range(natoms):
+                at = (slot * ND + j) * block + atom * tiles
                 derivs_out[atom * NB + slot, j * NO : (j + 1) * NO, :] = jnp.concatenate(
                     [
-                        wide[atom * tiles : (atom + 1) * tiles, q * LANES : (q + 1) * LANES]
+                        wide[at : at + tiles, q * LANES : (q + 1) * LANES]
                         for q in range(COPIES)
                     ],
                     axis=0,
@@ -146,18 +149,16 @@
     make_planes(local, planes_out, 0, row_matrix(2 * tiles, natoms))
 
     def one_cell(at, carry):
-        derivs = [
-            derivs_out[at, j * NO : (j + 1) * NO, :].astype(jnp.float32) for j in range(ND)
-        ]
+        derivs = [derivs_out[at, j * NO : (j + 1) * NO, :] for j in range(ND)]
         for i in range(ND):
             for half in range(2):
                 total = None
                 for j in range(ND):
-                    term = derivs[j] * rows[at, half, ND * i + j : ND * i + j + 1, :]
+                    row = rows[at, half, ND * i + j : ND * i + j + 1, :]
+                    weight = jnp.broadcast_to(row, (NO, LANES)).astype(jnp.bfloat16)
+                    term = derivs[j] * weight
                     total = term if total is None else total + term
-                kernel_out[at, i * NO : (i + 1) * NO, half * LANES : (half + 1) * LANES] = (
-                    total.astype(jnp.bfloat16)
-                )
+                kernel_out[at, i * NO : (i + 1) * NO, half * LANES : (half + 1) * LANES] = total
         return carry
 
     lax.fori_loop(0, natoms * NB, one_cell, 0, unroll=4)
@@ -190,57 +191,23 @@
     )(in_hbm(local), in_hbm(gradient), in_hbm(coupling))
 
 
-def sandwich_kernel(
-    count, natoms, neighbours_hbm, offsets_hbm, middle_planes, below2, below1, above1, above2,
-    kernel, derivs, out, neighbours, offsets, planes, blocks, sems,
-):
-    copies = [
-        pltpu.make_async_copy(neighbours_hbm, neighbours, sems.at[0]),
-        pltpu.make_async_copy(offsets_hbm, offsets, sems.at[1]),
-    ]
-    for copy in copies:
-        copy.start()
-
-    tiles = 2 * NO * NO // LANES
-    groups = 2 * count
-    order = row_matrix(tiles, natoms)
-    for piece, ref in ((0, below2), (1, below1), (3, above1), (4, above2)):
-        make_planes(ref, planes, piece * count, order)
-    planes[2 * count : 3 * count] = middle_planes[...]
-
-    fold = fold_matrix()
-    group = group_of(rest(iota(fold.shape, 1), LANES))
-    places = [fold * ones_where(group == g) for g in range(COPIES)]
-    for copy in copies:
-        copy.wait()
-    for e in range(count):
-        for half in range(2):
-            branches = range(half * COPIES, min(NS, (half + 1) * COPIES))
-            shifted_planes = [
-                planes[2 * count + e - (1 - 2 * (s % 2)) * offsets[s // 2]] for s in branches
-            ]
-            wide = dot(
-                jnp.concatenate(shifted_planes, axis=1),
-                jnp.concatenate(places[: len(branches)], axis=0),
-            ).astype(jnp.bfloat16)
-            for atom in range(natoms):
-                for q in range(COPIES):
-                    at = (e * COPIES + q) * tiles
-                    blocks[atom, at : at + tiles, half * LANES : (half + 1) * LANES] = wide[
-                        atom * tiles : (atom + 1) * tiles, q * LANES : (q + 1) * LANES
-                    ]
-
+def partner(index, step, size):
+    return index ^ step if size & (size - 1) == 0 else (index + step) % size
+
+
+def share_terms(atoms, groups, block_of, kernel, derivs):
+    tiles = groups * HI // 2
     lane_group = group_of(iota((NO, LANES), 1))
     masks = [ones_where(lane_group == g) for g in range(COPIES)]
     group = over(iota((NO, LANES), 1), NO)
     row_group = over(iota((HI, LANES), 1), NO)
     spans = -(-NB * ND // COPIES)
 
-    def middles(atom):
+    def middles(k):
         blocked = []
         for slot in range(NB):
             wide = lax.dot_general(
-                blocks[neighbours[slot, atom]], kernel[atom * NB + slot], NT,
+                block_of(k, slot), kernel[atoms[k] * NB + slot], NT,
                 preferred_element_type=jnp.float32,
             )
             wide = jnp.concatenate(
@@ -272,15 +239,15 @@
                         )
         return jnp.concatenate(pieces, axis=0).astype(jnp.bfloat16)
 
-    def sigmas(atom, right):
+    def sigmas(k, right):
         left = []
         for span in range(spans):
             total = None
             for g in range(COPIES):
-                k = span * COPIES + g
-                if k < NB * ND:
-                    at = (k % ND) * NO
-                    part = derivs[atom * NB + k // ND, at : at + NO, :] * masks[g]
+                pair = span * COPIES + g
+                if pair < NB * ND:
+                    at = (pair % ND) * NO
+                    part = derivs[atoms[k] * NB + pair // ND, at : at + NO, :] * masks[g]
                     total = part if total is None else total + part
             left.append(total)
         own = dot(jnp.concatenate(left, axis=1), right)
@@ -295,40 +262,103 @@
             placed.append(total)
         return placed
 
+    rights = [middles(k) for k in range(len(atoms))]
+    placed = []
+    for k, right in enumerate(rights):
+        placed.extend(sigmas(k, right))
     row, col = iota((LANES, LANES), 0), iota((LANES, LANES), 1)
     unmix = ones_where(col == (row - rest(row, NO)) + mixed(rest(row, NO)))
-    shares = out.shape[0]
+    return dot(jnp.concatenate(placed, axis=0).astype(jnp.bfloat16), unmix)
+
+
+def sandwich_kernel(
+    count, natoms, shares, neighbours_hbm, offsets_hbm, middle_planes,
+    below2, below1, above1, above2, kernel, derivs, *refs,
+):
+    outs, own_blocks = refs[: shares - 1], refs[shares - 1]
+    neighbours, offsets, planes, blocks, results, sems = refs[shares:]
+    copies = [
+        pltpu.make_async_copy(neighbours_hbm, neighbours, sems.at[0]),
+        pltpu.make_async_copy(offsets_hbm, offsets, sems.at[1]),
+    ]
+    for copy in copies:
+        copy.start()
+
+    tiles = 2 * NO * NO // LANES
+    groups = 2 * count
+    order = row_matrix(tiles, natoms)
+    for piece, ref in ((0, below2), (1, below1), (3, above1), (4, above2)):
+        make_planes(ref, planes, piece * count, order)
+    planes[2 * count : 3 * count] = middle_planes[...]
+
+    fold = fold_matrix()
+    group = group_of(rest(iota(fold.shape, 1), LANES))
+    places = [fold * ones_where(group == g) for g in range(COPIES)]
+    for copy in copies:
+        copy.wait()
+    for half in range(2):
+        branches = range(half * COPIES, min(NS, (half + 1) * COPIES))
+        shifted_planes = [
+            jnp.concatenate(
+                [
+                    planes[2 * count + e - (1 - 2 * (s % 2)) * offsets[s // 2]]
+                    for e in range(count)
+                ],
+                axis=0,
+            )
+            for s in branches
+        ]
+        wide = dot(
+            jnp.concatenate(shifted_planes, axis=1),
+            jnp.concatenate(places[: len(branches)], axis=0),
+        ).astype(jnp.bfloat16)
+        for e in range(count):
+            for atom in range(natoms):
+                for q in range(COPIES):
+                    at = (e * COPIES + q) * tiles
+                    start = (e * natoms + atom) * tiles
+                    blocks[atom, at : at + tiles, half * LANES : (half + 1) * LANES] = wide[
+                        start : start + tiles, q * LANES : (q + 1) * LANES
+                    ]
+
+    me = lax.axis_index("mom")
     share = natoms // shares
+    for k in range(share):
+        for slot in range(NB):
+            own_blocks[k * NB + slot] = blocks[neighbours[slot, me * share + k]]
 
     def one_share(step, carry):
-        atoms = [step * share + k for k in range(share)]
-        placed = []
-        for atom, right in zip(atoms, [middles(atom) for atom in atoms]):
-            placed.extend(sigmas(atom, right))
-        out[step] = dot(
-            jnp.concatenate(placed, axis=0).astype(jnp.bfloat16), unmix
+        first = partner(me, step, shares) * share
+        atoms = [first + k for k in range(share)]
+        results[step] = share_terms(
+            atoms, groups, lambda k, slot: blocks[neighbours[slot, atoms[k]]], kernel, derivs
         ).astype(jnp.bfloat16)
         return carry
 
-    lax.fori_loop(0, shares, one_share, 0)
+    lax.fori_loop(1, shares, one_share, 0)
+    for step in range(1, shares):
+        outs[step - 1][...] = results[step]
 
 
 def sandwich(window, middle_planes, kernel, derivs, neighbours, offsets, shares):
     below2, below1, above1, above2 = window
     count, natoms, size = below2.shape
     groups = 2 * count
-    rows = natoms * groups * HI
+    share = natoms // shares
+    rows = share * groups * HI
     return pl.pallas_call(
-        functools.partial(sandwich_kernel, count, natoms),
-        out_shape=jax.ShapeDtypeStruct((shares, rows // shares, LANES), jnp.bfloat16),
+        functools.partial(sandwich_kernel, count, natoms, shares),
+        out_shape=(jax.ShapeDtypeStruct((rows, LANES), jnp.bfloat16),) * (shares - 1)
+        + (jax.ShapeDtypeStruct((share * NB, groups * NO, 2 * LANES), jnp.bfloat16),),
         in_specs=[pl.BlockSpec(memory_space=pltpu.HBM)] * 2
         + [pl.BlockSpec(memory_space=pltpu.VMEM)] * 7,
-        out_specs=pl.BlockSpec(memory_space=pltpu.VMEM),
+        out_specs=[pl.BlockSpec(memory_space=pltpu.VMEM)] * shares,
         scratch_shapes=[
             pltpu.SMEM(neighbours.shape, jnp.int32),
             pltpu.SMEM(offsets.shape, jnp.int32),
             pltpu.VMEM((5 * count, natoms * size // LANES, LANES), jnp.bfloat16),
             pltpu.VMEM((natoms, groups * NO, 2 * LANES), jnp.bfloat16),
+            pltpu.VMEM((shares, rows, LANES), jnp.bfloat16),
             pltpu.SemaphoreType.DMA((2,)),
         ],
         compiler_params=pltpu.CompilerParams(vmem_limit_bytes=VMEM_LIMIT),
@@ -342,12 +372,38 @@
     )
 
 
-def combine_kernel(parts, out, total):
+def own_kernel(groups, blocks, kernel, derivs, out):
+    share = blocks.shape[0] // NB
+    first = lax.axis_index("mom") * share
+    out[...] = share_terms(
+        [first + k for k in range(share)], groups,
+        lambda k, slot: blocks[k * NB + slot], kernel, derivs,
+    )
+
+
+def own_share(blocks, kernel, derivs):
+    share = blocks.shape[0] // NB
+    groups = blocks.shape[1] // NO
+    return pl.pallas_call(
+        functools.partial(own_kernel, groups),
+        out_shape=jax.ShapeDtypeStruct((share * groups * HI, LANES), jnp.float32),
+        in_specs=[pl.BlockSpec(memory_space=pltpu.VMEM)] * 3,
+        out_specs=pl.BlockSpec(memory_space=pltpu.VMEM),
+        compiler_params=pltpu.CompilerParams(vmem_limit_bytes=VMEM_LIMIT),
+        cost_estimate=pl.CostEstimate(
+            flops=200_000_000, bytes_accessed=2_000_000, transcendentals=0
+        ),
+        name="own_share",
+    )(blocks, kernel, derivs)
+
+
+def combine_kernel(own, *refs):
+    parts, out, total = refs[:-2], refs[-2], refs[-1]
     count, share, width = out.shape
     tiles = width // LANES
-    summed = parts[0].astype(jnp.float32)
-    for k in range(1, parts.shape[0]):
-        summed = summed + parts[k].astype(jnp.float32)
+    summed = own[...]
+    for part in parts:
+        summed = summed + part[...].astype(jnp.float32)
     total[...] = summed
     for e in range(count):
         for t in range(tiles):
@@ -356,15 +412,16 @@
             ]
 
 
-def combine(parts, count, share):
+def combine(own, parts, count, share):
     return pl.pallas_call(
         combine_kernel,
         out_shape=jax.ShapeDtypeStruct((count, share, 2 * NO * NO), jnp.float32),
-        in_specs=[pl.BlockSpec(memory_space=pltpu.VMEM)],
+        in_specs=[pl.BlockSpec(memory_space=pltpu.VMEM)] * (1 + len(parts)),
         out_specs=pl.BlockSpec(memory_space=pltpu.VMEM),
-        scratch_shapes=[pltpu.VMEM(parts.shape[1:], jnp.float32)],
+        scratch_shapes=[pltpu.VMEM(own.shape, jnp.float32)],
+        compiler_params=pltpu.CompilerParams(vmem_limit_bytes=VMEM_LIMIT),
         name="combine",
-    )(parts)
+    )(own, *parts)
 
 
 def shifted(array, axis, by):
@@ -373,29 +430,24 @@
     return lax.ppermute(array, axis, pairs)
 
 
-def local_partial(window, coupling, gradient, neighbours, offsets, shares):
-    below2, below1, local, above1, above2 = window
-    kernel, derivs, planes = tables(
-        local, gradient, coupling.reshape(-1, 1, coupling.shape[-1])
+def body(green, coupling, gradient, neighbours, offsets):
+    local = green[0]
+    count, natoms, _ = local.shape
+    shares = lax.axis_size("mom")
+    remote = (
+        shifted(local, "energy", 2),
+        shifted(local, "energy", 1),
+        shifted(local, "energy", -1),
+        shifted(local, "energy", -2),
     )
-    remote = (below2, below1, above1, above2)
-    return sandwich(remote, planes, kernel, derivs, neighbours.T, offsets, shares)
-
-
-def body(green, coupling, gradient, neighbours, offsets):
-    local_block = green[0]
-    count, natoms, _ = local_block.shape
-    shares = lax.axis_size("mom")
-    window = (
-        shifted(local_block, "energy", 2),
-        shifted(local_block, "energy", 1),
-        local_block,
-        shifted(local_block, "energy", -1),
-        shifted(local_block, "energy", -2),
-    )
-    partial_terms = local_partial(window, coupling[0], gradient, neighbours, offsets, shares)
-    parts = lax.all_to_all(partial_terms, "mom", 0, 0, tiled=True)
-    return combine(parts, count, natoms // shares)
+    kernel, derivs, planes = tables(local, gradient, coupling.reshape(-1, 1, coupling.shape[-1]))
+    *terms, own_blocks = sandwich(remote, planes, kernel, derivs, neighbours.T, offsets, shares)
+    parts = [
+        lax.ppermute(term, "mom", [(i, partner(i, step, shares)) for i in range(shares)])
+        for step, term in enumerate(terms, 1)
+    ]
+    own = own_share(own_blocks, kernel, derivs)
+    return combine(own, parts, count, natoms // shares)
 
 
 def solution(mesh):

time: 32.1 us -> 27.9 us (0.87)
  blocking collectives: 7.76 us -> 0 us
  waiting for transfers between devices: 0.01 us -> 2.32 us
  starting transfers between devices: 12.7 us -> 14.8 us
  Pallas kernels: 11.3 us -> 10.4 us
    all_to_all x1 -> x0, blocking collectives: 7.76 us -> none  [body(): parts = lax.all_to_all(partial_terms, 'mom', 0, 0, tiled=True)]
    ppermute x0 -> x3, waiting for transfers between devices: none -> 2.31 us  [body(): lax.ppermute(term, 'mom', [(i, partner(i, step, shares)) for i in range(s...]
    ppermute x0 -> x3, starting transfers between devices: none -> 2.16 us  [body(): lax.ppermute(term, 'mom', [(i, partner(i, step, shares)) for i in range(s...]
    pallas_call x1, Pallas kernels: 1.6 us -> 0.69 us  [combine(): pl.pallas_call(combine_kernel, out_shape=jax.ShapeDtypeStruct((count, sha...]
    pallas_call x1 -> x2, Pallas kernels: 5.29 us -> 5.38 us  [the longest x1 4.42 us: sandwich(): pl.pallas_call(functools.partial(sandwich_kernel, count, natoms, shares),...]
  transfers between devices with their start and end apart: 4 -> 7, of which waited for: 0 -> 2; matrix products, arithmetic and copies ran while one was open for 0% -> 0% of each run, Pallas kernels for 14% -> 19%
where the time goes in v10:
time: 27.9 us; the launch traced here: 27.7 us
  starting transfers between devices  14.8 us (53%)
  Pallas kernels  10.4 us (37%)
  waiting for transfers between devices  2.32 us (8%)
    ppermute x4, starting transfers between devices, shifted(): return lax.ppermute(array, axis, pairs)  12.7 us
    pallas_call x1, Pallas kernels, sandwich(): pl.pallas_call(functools.partial(sandwich_kernel, count, natoms, shares),...  4.42 us
    pallas_call x1, Pallas kernels, tables(): pl.pallas_call(functools.partial(tables_kernel, natoms), out_shape=(jax.S...  4.33 us
    ppermute x3, waiting for transfers between devices, body(): lax.ppermute(term, 'mom', [(i, partner(i, step, shares)) for i in range(s...  2.31 us
    ppermute x3, starting transfers between devices, body(): lax.ppermute(term, 'mom', [(i, partner(i, step, shares)) for i in range(s...  2.16 us
    pallas_call x1, Pallas kernels, own_share(): pl.pallas_call(functools.partial(own_kernel, groups), out_shape=jax.Shape...  0.96 us
    pallas_call x1, Pallas kernels, combine(): pl.pallas_call(combine_kernel, out_shape=jax.ShapeDtypeStruct((count, sha...  0.69 us
  transfers between devices with their start and end apart: 7, of which 2 were waited for; matrix products, arithmetic and copies ran while one was open for 0% of the time, Pallas kernels for 19%

profile of v10, /device:TPU:0, one launch (start us, length us, event | category | flops | bytes accessed | tf_op | source)
XLA Modules:
  0.0 27.7 jit_solution(16451767940570554686)
XLA Ops:
  0.0 1.3 %collective-permute-start.3 = (bf16[2,16,2048]{2,1,0:T(8,128)(2,1)}, bf16[2,16,2048]{2,1,0:T(8,128)(2,1)S(1)}, u32[]{:S(2)}, u32[]{:S(2)}) collective-permute-start(bf16[2,16,2048]{2,1,0:T(8,128)(2,1)} %bitcast.4), channel_id=1, source_target_pairs={{8,0},{12,4},{16,8},{20,12},{24,16},{28,20},{9,1},{13,5},{17,9},{2... | collective-permute-start | bytes 393224 | tf_op jit(solution)/shard_map/ppermute | solution.py:430
  1.3 1.3 %collective-permute-start.2 = (bf16[2,16,2048]{2,1,0:T(8,128)(2,1)}, bf16[2,16,2048]{2,1,0:T(8,128)(2,1)S(1)}, u32[]{:S(2)}, u32[]{:S(2)}) collective-permute-start(bf16[2,16,2048]{2,1,0:T(8,128)(2,1)} %bitcast.5), channel_id=1, source_target_pairs={{4,0},{8,4},{12,8},{16,12},{20,16},{24,20},{28,24},{5,1},{9,5},{13... | collective-permute-start | bytes 393224 | tf_op jit(solution)/shard_map/ppermute | solution.py:430
  2.6 5.5 %collective-permute-start.1 = (bf16[2,16,2048]{2,1,0:T(8,128)(2,1)}, bf16[2,16,2048]{2,1,0:T(8,128)(2,1)S(1)}, u32[]{:S(2)}, u32[]{:S(2)}) collective-permute-start(bf16[2,16,2048]{2,1,0:T(8,128)(2,1)} %bitcast.6), channel_id=1, source_target_pairs={{0,4},{4,8},{8,12},{12,16},{16,20},{20,24},{24,28},{1,5},{5,9},{9,... | collective-permute-start | bytes 393224 | tf_op jit(solution)/shard_map/ppermute | solution.py:430
  8.1 4.6 %collective-permute-start = (bf16[2,16,2048]{2,1,0:T(8,128)(2,1)}, bf16[2,16,2048]{2,1,0:T(8,128)(2,1)S(1)}, u32[]{:S(2)}, u32[]{:S(2)}) collective-permute-start(bf16[2,16,2048]{2,1,0:T(8,128)(2,1)} %bitcast.7), channel_id=1, source_target_pairs={{0,8},{4,12},{8,16},{12,20},{16,24},{20,28},{1,9},{5,13},{9,17},{1... | collective-permute-start | bytes 393224 | tf_op jit(solution)/shard_map/ppermute | solution.py:430
  12.7 4.3 %tables.1 = (bf16[80,96,256]{2,1,0:T(8,128)(2,1)S(1)}, bf16[80,96,128]{2,1,0:T(8,128)(2,1)S(1)}, bf16[2,256,128]{2,1,0:T(8,128)(2,1)S(1)}) custom-call(bf16[2,16,2048]{2,1,0:T(8,128)(2,1)} %bitcast.8, bf16[5,3,16,1024]{3,2,1,0:T(8,128)(2,1)} %gradient_hbm.1, f32[270,1,16]{2,1,0:T(1,128)} %bitcast.3), custom_call_target="tpu_custom_call" | custom-call | flops 200000000 | bytes 6000000 | tf_op jit(solution)/shard_map/tables/pallas_call | solution.py:170
  17.1 0.0 collective-permute-done.3.above2
  17.1 0.0 collective-permute-done.2.above1
  17.1 0.0 collective-permute-done.1.below1
  17.1 0.0 collective-permute-done.below2
  17.1 4.4 %sandwich.1 = (bf16[128,128]{1,0:T(8,128)(2,1)S(1)}, bf16[128,128]{1,0:T(8,128)(2,1)S(1)}, bf16[128,128]{1,0:T(8,128)(2,1)S(1)}, bf16[20,128,256]{2,1,0:T(8,128)(2,1)S(1)}) custom-call(s32[5,16]{1,0:T(8,128)} %bitcast.9, s32[3]{0:T(128)} %offsets_hbm.1, bf16[2,256,128]{2,1,0:T(8,128)(2,1)S(1)} %get-tuple-element.12.middle_planes, ...), custom_call_target="tpu_custom_call" | custom-call | flops 800000000 | bytes 7000000 | tf_op jit(solution)/shard_map/sandwich/pallas_call | solution.py:349
  21.5 0.1 collective-permute-start.4
  21.6 2.0 %collective-permute-start.5 = (bf16[128,128]{1,0:T(8,128)(2,1)S(1)}, bf16[128,128]{1,0:T(8,128)(2,1)S(1)}, u32[]{:S(2)}, u32[]{:S(2)}) collective-permute-start(bf16[128,128]{1,0:T(8,128)(2,1)S(1)} %get-tuple-element.17), channel_id=1, source_target_pairs={{0,2},{1,3},{2,0},{3,1},{4,6},{5,7},{6,4},{7,5},{8,10},{9,11},{10,... | collective-permute-start | bytes 98312 | tf_op jit(solution)/shard_map/ppermute | solution.py:446
  23.6 0.1 collective-permute-start.6
  23.7 1.0 %own_share.1.own = f32[128,128]{1,0:T(8,128)S(1)} custom-call(bf16[20,128,256]{2,1,0:T(8,128)(2,1)S(1)} %get-tuple-element.15.blocks, bf16[80,96,256]{2,1,0:T(8,128)(2,1)S(1)} %get-tuple-element.13.kernel, bf16[80,96,128]{2,1,0:T(8,128)(2,1)S(1)} %get-tuple-element.14.derivs), custom_call_target="tpu_custom_call" | custom-call | flops 200000000 | bytes 2000000 | tf_op jit(solution)/shard_map/own_share/pallas_call | solution.py:387
  24.7 0.0 collective-permute-done.4.refs_0_
  24.7 0.9 %collective-permute-done.5.refs_1_ = bf16[128,128]{1,0:T(8,128)(2,1)S(1)} collective-permute-done((bf16[128,128]{1,0:T(8,128)(2,1)S(1)}, bf16[128,128]{1,0:T(8,128)(2,1)S(1)}, u32[]{:S(2)}, u32[]{:S(2)}) %collective-permute-start.5) | collective-permute-done | bytes 32800 | tf_op jit(solution)/shard_map/ppermute | solution.py:446
  25.6 1.4 %collective-permute-done.6.refs_2_ = bf16[128,128]{1,0:T(8,128)(2,1)S(1)} collective-permute-done((bf16[128,128]{1,0:T(8,128)(2,1)S(1)}, bf16[128,128]{1,0:T(8,128)(2,1)S(1)}, u32[]{:S(2)}, u32[]{:S(2)}) %collective-permute-start.6) | collective-permute-done | bytes 32800 | tf_op jit(solution)/shard_map/ppermute | solution.py:446
  27.0 0.7 %combine.1 = f32[2,4,2048]{2,1,0:T(4,128)} custom-call(f32[128,128]{1,0:T(8,128)S(1)} %own_share.1.own, bf16[128,128]{1,0:T(8,128)(2,1)S(1)} %collective-permute-done.4.refs_0_, bf16[128,128]{1,0:T(8,128)(2,1)S(1)} %collective-permute-done.5.refs_1_, bf16[128,128]{1,0:T(8,128)(2,1)S(1)} %collective-permute-done.6.refs_2_), custom_call_target="tpu_custom_call" | custom-call | tf_op jit(solution)/shard_map/combine/pallas_call | solution.py:416
Async XLA Ops:
  0.0 17.1 %collective-permute-start.3 = (bf16[2,16,2048]{2,1,0:T(8,128)(2,1)}, bf16[2,16,2048]{2,1,0:T(8,128)(2,1)S(1)}, u32[]{:S(2)}, u32[]{:S(2)}) collective-permute-start(bf16[2,16,2048]{2,1,0:T(8,128)(2,1)} %bitcast.4), channel_id=1, source_target_pairs={{8,0},{12,4},{16,8},{20,12},{24,16},{28,20},{9,1},{13,5},{17,9},{2... | collective-permute-start | bytes 393224 | tf_op jit(solution)/shard_map/ppermute | solution.py:430
  1.3 15.8 %collective-permute-start.2 = (bf16[2,16,2048]{2,1,0:T(8,128)(2,1)}, bf16[2,16,2048]{2,1,0:T(8,128)(2,1)S(1)}, u32[]{:S(2)}, u32[]{:S(2)}) collective-permute-start(bf16[2,16,2048]{2,1,0:T(8,128)(2,1)} %bitcast.5), channel_id=1, source_target_pairs={{4,0},{8,4},{12,8},{16,12},{20,16},{24,20},{28,24},{5,1},{9,5},{13... | collective-permute-start | bytes 393224 | tf_op jit(solution)/shard_map/ppermute | solution.py:430
  2.6 14.5 %collective-permute-start.1 = (bf16[2,16,2048]{2,1,0:T(8,128)(2,1)}, bf16[2,16,2048]{2,1,0:T(8,128)(2,1)S(1)}, u32[]{:S(2)}, u32[]{:S(2)}) collective-permute-start(bf16[2,16,2048]{2,1,0:T(8,128)(2,1)} %bitcast.6), channel_id=1, source_target_pairs={{0,4},{4,8},{8,12},{12,16},{16,20},{20,24},{24,28},{1,5},{5,9},{9,... | collective-permute-start | bytes 393224 | tf_op jit(solution)/shard_map/ppermute | solution.py:430
  8.1 9.0 %collective-permute-start = (bf16[2,16,2048]{2,1,0:T(8,128)(2,1)}, bf16[2,16,2048]{2,1,0:T(8,128)(2,1)S(1)}, u32[]{:S(2)}, u32[]{:S(2)}) collective-permute-start(bf16[2,16,2048]{2,1,0:T(8,128)(2,1)} %bitcast.7), channel_id=1, source_target_pairs={{0,8},{4,12},{8,16},{12,20},{16,24},{20,28},{1,9},{5,13},{9,17},{1... | collective-permute-start | bytes 393224 | tf_op jit(solution)/shard_map/ppermute | solution.py:430
  21.5 3.1 %collective-permute-start.4 = (bf16[128,128]{1,0:T(8,128)(2,1)S(1)}, bf16[128,128]{1,0:T(8,128)(2,1)S(1)}, u32[]{:S(2)}, u32[]{:S(2)}) collective-permute-start(bf16[128,128]{1,0:T(8,128)(2,1)S(1)} %get-tuple-element.16), channel_id=1, source_target_pairs={{0,1},{1,0},{2,3},{3,2},{4,5},{5,4},{6,7},{7,6},{8,9},{9,8},{10,11... | collective-permute-start | bytes 98312 | tf_op jit(solution)/shard_map/ppermute | solution.py:446
  21.6 4.0 %collective-permute-start.5 = (bf16[128,128]{1,0:T(8,128)(2,1)S(1)}, bf16[128,128]{1,0:T(8,128)(2,1)S(1)}, u32[]{:S(2)}, u32[]{:S(2)}) collective-permute-start(bf16[128,128]{1,0:T(8,128)(2,1)S(1)} %get-tuple-element.17), channel_id=1, source_target_pairs={{0,2},{1,3},{2,0},{3,1},{4,6},{5,7},{6,4},{7,5},{8,10},{9,11},{10,... | collective-permute-start | bytes 98312 | tf_op jit(solution)/shard_map/ppermute | solution.py:446
  23.6 3.3 %collective-permute-start.6 = (bf16[128,128]{1,0:T(8,128)(2,1)S(1)}, bf16[128,128]{1,0:T(8,128)(2,1)S(1)}, u32[]{:S(2)}, u32[]{:S(2)}) collective-permute-start(bf16[128,128]{1,0:T(8,128)(2,1)S(1)} %get-tuple-element.18), channel_id=1, source_target_pairs={{0,3},{1,2},{2,1},{3,0},{4,7},{5,6},{6,5},{7,4},{8,11},{9,10},{10,... | collective-permute-start | bytes 98312 | tf_op jit(solution)/shard_map/ppermute | solution.py:446

commit v11 on v10

--- a/solution.py
+++ b/solution.py
@@ -74,11 +74,12 @@
     return jnp.dot(left, right, preferred_element_type=jnp.float32)
 
 
-def make_planes(block, planes, at, order):
+def make_planes(block, planes, at, order, factor=None):
     count = block.shape[0]
-    ordered = dot(
-        order, jnp.concatenate([stack_tiles(block[e]) for e in range(count)], axis=1)
-    ).astype(jnp.bfloat16)
+    ordered = dot(order, jnp.concatenate([stack_tiles(block[e]) for e in range(count)], axis=1))
+    if factor is not None:
+        ordered = ordered * factor
+    ordered = ordered.astype(jnp.bfloat16)
     for e in range(count):
         planes[at + e] = ordered[:, e * LANES : (e + 1) * LANES]
 
@@ -273,7 +274,7 @@
 
 def sandwich_kernel(
     count, natoms, shares, neighbours_hbm, offsets_hbm, middle_planes,
-    below2, below1, above1, above2, kernel, derivs, *refs,
+    near_even, near_odd, far_odd, far_even, kernel, derivs, *refs,
 ):
     outs, own_blocks = refs[: shares - 1], refs[shares - 1]
     neighbours, offsets, planes, blocks, results, sems = refs[shares:]
@@ -287,8 +288,13 @@
     tiles = 2 * NO * NO // LANES
     groups = 2 * count
     order = row_matrix(tiles, natoms)
-    for piece, ref in ((0, below2), (1, below1), (3, above1), (4, above2)):
-        make_planes(ref, planes, piece * count, order)
+    place, length = lax.axis_index("energy"), lax.axis_size("energy")
+    for ref, reach, odd in (
+        (near_even, 1, 0), (near_odd, 1, 1), (far_odd, 2, 1), (far_even, 2, 0)
+    ):
+        other = neighbour(place, reach, odd)
+        exists = ((other >= 0) & (other < length)).astype(jnp.float32)
+        make_planes(ref, planes, (2 + other - place) * count, order, exists)
     planes[2 * count : 3 * count] = middle_planes[...]
 
     fold = fold_matrix()
@@ -341,8 +347,7 @@
 
 
 def sandwich(window, middle_planes, kernel, derivs, neighbours, offsets, shares):
-    below2, below1, above1, above2 = window
-    count, natoms, size = below2.shape
+    count, natoms, size = window[0].shape
     groups = 2 * count
     share = natoms // shares
     rows = share * groups * HI
@@ -368,7 +373,7 @@
         name="sandwich",
     )(
         in_hbm(neighbours), in_hbm(offsets),
-        middle_planes, below2, below1, above1, above2, kernel, derivs,
+        middle_planes, *window, kernel, derivs,
     )
 
 
@@ -424,9 +429,14 @@
     )(own, *parts)
 
 
-def shifted(array, axis, by):
+def neighbour(index, reach, odd):
+    return ((index + odd * reach) ^ reach) - odd * reach
+
+
+def exchanged(array, axis, reach, odd):
     length = lax.axis_size(axis)
-    pairs = [(i, i + by) for i in range(length) if 0 <= i + by < length]
+    others = [neighbour(i, reach, odd) for i in range(length)]
+    pairs = [(i, other if 0 <= other < length else i) for i, other in enumerate(others)]
     return lax.ppermute(array, axis, pairs)
 
 
@@ -435,10 +445,10 @@
     count, natoms, _ = local.shape
     shares = lax.axis_size("mom")
     remote = (
-        shifted(local, "energy", 2),
-        shifted(local, "energy", 1),
-        shifted(local, "energy", -1),
-        shifted(local, "energy", -2),
+        exchanged(local, "energy", 1, 0),
+        exchanged(local, "energy", 1, 1),
+        exchanged(local, "energy", 2, 1),
+        exchanged(local, "energy", 2, 0),
     )
     kernel, derivs, planes = tables(local, gradient, coupling.reshape(-1, 1, coupling.shape[-1]))
     *terms, own_blocks = sandwich(remote, planes, kernel, derivs, neighbours.T, offsets, shares)

time: 27.9 us -> 26.3 us (0.943)
  starting transfers between devices: 14.8 us -> 13.5 us
    ppermute x4, starting transfers between devices: 12.7 us -> 11.5 us  [exchanged(): return lax.ppermute(array, axis, pairs)]
  transfers between devices with their start and end apart: 7 -> 7, of which waited for: 2 -> 2; matrix products, arithmetic and copies ran while one was open for 0% -> 0% of each run, Pallas kernels for 19% -> 20%
where the time goes in v11:
time: 26.3 us; the launch traced here: 26.1 us
  starting transfers between devices  13.5 us (51%)
  Pallas kernels  10.4 us (40%)
  waiting for transfers between devices  2.12 us (8%)
    ppermute x4, starting transfers between devices, exchanged(): return lax.ppermute(array, axis, pairs)  11.5 us
    pallas_call x1, Pallas kernels, sandwich(): pl.pallas_call(functools.partial(sandwich_kernel, count, natoms, shares),...  4.44 us
    pallas_call x1, Pallas kernels, tables(): pl.pallas_call(functools.partial(tables_kernel, natoms), out_shape=(jax.S...  4.33 us
    ppermute x3, waiting for transfers between devices, body(): lax.ppermute(term, 'mom', [(i, partner(i, step, shares)) for i in range(s...  2.11 us
    ppermute x3, starting transfers between devices, body(): lax.ppermute(term, 'mom', [(i, partner(i, step, shares)) for i in range(s...  1.93 us
    pallas_call x1, Pallas kernels, own_share(): pl.pallas_call(functools.partial(own_kernel, groups), out_shape=jax.Shape...  0.96 us
    pallas_call x1, Pallas kernels, combine(): pl.pallas_call(combine_kernel, out_shape=jax.ShapeDtypeStruct((count, sha...  0.69 us
  transfers between devices with their start and end apart: 7, of which 2 were waited for; matrix products, arithmetic and copies ran while one was open for 0% of the time, Pallas kernels for 20%

profile of v11, /device:TPU:0, one launch (start us, length us, event | category | flops | bytes accessed | tf_op | source)
XLA Modules:
  0.0 26.1 jit_solution(5407772192272409708)
XLA Ops:
  0.0 3.0 %collective-permute-start.3 = (bf16[2,16,2048]{2,1,0:T(8,128)(2,1)}, bf16[2,16,2048]{2,1,0:T(8,128)(2,1)S(1)}, u32[]{:S(2)}, u32[]{:S(2)}) collective-permute-start(bf16[2,16,2048]{2,1,0:T(8,128)(2,1)} %bitcast.4), channel_id=1, source_target_pairs={{0,8},{4,12},{8,0},{12,4},{16,24},{20,28},{24,16},{28,20},{1,9},{5... | collective-permute-start | bytes 393224 | tf_op jit(solution)/shard_map/ppermute | solution.py:440
  3.0 1.6 %collective-permute-start.2 = (bf16[2,16,2048]{2,1,0:T(8,128)(2,1)}, bf16[2,16,2048]{2,1,0:T(8,128)(2,1)S(1)}, u32[]{:S(2)}, u32[]{:S(2)}) collective-permute-start(bf16[2,16,2048]{2,1,0:T(8,128)(2,1)} %bitcast.5), channel_id=1, source_target_pairs={{0,0},{4,4},{8,16},{12,20},{16,8},{20,12},{24,24},{28,28},{1,1},{5... | collective-permute-start | bytes 393224 | tf_op jit(solution)/shard_map/ppermute | solution.py:440
  4.6 1.6 %collective-permute-start.1 = (bf16[2,16,2048]{2,1,0:T(8,128)(2,1)}, bf16[2,16,2048]{2,1,0:T(8,128)(2,1)S(1)}, u32[]{:S(2)}, u32[]{:S(2)}) collective-permute-start(bf16[2,16,2048]{2,1,0:T(8,128)(2,1)} %bitcast.6), channel_id=1, source_target_pairs={{0,0},{4,8},{8,4},{12,16},{16,12},{20,24},{24,20},{28,28},{1,1},{5... | collective-permute-start | bytes 393224 | tf_op jit(solution)/shard_map/ppermute | solution.py:440
  6.1 5.4 %collective-permute-start = (bf16[2,16,2048]{2,1,0:T(8,128)(2,1)}, bf16[2,16,2048]{2,1,0:T(8,128)(2,1)S(1)}, u32[]{:S(2)}, u32[]{:S(2)}) collective-permute-start(bf16[2,16,2048]{2,1,0:T(8,128)(2,1)} %bitcast.7), channel_id=1, source_target_pairs={{0,4},{4,0},{8,12},{12,8},{16,20},{20,16},{24,28},{28,24},{1,5},{5... | collective-permute-start | bytes 393224 | tf_op jit(solution)/shard_map/ppermute | solution.py:440
  11.5 4.3 %tables.1 = (bf16[80,96,256]{2,1,0:T(8,128)(2,1)S(1)}, bf16[80,96,128]{2,1,0:T(8,128)(2,1)S(1)}, bf16[2,256,128]{2,1,0:T(8,128)(2,1)S(1)}) custom-call(bf16[2,16,2048]{2,1,0:T(8,128)(2,1)} %bitcast.8, bf16[5,3,16,1024]{3,2,1,0:T(8,128)(2,1)} %gradient_hbm.1, f32[270,1,16]{2,1,0:T(1,128)} %bitcast.3), custom_call_target="tpu_custom_call" | custom-call | flops 200000000 | bytes 6000000 | tf_op jit(solution)/shard_map/tables/pallas_call | solution.py:171
  15.9 0.0 collective-permute-done.3.far_even
  15.9 0.0 collective-permute-done.2.far_odd
  15.9 0.0 collective-permute-done.1.near_odd
  15.9 0.0 collective-permute-done.near_even
  15.9 4.4 %sandwich.1 = (bf16[128,128]{1,0:T(8,128)(2,1)S(1)}, bf16[128,128]{1,0:T(8,128)(2,1)S(1)}, bf16[128,128]{1,0:T(8,128)(2,1)S(1)}, bf16[20,128,256]{2,1,0:T(8,128)(2,1)S(1)}) custom-call(s32[5,16]{1,0:T(8,128)} %bitcast.9, s32[3]{0:T(128)} %offsets_hbm.1, bf16[2,256,128]{2,1,0:T(8,128)(2,1)S(1)} %get-tuple-element.12.middle_planes, ...), custom_call_target="tpu_custom_call" | custom-call | flops 800000000 | bytes 7000000 | tf_op jit(solution)/shard_map/sandwich/pallas_call | solution.py:354
  20.4 0.1 collective-permute-start.4
  20.4 1.6 %collective-permute-start.5 = (bf16[128,128]{1,0:T(8,128)(2,1)S(1)}, bf16[128,128]{1,0:T(8,128)(2,1)S(1)}, u32[]{:S(2)}, u32[]{:S(2)}) collective-permute-start(bf16[128,128]{1,0:T(8,128)(2,1)S(1)} %get-tuple-element.17), channel_id=1, source_target_pairs={{0,2},{1,3},{2,0},{3,1},{4,6},{5,7},{6,4},{7,5},{8,10},{9,11},{10,... | collective-permute-start | bytes 98312 | tf_op jit(solution)/shard_map/ppermute | solution.py:456
  22.0 0.3 %collective-permute-start.6 = (bf16[128,128]{1,0:T(8,128)(2,1)S(1)}, bf16[128,128]{1,0:T(8,128)(2,1)S(1)}, u32[]{:S(2)}, u32[]{:S(2)}) collective-permute-start(bf16[128,128]{1,0:T(8,128)(2,1)S(1)} %get-tuple-element.18), channel_id=1, source_target_pairs={{0,3},{1,2},{2,1},{3,0},{4,7},{5,6},{6,5},{7,4},{8,11},{9,10},{10,... | collective-permute-start | bytes 98312 | tf_op jit(solution)/shard_map/ppermute | solution.py:456
  22.3 1.0 %own_share.1.own = f32[128,128]{1,0:T(8,128)S(1)} custom-call(bf16[20,128,256]{2,1,0:T(8,128)(2,1)S(1)} %get-tuple-element.15.blocks, bf16[80,96,256]{2,1,0:T(8,128)(2,1)S(1)} %get-tuple-element.13.kernel, bf16[80,96,128]{2,1,0:T(8,128)(2,1)S(1)} %get-tuple-element.14.derivs), custom_call_target="tpu_custom_call" | custom-call | flops 200000000 | bytes 2000000 | tf_op jit(solution)/shard_map/own_share/pallas_call | solution.py:392
  23.3 0.0 collective-permute-done.4.refs_0_
  23.3 1.2 %collective-permute-done.5.refs_1_ = bf16[128,128]{1,0:T(8,128)(2,1)S(1)} collective-permute-done((bf16[128,128]{1,0:T(8,128)(2,1)S(1)}, bf16[128,128]{1,0:T(8,128)(2,1)S(1)}, u32[]{:S(2)}, u32[]{:S(2)}) %collective-permute-start.5) | collective-permute-done | bytes 32800 | tf_op jit(solution)/shard_map/ppermute | solution.py:456
  24.4 0.9 %collective-permute-done.6.refs_2_ = bf16[128,128]{1,0:T(8,128)(2,1)S(1)} collective-permute-done((bf16[128,128]{1,0:T(8,128)(2,1)S(1)}, bf16[128,128]{1,0:T(8,128)(2,1)S(1)}, u32[]{:S(2)}, u32[]{:S(2)}) %collective-permute-start.6) | collective-permute-done | bytes 32800 | tf_op jit(solution)/shard_map/ppermute | solution.py:456
  25.4 0.7 %combine.1 = f32[2,4,2048]{2,1,0:T(4,128)} custom-call(f32[128,128]{1,0:T(8,128)S(1)} %own_share.1.own, bf16[128,128]{1,0:T(8,128)(2,1)S(1)} %collective-permute-done.4.refs_0_, bf16[128,128]{1,0:T(8,128)(2,1)S(1)} %collective-permute-done.5.refs_1_, bf16[128,128]{1,0:T(8,128)(2,1)S(1)} %collective-permute-done.6.refs_2_), custom_call_target="tpu_custom_call" | custom-call | tf_op jit(solution)/shard_map/combine/pallas_call | solution.py:421
Async XLA Ops:
  0.0 15.9 %collective-permute-start.3 = (bf16[2,16,2048]{2,1,0:T(8,128)(2,1)}, bf16[2,16,2048]{2,1,0:T(8,128)(2,1)S(1)}, u32[]{:S(2)}, u32[]{:S(2)}) collective-permute-start(bf16[2,16,2048]{2,1,0:T(8,128)(2,1)} %bitcast.4), channel_id=1, source_target_pairs={{0,8},{4,12},{8,0},{12,4},{16,24},{20,28},{24,16},{28,20},{1,9},{5... | collective-permute-start | bytes 393224 | tf_op jit(solution)/shard_map/ppermute | solution.py:440
  3.0 12.9 %collective-permute-start.2 = (bf16[2,16,2048]{2,1,0:T(8,128)(2,1)}, bf16[2,16,2048]{2,1,0:T(8,128)(2,1)S(1)}, u32[]{:S(2)}, u32[]{:S(2)}) collective-permute-start(bf16[2,16,2048]{2,1,0:T(8,128)(2,1)} %bitcast.5), channel_id=1, source_target_pairs={{0,0},{4,4},{8,16},{12,20},{16,8},{20,12},{24,24},{28,28},{1,1},{5... | collective-permute-start | bytes 393224 | tf_op jit(solution)/shard_map/ppermute | solution.py:440
  4.6 11.3 %collective-permute-start.1 = (bf16[2,16,2048]{2,1,0:T(8,128)(2,1)}, bf16[2,16,2048]{2,1,0:T(8,128)(2,1)S(1)}, u32[]{:S(2)}, u32[]{:S(2)}) collective-permute-start(bf16[2,16,2048]{2,1,0:T(8,128)(2,1)} %bitcast.6), channel_id=1, source_target_pairs={{0,0},{4,8},{8,4},{12,16},{16,12},{20,24},{24,20},{28,28},{1,1},{5... | collective-permute-start | bytes 393224 | tf_op jit(solution)/shard_map/ppermute | solution.py:440
  6.1 9.8 %collective-permute-start = (bf16[2,16,2048]{2,1,0:T(8,128)(2,1)}, bf16[2,16,2048]{2,1,0:T(8,128)(2,1)S(1)}, u32[]{:S(2)}, u32[]{:S(2)}) collective-permute-start(bf16[2,16,2048]{2,1,0:T(8,128)(2,1)} %bitcast.7), channel_id=1, source_target_pairs={{0,4},{4,0},{8,12},{12,8},{16,20},{20,16},{24,28},{28,24},{1,5},{5... | collective-permute-start | bytes 393224 | tf_op jit(solution)/shard_map/ppermute | solution.py:440
  20.4 2.9 %collective-permute-start.4 = (bf16[128,128]{1,0:T(8,128)(2,1)S(1)}, bf16[128,128]{1,0:T(8,128)(2,1)S(1)}, u32[]{:S(2)}, u32[]{:S(2)}) collective-permute-start(bf16[128,128]{1,0:T(8,128)(2,1)S(1)} %get-tuple-element.16), channel_id=1, source_target_pairs={{0,1},{1,0},{2,3},{3,2},{4,5},{5,4},{6,7},{7,6},{8,9},{9,8},{10,11... | collective-permute-start | bytes 98312 | tf_op jit(solution)/shard_map/ppermute | solution.py:456
  20.4 4.0 %collective-permute-start.5 = (bf16[128,128]{1,0:T(8,128)(2,1)S(1)}, bf16[128,128]{1,0:T(8,128)(2,1)S(1)}, u32[]{:S(2)}, u32[]{:S(2)}) collective-permute-start(bf16[128,128]{1,0:T(8,128)(2,1)S(1)} %get-tuple-element.17), channel_id=1, source_target_pairs={{0,2},{1,3},{2,0},{3,1},{4,6},{5,7},{6,4},{7,5},{8,10},{9,11},{10,... | collective-permute-start | bytes 98312 | tf_op jit(solution)/shard_map/ppermute | solution.py:456
  22.0 3.3 %collective-permute-start.6 = (bf16[128,128]{1,0:T(8,128)(2,1)S(1)}, bf16[128,128]{1,0:T(8,128)(2,1)S(1)}, u32[]{:S(2)}, u32[]{:S(2)}) collective-permute-start(bf16[128,128]{1,0:T(8,128)(2,1)S(1)} %get-tuple-element.18), channel_id=1, source_target_pairs={{0,3},{1,2},{2,1},{3,0},{4,7},{5,6},{6,5},{7,4},{8,11},{9,10},{10,... | collective-permute-start | bytes 98312 | tf_op jit(solution)/shard_map/ppermute | solution.py:456

commit v12 on v11

--- a/solution.py
+++ b/solution.py
@@ -74,35 +74,29 @@
     return jnp.dot(left, right, preferred_element_type=jnp.float32)
 
 
-def make_planes(block, planes, at, order, factor=None):
+def make_planes(block, planes, at, order):
     count = block.shape[0]
     ordered = dot(order, jnp.concatenate([stack_tiles(block[e]) for e in range(count)], axis=1))
-    if factor is not None:
-        ordered = ordered * factor
     ordered = ordered.astype(jnp.bfloat16)
     for e in range(count):
         planes[at + e] = ordered[:, e * LANES : (e + 1) * LANES]
 
 
-def tables_kernel(
-    natoms, local_hbm, gradient_hbm, coupling_hbm, kernel_out, derivs_out, planes_out,
-    local, gradient, coupling, rows, sems,
+def weights_kernel(
+    natoms, local_hbm, gradient_hbm, coupling_hbm, rows, planes_out, local_out, gradient_out,
+    coupling, sems,
 ):
     copies = [
         pltpu.make_async_copy(coupling_hbm.at[:, 0, :], coupling, sems.at[0]),
-        pltpu.make_async_copy(gradient_hbm, gradient, sems.at[1]),
-        pltpu.make_async_copy(local_hbm, local, sems.at[2]),
+        pltpu.make_async_copy(local_hbm, local_out, sems.at[1]),
+        pltpu.make_async_copy(gradient_hbm, gradient_out, sems.at[2]),
     ]
     for copy in copies:
         copy.start()
 
-    tiles = NO * NO // LANES
-    block = natoms * tiles
     cells = ND * ND * NB
     depth = rows.shape[2]
     width = -(-NS * cells // LANES) * LANES
-    fold = fold_matrix()
-    order = row_matrix(tiles, natoms)
     lane = iota((width, 2 * LANES), 1)
     branch = over(lane, LANES) * COPIES + group_of(rest(lane, LANES))
     lane = iota((width, 2 * LANES), 0) - branch * cells
@@ -112,8 +106,11 @@
     chosen = lane == 0
     for s in range(1, NS):
         chosen = chosen | (lane == s * cells)
+    order = row_matrix(2 * NO * NO // LANES, natoms)
 
     copies[0].wait()
+    copies[1].wait()
+    make_planes(local_out, planes_out, 0, order)
     table = jnp.transpose(coupling[...])
     table = jnp.concatenate(
         [table, jnp.zeros((natoms, width - NS * cells), jnp.float32)], axis=1
@@ -128,8 +125,16 @@
             rows[at, half] = wide[
                 at * depth : (at + 1) * depth, half * LANES : (half + 1) * LANES
             ]
-
-    copies[1].wait()
+    copies[2].wait()
+
+
+def slots_kernel(natoms, gradient, local, received, derivs_out, local_out, planes_out):
+    local_out[...] = local[...]
+    make_planes(received, planes_out, 0, row_matrix(received.shape[2] // LANES, natoms))
+    tiles = NO * NO // LANES
+    block = natoms * tiles
+    fold = fold_matrix()
+    order = row_matrix(tiles, natoms)
     flats = [stack_tiles(gradient[slot, j]) for slot in range(NB) for j in range(ND)]
     ordered = dot(order, jnp.concatenate(flats, axis=1)).astype(jnp.bfloat16)
     stacked = [ordered[:, at : at + LANES] for at in range(0, NB * ND * LANES, LANES)]
@@ -146,11 +151,15 @@
                     axis=0,
                 ).astype(jnp.bfloat16)
 
-    copies[2].wait()
-    make_planes(local, planes_out, 0, row_matrix(2 * tiles, natoms))
+
+def tables_kernel(rows, derivs_in, local, received, kernel_out, local_out, planes_out):
+    local_out[...] = local[...]
+    make_planes(
+        received, planes_out, 0, row_matrix(received.shape[2] // LANES, received.shape[1])
+    )
 
     def one_cell(at, carry):
-        derivs = [derivs_out[at, j * NO : (j + 1) * NO, :] for j in range(ND)]
+        derivs = [derivs_in[at, j * NO : (j + 1) * NO, :] for j in range(ND)]
         for i in range(ND):
             for half in range(2):
                 total = None
@@ -162,34 +171,68 @@
                 kernel_out[at, i * NO : (i + 1) * NO, half * LANES : (half + 1) * LANES] = total
         return carry
 
-    lax.fori_loop(0, natoms * NB, one_cell, 0, unroll=4)
-
-
-def tables(local, gradient, coupling):
-    energies, natoms, size = local.shape
-    count = NB * natoms
-    return pl.pallas_call(
-        functools.partial(tables_kernel, natoms),
-        out_shape=(
-            jax.ShapeDtypeStruct((count, ND * NO, 2 * LANES), jnp.bfloat16),
-            jax.ShapeDtypeStruct((count, ND * NO, LANES), jnp.bfloat16),
-            jax.ShapeDtypeStruct((energies, natoms * size // LANES, LANES), jnp.bfloat16),
+    lax.fori_loop(0, kernel_out.shape[0], one_cell, 0, unroll=4)
+
+
+def on_device(kernel, name, outs, flops, scratch=()):
+    def call(*operands, hbm=()):
+        spaces = [pltpu.HBM] * len(hbm) + [pltpu.VMEM] * len(operands)
+        return pl.pallas_call(
+            kernel,
+            out_shape=outs,
+            in_specs=[pl.BlockSpec(memory_space=space) for space in spaces],
+            out_specs=jax.tree.map(lambda _: pl.BlockSpec(memory_space=pltpu.VMEM), outs),
+            scratch_shapes=list(scratch),
+            compiler_params=pltpu.CompilerParams(vmem_limit_bytes=VMEM_LIMIT),
+            cost_estimate=pl.CostEstimate(
+                flops=flops, bytes_accessed=6_000_000, transcendentals=0
+            ),
+            name=name,
+        )(*[in_hbm(array) for array in hbm], *operands)
+
+    return call
+
+
+def planes_of(block):
+    energies, natoms, size = block.shape
+    return jax.ShapeDtypeStruct((energies, natoms * size // LANES, LANES), block.dtype)
+
+
+def like(array):
+    return jax.ShapeDtypeStruct(array.shape, array.dtype)
+
+
+def weights(local, gradient, coupling):
+    count = NB * local.shape[1]
+    return on_device(
+        functools.partial(weights_kernel, local.shape[1]), "weights",
+        (
+            jax.ShapeDtypeStruct((count, 2, 2 * HI, LANES), jnp.float32),
+            planes_of(local), like(local), like(gradient),
         ),
-        in_specs=[pl.BlockSpec(memory_space=pltpu.HBM)] * 3,
-        out_specs=[pl.BlockSpec(memory_space=pltpu.VMEM)] * 3,
-        scratch_shapes=[
-            pltpu.VMEM(local.shape, local.dtype),
-            pltpu.VMEM(gradient.shape, gradient.dtype),
-            pltpu.VMEM((coupling.shape[0], natoms), jnp.float32),
-            pltpu.VMEM((count, 2, 2 * HI, LANES), jnp.float32),
+        200_000_000,
+        (
+            pltpu.VMEM((coupling.shape[0], local.shape[1]), jnp.float32),
             pltpu.SemaphoreType.DMA((3,)),
-        ],
-        compiler_params=pltpu.CompilerParams(vmem_limit_bytes=VMEM_LIMIT),
-        cost_estimate=pl.CostEstimate(
-            flops=200_000_000, bytes_accessed=6_000_000, transcendentals=0
         ),
-        name="tables",
-    )(in_hbm(local), in_hbm(gradient), in_hbm(coupling))
+    )(hbm=(local, gradient, coupling))
+
+
+def slots(gradient, local, received):
+    natoms = gradient.shape[2]
+    derivs = jax.ShapeDtypeStruct((NB * natoms, ND * NO, LANES), jnp.bfloat16)
+    return on_device(
+        functools.partial(slots_kernel, natoms), "slots",
+        (derivs, like(local), planes_of(received)), 200_000_000,
+    )(gradient, local, received)
+
+
+def tables(rows, derivs, local, received):
+    kernel = jax.ShapeDtypeStruct((rows.shape[0], ND * NO, 2 * LANES), jnp.bfloat16)
+    return on_device(
+        tables_kernel, "tables",
+        (kernel, like(local), planes_of(received)), 200_000_000,
+    )(rows, derivs, local, received)
 
 
 def partner(index, step, size):
@@ -274,7 +317,7 @@
 
 def sandwich_kernel(
     count, natoms, shares, neighbours_hbm, offsets_hbm, middle_planes,
-    near_even, near_odd, far_odd, far_even, kernel, derivs, *refs,
+    far_even, far_odd, near_odd, near_even, kernel, derivs, *refs,
 ):
     outs, own_blocks = refs[: shares - 1], refs[shares - 1]
     neighbours, offsets, planes, blocks, results, sems = refs[shares:]
@@ -290,11 +333,22 @@
     order = row_matrix(tiles, natoms)
     place, length = lax.axis_index("energy"), lax.axis_size("energy")
     for ref, reach, odd in (
-        (near_even, 1, 0), (near_odd, 1, 1), (far_odd, 2, 1), (far_even, 2, 0)
+        (far_even, 2, 0), (far_odd, 2, 1), (near_odd, 1, 1), (near_even, 1, 0)
     ):
         other = neighbour(place, reach, odd)
-        exists = ((other >= 0) & (other < length)).astype(jnp.float32)
-        make_planes(ref, planes, (2 + other - place) * count, order, exists)
+        exists = (other >= 0) & (other < length)
+        at = (2 + other - place) * count
+        if reach == 1:
+            make_planes(ref, planes, at, order)
+        else:
+            for e in range(count):
+                planes[at + e] = ref[e]
+
+        @pl.when(jnp.logical_not(exists))
+        def _():
+            for e in range(count):
+                planes[at + e] = jnp.zeros(planes.shape[1:], planes.dtype)
+
     planes[2 * count : 3 * count] = middle_planes[...]
 
     fold = fold_matrix()
@@ -347,7 +401,7 @@
 
 
 def sandwich(window, middle_planes, kernel, derivs, neighbours, offsets, shares):
-    count, natoms, size = window[0].shape
+    count, natoms, size = window[-1].shape
     groups = 2 * count
     share = natoms // shares
     rows = share * groups * HI
@@ -444,13 +498,16 @@
     local = green[0]
     count, natoms, _ = local.shape
     shares = lax.axis_size("mom")
-    remote = (
-        exchanged(local, "energy", 1, 0),
-        exchanged(local, "energy", 1, 1),
-        exchanged(local, "energy", 2, 1),
-        exchanged(local, "energy", 2, 0),
+    far_even = exchanged(local, "energy", 2, 0)
+    rows, planes, local, gradient = weights(
+        local, gradient, coupling.reshape(-1, 1, coupling.shape[-1])
     )
-    kernel, derivs, planes = tables(local, gradient, coupling.reshape(-1, 1, coupling.shape[-1]))
+    far_odd = exchanged(local, "energy", 2, 1)
+    derivs, local, far_even = slots(gradient, local, far_even)
+    near_odd = exchanged(local, "energy", 1, 1)
+    kernel, local, far_odd = tables(rows, derivs, local, far_odd)
+    near_even = exchanged(local, "energy", 1, 0)
+    remote = (far_even, far_odd, near_odd, near_even)
     *terms, own_blocks = sandwich(remote, planes, kernel, derivs, neighbours.T, offsets, shares)
     parts = [
         lax.ppermute(term, "mom", [(i, partner(i, step, shares)) for i in range(shares)])

time: 26.3 us -> 28.9 us (1.099)
  waiting for transfers between devices: 2.12 us -> 6.5 us
  starting transfers between devices: 13.5 us -> 12 us
  Pallas kernels: 10.4 us -> 10.1 us
    ppermute x4, waiting for transfers between devices: 0.01 us -> 4.39 us  [exchanged(): return lax.ppermute(array, axis, pairs)]
    ppermute x4, starting transfers between devices: 11.5 us -> 10.1 us  [exchanged(): return lax.ppermute(array, axis, pairs)]
    pallas_call x1 -> x3, Pallas kernels: 4.33 us -> 4.21 us  [call(): pl.pallas_call(kernel, out_shape=outs, in_specs=[pl.BlockSpec(memory_spac...]
  transfers between devices with their start and end apart: 7 -> 7, of which waited for: 2 -> 4; matrix products, arithmetic and copies ran while one was open for 0% -> 0% of each run, Pallas kernels for 20% -> 18%
where the time goes in v12:
time: 28.9 us; the launch traced here: 28.7 us
  starting transfers between devices  12 us (42%)
  Pallas kernels  10.1 us (35%)
  waiting for transfers between devices  6.5 us (22%)
    ppermute x4, starting transfers between devices, exchanged(): return lax.ppermute(array, axis, pairs)  10.1 us
    ppermute x4, waiting for transfers between devices, exchanged(): return lax.ppermute(array, axis, pairs)  4.39 us
    pallas_call x1, Pallas kernels, sandwich(): pl.pallas_call(functools.partial(sandwich_kernel, count, natoms, shares),...  4.29 us
    pallas_call x3, Pallas kernels, call(): pl.pallas_call(kernel, out_shape=outs, in_specs=[pl.BlockSpec(memory_spac...  4.21 us
    ppermute x3, waiting for transfers between devices, body(): lax.ppermute(term, 'mom', [(i, partner(i, step, shares)) for i in range(s...  2.11 us
    ppermute x3, starting transfers between devices, body(): lax.ppermute(term, 'mom', [(i, partner(i, step, shares)) for i in range(s...  1.93 us
    pallas_call x1, Pallas kernels, own_share(): pl.pallas_call(functools.partial(own_kernel, groups), out_shape=jax.Shape...  0.96 us
    pallas_call x1, Pallas kernels, combine(): pl.pallas_call(combine_kernel, out_shape=jax.ShapeDtypeStruct((count, sha...  0.69 us
  transfers between devices with their start and end apart: 7, of which 4 were waited for; matrix products, arithmetic and copies ran while one was open for 0% of the time, Pallas kernels for 18%

profile of v12, /device:TPU:0, one launch (start us, length us, event | category | flops | bytes accessed | tf_op | source)
XLA Modules:
  0.0 28.7 jit_solution(13716727166232524496)
XLA Ops:
  0.0 3.0 %collective-permute-start = (bf16[2,16,2048]{2,1,0:T(8,128)(2,1)}, bf16[2,16,2048]{2,1,0:T(8,128)(2,1)S(1)}, u32[]{:S(2)}, u32[]{:S(2)}) collective-permute-start(bf16[2,16,2048]{2,1,0:T(8,128)(2,1)} %bitcast.4), channel_id=1, source_target_pairs={{0,8},{4,12},{8,0},{12,4},{16,24},{20,28},{24,16},{28,20},{1,9},{5... | collective-permute-start | bytes 393224 | tf_op jit(solution)/shard_map/ppermute | solution.py:494
  3.0 1.6 %weights.1 = (f32[80,2,16,128]{3,2,1,0:T(8,128)S(1)}, bf16[2,256,128]{2,1,0:T(8,128)(2,1)S(1)}, bf16[2,16,2048]{2,1,0:T(8,128)(2,1)S(1)}, bf16[5,3,16,1024]{3,2,1,0:T(8,128)(2,1)S(1)}) custom-call(bf16[2,16,2048]{2,1,0:T(8,128)(2,1)} %bitcast.5, bf16[5,3,16,1024]{3,2,1,0:T(8,128)(2,1)} %gradient_hbm.1, f32[270,1,16]{2,1,0:T(1,128)} %bitcast.3), custom_call_target="tpu_custom_call" | custom-call | flops 200000000 | bytes 6000000 | tf_op jit(solution)/shard_map/weights/pallas_call | solution.py:180
  4.6 0.7 %collective-permute-start.1 = (bf16[2,16,2048]{2,1,0:T(8,128)(2,1)S(1)}, bf16[2,16,2048]{2,1,0:T(8,128)(2,1)S(1)}, u32[]{:S(2)}, u32[]{:S(2)}) collective-permute-start(bf16[2,16,2048]{2,1,0:T(8,128)(2,1)S(1)} %get-tuple-element.21.local), channel_id=1, source_target_pairs={{0,0},{4,4},{8,16},{12,20},{16,8},{20,12},{24,24},{28,28},{1,1},{5... | collective-permute-start | bytes 393224 | tf_op jit(solution)/shard_map/ppermute | solution.py:494
  5.3 1.4 %collective-permute-done.received = bf16[2,16,2048]{2,1,0:T(8,128)(2,1)S(1)} collective-permute-done((bf16[2,16,2048]{2,1,0:T(8,128)(2,1)}, bf16[2,16,2048]{2,1,0:T(8,128)(2,1)S(1)}, u32[]{:S(2)}, u32[]{:S(2)}) %collective-permute-start) | collective-permute-done | bytes 131104 | tf_op jit(solution)/shard_map/ppermute | solution.py:494
  6.7 0.8 %slots.1 = (bf16[80,96,128]{2,1,0:T(8,128)(2,1)S(1)}, bf16[2,16,2048]{2,1,0:T(8,128)(2,1)S(1)}, bf16[2,256,128]{2,1,0:T(8,128)(2,1)S(1)}) custom-call(bf16[5,3,16,1024]{3,2,1,0:T(8,128)(2,1)S(1)} %get-tuple-element.20.gradient, bf16[2,16,2048]{2,1,0:T(8,128)(2,1)S(1)} %get-tuple-element.21.local, bf16[2,16,2048]{2,1,0:T(8,128)(2,1)S(1)} %collective-permute-done.received), custom_call_target="tpu_custom_call" | custom-call | flops 200000000 | bytes 6000000 | tf_op jit(solution)/shard_map/slots/pallas_call | solution.py:180
  7.6 0.7 %collective-permute-start.2 = (bf16[2,16,2048]{2,1,0:T(8,128)(2,1)S(1)}, bf16[2,16,2048]{2,1,0:T(8,128)(2,1)S(1)}, u32[]{:S(2)}, u32[]{:S(2)}) collective-permute-start(bf16[2,16,2048]{2,1,0:T(8,128)(2,1)S(1)} %get-tuple-element.25.local), channel_id=1, source_target_pairs={{0,0},{4,8},{8,4},{12,16},{16,12},{20,24},{24,20},{28,28},{1,1},{5... | collective-permute-start | bytes 393224 | tf_op jit(solution)/shard_map/ppermute | solution.py:494
  8.2 0.0 collective-permute-done.1.received
  8.3 1.8 %tables.1 = (bf16[80,96,256]{2,1,0:T(8,128)(2,1)S(1)}, bf16[2,16,2048]{2,1,0:T(8,128)(2,1)S(1)}, bf16[2,256,128]{2,1,0:T(8,128)(2,1)S(1)}) custom-call(f32[80,2,16,128]{3,2,1,0:T(8,128)S(1)} %get-tuple-element.23.rows, bf16[80,96,128]{2,1,0:T(8,128)(2,1)S(1)} %get-tuple-element.24.derivs_in.derivs, bf16[2,16,2048]{2,1,0:T(8,128)(2,1)S(1)} %get-tuple-element.25.local, ...), custom_call_target="tpu_custom_call" | custom-call | flops 200000000 | bytes 6000000 | tf_op jit(solution)/shard_map/tables/pallas_call | solution.py:180
  10.1 5.7 %collective-permute-start.3 = (bf16[2,16,2048]{2,1,0:T(8,128)(2,1)S(1)}, bf16[2,16,2048]{2,1,0:T(8,128)(2,1)S(1)}, u32[]{:S(2)}, u32[]{:S(2)}) collective-permute-start(bf16[2,16,2048]{2,1,0:T(8,128)(2,1)S(1)} %get-tuple-element.27), channel_id=1, source_target_pairs={{0,4},{4,0},{8,12},{12,8},{16,20},{20,16},{24,28},{28,24},{1,5},{5... | collective-permute-start | bytes 393224 | tf_op jit(solution)/shard_map/ppermute | solution.py:494
  15.8 0.0 collective-permute-done.2.near_odd
  15.8 2.9 %collective-permute-done.3.near_even = bf16[2,16,2048]{2,1,0:T(8,128)(2,1)S(1)} collective-permute-done((bf16[2,16,2048]{2,1,0:T(8,128)(2,1)S(1)}, bf16[2,16,2048]{2,1,0:T(8,128)(2,1)S(1)}, u32[]{:S(2)}, u32[]{:S(2)}) %collective-permute-start.3) | collective-permute-done | bytes 131104 | tf_op jit(solution)/shard_map/ppermute | solution.py:494
  18.7 4.3 %sandwich.1 = (bf16[128,128]{1,0:T(8,128)(2,1)S(1)}, bf16[128,128]{1,0:T(8,128)(2,1)S(1)}, bf16[128,128]{1,0:T(8,128)(2,1)S(1)}, bf16[20,128,256]{2,1,0:T(8,128)(2,1)S(1)}) custom-call(s32[5,16]{1,0:T(8,128)} %bitcast.6, s32[3]{0:T(128)} %offsets_hbm.1, bf16[2,256,128]{2,1,0:T(8,128)(2,1)S(1)} %get-tuple-element.19.middle_planes, ...), custom_call_target="tpu_custom_call" | custom-call | flops 800000000 | bytes 7000000 | tf_op jit(solution)/shard_map/sandwich/pallas_call | solution.py:408
  23.0 0.1 collective-permute-start.4
  23.1 1.6 %collective-permute-start.5 = (bf16[128,128]{1,0:T(8,128)(2,1)S(1)}, bf16[128,128]{1,0:T(8,128)(2,1)S(1)}, u32[]{:S(2)}, u32[]{:S(2)}) collective-permute-start(bf16[128,128]{1,0:T(8,128)(2,1)S(1)} %get-tuple-element.31), channel_id=1, source_target_pairs={{0,2},{1,3},{2,0},{3,1},{4,6},{5,7},{6,4},{7,5},{8,10},{9,11},{10,... | collective-permute-start | bytes 98312 | tf_op jit(solution)/shard_map/ppermute | solution.py:513
  24.7 0.3 collective-permute-start.6
  25.0 1.0 %own_share.1.own = f32[128,128]{1,0:T(8,128)S(1)} custom-call(bf16[20,128,256]{2,1,0:T(8,128)(2,1)S(1)} %get-tuple-element.29.blocks, bf16[80,96,256]{2,1,0:T(8,128)(2,1)S(1)} %get-tuple-element.28.kernel, bf16[80,96,128]{2,1,0:T(8,128)(2,1)S(1)} %get-tuple-element.24.derivs_in.derivs), custom_call_target="tpu_custom_call" | custom-call | flops 200000000 | bytes 2000000 | tf_op jit(solution)/shard_map/own_share/pallas_call | solution.py:446
  25.9 0.0 collective-permute-done.4.refs_0_
  25.9 1.2 %collective-permute-done.5.refs_1_ = bf16[128,128]{1,0:T(8,128)(2,1)S(1)} collective-permute-done((bf16[128,128]{1,0:T(8,128)(2,1)S(1)}, bf16[128,128]{1,0:T(8,128)(2,1)S(1)}, u32[]{:S(2)}, u32[]{:S(2)}) %collective-permute-start.5) | collective-permute-done | bytes 32800 | tf_op jit(solution)/shard_map/ppermute | solution.py:513
  27.1 0.9 %collective-permute-done.6.refs_2_ = bf16[128,128]{1,0:T(8,128)(2,1)S(1)} collective-permute-done((bf16[128,128]{1,0:T(8,128)(2,1)S(1)}, bf16[128,128]{1,0:T(8,128)(2,1)S(1)}, u32[]{:S(2)}, u32[]{:S(2)}) %collective-permute-start.6) | collective-permute-done | bytes 32800 | tf_op jit(solution)/shard_map/ppermute | solution.py:513
  28.0 0.7 %combine.1 = f32[2,4,2048]{2,1,0:T(4,128)} custom-call(f32[128,128]{1,0:T(8,128)S(1)} %own_share.1.own, bf16[128,128]{1,0:T(8,128)(2,1)S(1)} %collective-permute-done.4.refs_0_, bf16[128,128]{1,0:T(8,128)(2,1)S(1)} %collective-permute-done.5.refs_1_, bf16[128,128]{1,0:T(8,128)(2,1)S(1)} %collective-permute-done.6.refs_2_), custom_call_target="tpu_custom_call" | custom-call | tf_op jit(solution)/shard_map/combine/pallas_call | solution.py:475
Async XLA Ops:
  0.0 6.7 %collective-permute-start = (bf16[2,16,2048]{2,1,0:T(8,128)(2,1)}, bf16[2,16,2048]{2,1,0:T(8,128)(2,1)S(1)}, u32[]{:S(2)}, u32[]{:S(2)}) collective-permute-start(bf16[2,16,2048]{2,1,0:T(8,128)(2,1)} %bitcast.4), channel_id=1, source_target_pairs={{0,8},{4,12},{8,0},{12,4},{16,24},{20,28},{24,16},{28,20},{1,9},{5... | collective-permute-start | bytes 393224 | tf_op jit(solution)/shard_map/ppermute | solution.py:494
  4.6 3.6 %collective-permute-start.1 = (bf16[2,16,2048]{2,1,0:T(8,128)(2,1)S(1)}, bf16[2,16,2048]{2,1,0:T(8,128)(2,1)S(1)}, u32[]{:S(2)}, u32[]{:S(2)}) collective-permute-start(bf16[2,16,2048]{2,1,0:T(8,128)(2,1)S(1)} %get-tuple-element.21.local), channel_id=1, source_target_pairs={{0,0},{4,4},{8,16},{12,20},{16,8},{20,12},{24,24},{28,28},{1,1},{5... | collective-permute-start | bytes 393224 | tf_op jit(solution)/shard_map/ppermute | solution.py:494
  7.6 8.2 %collective-permute-start.2 = (bf16[2,16,2048]{2,1,0:T(8,128)(2,1)S(1)}, bf16[2,16,2048]{2,1,0:T(8,128)(2,1)S(1)}, u32[]{:S(2)}, u32[]{:S(2)}) collective-permute-start(bf16[2,16,2048]{2,1,0:T(8,128)(2,1)S(1)} %get-tuple-element.25.local), channel_id=1, source_target_pairs={{0,0},{4,8},{8,4},{12,16},{16,12},{20,24},{24,20},{28,28},{1,1},{5... | collective-permute-start | bytes 393224 | tf_op jit(solution)/shard_map/ppermute | solution.py:494
  10.1 8.7 %collective-permute-start.3 = (bf16[2,16,2048]{2,1,0:T(8,128)(2,1)S(1)}, bf16[2,16,2048]{2,1,0:T(8,128)(2,1)S(1)}, u32[]{:S(2)}, u32[]{:S(2)}) collective-permute-start(bf16[2,16,2048]{2,1,0:T(8,128)(2,1)S(1)} %get-tuple-element.27), channel_id=1, source_target_pairs={{0,4},{4,0},{8,12},{12,8},{16,20},{20,16},{24,28},{28,24},{1,5},{5... | collective-permute-start | bytes 393224 | tf_op jit(solution)/shard_map/ppermute | solution.py:494
  23.0 2.9 %collective-permute-start.4 = (bf16[128,128]{1,0:T(8,128)(2,1)S(1)}, bf16[128,128]{1,0:T(8,128)(2,1)S(1)}, u32[]{:S(2)}, u32[]{:S(2)}) collective-permute-start(bf16[128,128]{1,0:T(8,128)(2,1)S(1)} %get-tuple-element.30), channel_id=1, source_target_pairs={{0,1},{1,0},{2,3},{3,2},{4,5},{5,4},{6,7},{7,6},{8,9},{9,8},{10,11... | collective-permute-start | bytes 98312 | tf_op jit(solution)/shard_map/ppermute | solution.py:513
  23.1 4.0 %collective-permute-start.5 = (bf16[128,128]{1,0:T(8,128)(2,1)S(1)}, bf16[128,128]{1,0:T(8,128)(2,1)S(1)}, u32[]{:S(2)}, u32[]{:S(2)}) collective-permute-start(bf16[128,128]{1,0:T(8,128)(2,1)S(1)} %get-tuple-element.31), channel_id=1, source_target_pairs={{0,2},{1,3},{2,0},{3,1},{4,6},{5,7},{6,4},{7,5},{8,10},{9,11},{10,... | collective-permute-start | bytes 98312 | tf_op jit(solution)/shard_map/ppermute | solution.py:513
  24.7 3.3 %collective-permute-start.6 = (bf16[128,128]{1,0:T(8,128)(2,1)S(1)}, bf16[128,128]{1,0:T(8,128)(2,1)S(1)}, u32[]{:S(2)}, u32[]{:S(2)}) collective-permute-start(bf16[128,128]{1,0:T(8,128)(2,1)S(1)} %get-tuple-element.32), channel_id=1, source_target_pairs={{0,3},{1,2},{2,1},{3,0},{4,7},{5,6},{6,5},{7,4},{8,11},{9,10},{10,... | collective-permute-start | bytes 98312 | tf_op jit(solution)/shard_map/ppermute | solution.py:513

commit v13 on v11

--- a/solution.py
+++ b/solution.py
@@ -274,7 +274,7 @@
 
 def sandwich_kernel(
     count, natoms, shares, neighbours_hbm, offsets_hbm, middle_planes,
-    near_even, near_odd, far_odd, far_even, kernel, derivs, *refs,
+    near_odd, far_odd, far_even, near_even, kernel, derivs, *refs,
 ):
     outs, own_blocks = refs[: shares - 1], refs[shares - 1]
     neighbours, offsets, planes, blocks, results, sems = refs[shares:]
@@ -290,7 +290,7 @@
     order = row_matrix(tiles, natoms)
     place, length = lax.axis_index("energy"), lax.axis_size("energy")
     for ref, reach, odd in (
-        (near_even, 1, 0), (near_odd, 1, 1), (far_odd, 2, 1), (far_even, 2, 0)
+        (near_odd, 1, 1), (far_odd, 2, 1), (far_even, 2, 0), (near_even, 1, 0)
     ):
         other = neighbour(place, reach, odd)
         exists = ((other >= 0) & (other < length)).astype(jnp.float32)
@@ -445,10 +445,10 @@
     count, natoms, _ = local.shape
     shares = lax.axis_size("mom")
     remote = (
-        exchanged(local, "energy", 1, 0),
         exchanged(local, "energy", 1, 1),
         exchanged(local, "energy", 2, 1),
         exchanged(local, "energy", 2, 0),
+        exchanged(local, "energy", 1, 0),
     )
     kernel, derivs, planes = tables(local, gradient, coupling.reshape(-1, 1, coupling.shape[-1]))
     *terms, own_blocks = sandwich(remote, planes, kernel, derivs, neighbours.T, offsets, shares)

time: 26.3 us -> 25.2 us (0.958)
  the two profiles are of different devices: /device:TPU:0 before, /device:TPU:9 now
where the time goes in v13:
time: 25.2 us; the launch traced here: 25 us
  starting transfers between devices  12.1 us (48%)
  Pallas kernels  10.4 us (41%)
  waiting for transfers between devices  2.46 us (10%)
    ppermute x4, starting transfers between devices, exchanged(): return lax.ppermute(array, axis, pairs)  7.62 us
    ppermute x3, starting transfers between devices, body(): lax.ppermute(term, 'mom', [(i, partner(i, step, shares)) for i in range(s...  4.44 us
    pallas_call x1, Pallas kernels, sandwich(): pl.pallas_call(functools.partial(sandwich_kernel, count, natoms, shares),...  4.43 us
    pallas_call x1, Pallas kernels, tables(): pl.pallas_call(functools.partial(tables_kernel, natoms), out_shape=(jax.S...  4.33 us
    ppermute x3, waiting for transfers between devices, body(): lax.ppermute(term, 'mom', [(i, partner(i, step, shares)) for i in range(s...  1.93 us
    pallas_call x1, Pallas kernels, own_share(): pl.pallas_call(functools.partial(own_kernel, groups), out_shape=jax.Shape...  0.96 us
    pallas_call x1, Pallas kernels, combine(): pl.pallas_call(combine_kernel, out_shape=jax.ShapeDtypeStruct((count, sha...  0.69 us
    ppermute x4, waiting for transfers between devices, exchanged(): return lax.ppermute(array, axis, pairs)  0.53 us
  transfers between devices with their start and end apart: 7, of which 3 were waited for; matrix products, arithmetic and copies ran while one was open for 0% of the time, Pallas kernels for 21%

profile of v13, /device:TPU:9, one launch (start us, length us, event | category | flops | bytes accessed | tf_op | source)
XLA Modules:
  0.0 25.0 jit_solution(10644981720454660899)
XLA Ops:
  0.0 1.2 %collective-permute-start.3 = (bf16[2,16,2048]{2,1,0:T(8,128)(2,1)}, bf16[2,16,2048]{2,1,0:T(8,128)(2,1)S(1)}, u32[]{:S(2)}, u32[]{:S(2)}) collective-permute-start(bf16[2,16,2048]{2,1,0:T(8,128)(2,1)} %bitcast.4), channel_id=1, source_target_pairs={{0,4},{4,0},{8,12},{12,8},{16,20},{20,16},{24,28},{28,24},{1,5},{5... | collective-permute-start | bytes 393224 | tf_op jit(solution)/shard_map/ppermute | solution.py:440
  1.2 0.2 collective-permute-start.2
  1.4 4.3 %collective-permute-start.1 = (bf16[2,16,2048]{2,1,0:T(8,128)(2,1)}, bf16[2,16,2048]{2,1,0:T(8,128)(2,1)S(1)}, u32[]{:S(2)}, u32[]{:S(2)}) collective-permute-start(bf16[2,16,2048]{2,1,0:T(8,128)(2,1)} %bitcast.6), channel_id=1, source_target_pairs={{0,0},{4,4},{8,16},{12,20},{16,8},{20,12},{24,24},{28,28},{1,1},{5... | collective-permute-start | bytes 393224 | tf_op jit(solution)/shard_map/ppermute | solution.py:440
  5.7 1.9 %collective-permute-start = (bf16[2,16,2048]{2,1,0:T(8,128)(2,1)}, bf16[2,16,2048]{2,1,0:T(8,128)(2,1)S(1)}, u32[]{:S(2)}, u32[]{:S(2)}) collective-permute-start(bf16[2,16,2048]{2,1,0:T(8,128)(2,1)} %bitcast.7), channel_id=1, source_target_pairs={{0,0},{4,8},{8,4},{12,16},{16,12},{20,24},{24,20},{28,28},{1,1},{5... | collective-permute-start | bytes 393224 | tf_op jit(solution)/shard_map/ppermute | solution.py:440
  7.6 4.3 %tables.1 = (bf16[80,96,256]{2,1,0:T(8,128)(2,1)S(1)}, bf16[80,96,128]{2,1,0:T(8,128)(2,1)S(1)}, bf16[2,256,128]{2,1,0:T(8,128)(2,1)S(1)}) custom-call(bf16[2,16,2048]{2,1,0:T(8,128)(2,1)} %bitcast.8, bf16[5,3,16,1024]{3,2,1,0:T(8,128)(2,1)} %gradient_hbm.1, f32[270,1,16]{2,1,0:T(1,128)} %bitcast.3), custom_call_target="tpu_custom_call" | custom-call | flops 200000000 | bytes 6000000 | tf_op jit(solution)/shard_map/tables/pallas_call | solution.py:171
  12.0 0.0 collective-permute-done.3.near_even
  12.0 0.0 collective-permute-done.2.far_even
  12.0 0.0 collective-permute-done.1.far_odd
  12.0 0.5 %collective-permute-done.near_odd = bf16[2,16,2048]{2,1,0:T(8,128)(2,1)S(1)} collective-permute-done((bf16[2,16,2048]{2,1,0:T(8,128)(2,1)}, bf16[2,16,2048]{2,1,0:T(8,128)(2,1)S(1)}, u32[]{:S(2)}, u32[]{:S(2)}) %collective-permute-start) | collective-permute-done | bytes 131104 | tf_op jit(solution)/shard_map/ppermute | solution.py:440
  12.5 4.4 %sandwich.1 = (bf16[128,128]{1,0:T(8,128)(2,1)S(1)}, bf16[128,128]{1,0:T(8,128)(2,1)S(1)}, bf16[128,128]{1,0:T(8,128)(2,1)S(1)}, bf16[20,128,256]{2,1,0:T(8,128)(2,1)S(1)}) custom-call(s32[5,16]{1,0:T(8,128)} %bitcast.9, s32[3]{0:T(128)} %offsets_hbm.1, bf16[2,256,128]{2,1,0:T(8,128)(2,1)S(1)} %get-tuple-element.12.middle_planes, ...), custom_call_target="tpu_custom_call" | custom-call | flops 800000000 | bytes 7000000 | tf_op jit(solution)/shard_map/sandwich/pallas_call | solution.py:354
  17.0 2.7 %collective-permute-start.4 = (bf16[128,128]{1,0:T(8,128)(2,1)S(1)}, bf16[128,128]{1,0:T(8,128)(2,1)S(1)}, u32[]{:S(2)}, u32[]{:S(2)}) collective-permute-start(bf16[128,128]{1,0:T(8,128)(2,1)S(1)} %get-tuple-element.16), channel_id=1, source_target_pairs={{0,1},{1,0},{2,3},{3,2},{4,5},{5,4},{6,7},{7,6},{8,9},{9,8},{10,11... | collective-permute-start | bytes 98312 | tf_op jit(solution)/shard_map/ppermute | solution.py:456
  19.7 1.3 %collective-permute-start.5 = (bf16[128,128]{1,0:T(8,128)(2,1)S(1)}, bf16[128,128]{1,0:T(8,128)(2,1)S(1)}, u32[]{:S(2)}, u32[]{:S(2)}) collective-permute-start(bf16[128,128]{1,0:T(8,128)(2,1)S(1)} %get-tuple-element.17), channel_id=1, source_target_pairs={{0,2},{1,3},{2,0},{3,1},{4,6},{5,7},{6,4},{7,5},{8,10},{9,11},{10,... | collective-permute-start | bytes 98312 | tf_op jit(solution)/shard_map/ppermute | solution.py:456
  21.0 0.5 %collective-permute-start.6 = (bf16[128,128]{1,0:T(8,128)(2,1)S(1)}, bf16[128,128]{1,0:T(8,128)(2,1)S(1)}, u32[]{:S(2)}, u32[]{:S(2)}) collective-permute-start(bf16[128,128]{1,0:T(8,128)(2,1)S(1)} %get-tuple-element.18), channel_id=1, source_target_pairs={{0,3},{1,2},{2,1},{3,0},{4,7},{5,6},{6,5},{7,4},{8,11},{9,10},{10,... | collective-permute-start | bytes 98312 | tf_op jit(solution)/shard_map/ppermute | solution.py:456
  21.4 1.0 %own_share.1.own = f32[128,128]{1,0:T(8,128)S(1)} custom-call(bf16[20,128,256]{2,1,0:T(8,128)(2,1)S(1)} %get-tuple-element.15.blocks, bf16[80,96,256]{2,1,0:T(8,128)(2,1)S(1)} %get-tuple-element.13.kernel, bf16[80,96,128]{2,1,0:T(8,128)(2,1)S(1)} %get-tuple-element.14.derivs), custom_call_target="tpu_custom_call" | custom-call | flops 200000000 | bytes 2000000 | tf_op jit(solution)/shard_map/own_share/pallas_call | solution.py:392
  22.4 0.0 collective-permute-done.4.refs_0_
  22.4 0.1 collective-permute-done.5.refs_1_
  22.5 1.8 %collective-permute-done.6.refs_2_ = bf16[128,128]{1,0:T(8,128)(2,1)S(1)} collective-permute-done((bf16[128,128]{1,0:T(8,128)(2,1)S(1)}, bf16[128,128]{1,0:T(8,128)(2,1)S(1)}, u32[]{:S(2)}, u32[]{:S(2)}) %collective-permute-start.6) | collective-permute-done | bytes 32800 | tf_op jit(solution)/shard_map/ppermute | solution.py:456
  24.3 0.7 %combine.1 = f32[2,4,2048]{2,1,0:T(4,128)} custom-call(f32[128,128]{1,0:T(8,128)S(1)} %own_share.1.own, bf16[128,128]{1,0:T(8,128)(2,1)S(1)} %collective-permute-done.4.refs_0_, bf16[128,128]{1,0:T(8,128)(2,1)S(1)} %collective-permute-done.5.refs_1_, bf16[128,128]{1,0:T(8,128)(2,1)S(1)} %collective-permute-done.6.refs_2_), custom_call_target="tpu_custom_call" | custom-call | tf_op jit(solution)/shard_map/combine/pallas_call | solution.py:421
Async XLA Ops:
  0.0 12.0 %collective-permute-start.3 = (bf16[2,16,2048]{2,1,0:T(8,128)(2,1)}, bf16[2,16,2048]{2,1,0:T(8,128)(2,1)S(1)}, u32[]{:S(2)}, u32[]{:S(2)}) collective-permute-start(bf16[2,16,2048]{2,1,0:T(8,128)(2,1)} %bitcast.4), channel_id=1, source_target_pairs={{0,4},{4,0},{8,12},{12,8},{16,20},{20,16},{24,28},{28,24},{1,5},{5... | collective-permute-start | bytes 393224 | tf_op jit(solution)/shard_map/ppermute | solution.py:440
  1.2 10.8 %collective-permute-start.2 = (bf16[2,16,2048]{2,1,0:T(8,128)(2,1)}, bf16[2,16,2048]{2,1,0:T(8,128)(2,1)S(1)}, u32[]{:S(2)}, u32[]{:S(2)}) collective-permute-start(bf16[2,16,2048]{2,1,0:T(8,128)(2,1)} %bitcast.5), channel_id=1, source_target_pairs={{0,8},{4,12},{8,0},{12,4},{16,24},{20,28},{24,16},{28,20},{1,9},{5... | collective-permute-start | bytes 393224 | tf_op jit(solution)/shard_map/ppermute | solution.py:440
  1.4 10.6 %collective-permute-start.1 = (bf16[2,16,2048]{2,1,0:T(8,128)(2,1)}, bf16[2,16,2048]{2,1,0:T(8,128)(2,1)S(1)}, u32[]{:S(2)}, u32[]{:S(2)}) collective-permute-start(bf16[2,16,2048]{2,1,0:T(8,128)(2,1)} %bitcast.6), channel_id=1, source_target_pairs={{0,0},{4,4},{8,16},{12,20},{16,8},{20,12},{24,24},{28,28},{1,1},{5... | collective-permute-start | bytes 393224 | tf_op jit(solution)/shard_map/ppermute | solution.py:440
  5.7 6.8 %collective-permute-start = (bf16[2,16,2048]{2,1,0:T(8,128)(2,1)}, bf16[2,16,2048]{2,1,0:T(8,128)(2,1)S(1)}, u32[]{:S(2)}, u32[]{:S(2)}) collective-permute-start(bf16[2,16,2048]{2,1,0:T(8,128)(2,1)} %bitcast.7), channel_id=1, source_target_pairs={{0,0},{4,8},{8,4},{12,16},{16,12},{20,24},{24,20},{28,28},{1,1},{5... | collective-permute-start | bytes 393224 | tf_op jit(solution)/shard_map/ppermute | solution.py:440
  17.0 5.4 %collective-permute-start.4 = (bf16[128,128]{1,0:T(8,128)(2,1)S(1)}, bf16[128,128]{1,0:T(8,128)(2,1)S(1)}, u32[]{:S(2)}, u32[]{:S(2)}) collective-permute-start(bf16[128,128]{1,0:T(8,128)(2,1)S(1)} %get-tuple-element.16), channel_id=1, source_target_pairs={{0,1},{1,0},{2,3},{3,2},{4,5},{5,4},{6,7},{7,6},{8,9},{9,8},{10,11... | collective-permute-start | bytes 98312 | tf_op jit(solution)/shard_map/ppermute | solution.py:456
  19.7 2.8 %collective-permute-start.5 = (bf16[128,128]{1,0:T(8,128)(2,1)S(1)}, bf16[128,128]{1,0:T(8,128)(2,1)S(1)}, u32[]{:S(2)}, u32[]{:S(2)}) collective-permute-start(bf16[128,128]{1,0:T(8,128)(2,1)S(1)} %get-tuple-element.17), channel_id=1, source_target_pairs={{0,2},{1,3},{2,0},{3,1},{4,6},{5,7},{6,4},{7,5},{8,10},{9,11},{10,... | collective-permute-start | bytes 98312 | tf_op jit(solution)/shard_map/ppermute | solution.py:456
  21.0 3.3 %collective-permute-start.6 = (bf16[128,128]{1,0:T(8,128)(2,1)S(1)}, bf16[128,128]{1,0:T(8,128)(2,1)S(1)}, u32[]{:S(2)}, u32[]{:S(2)}) collective-permute-start(bf16[128,128]{1,0:T(8,128)(2,1)S(1)} %get-tuple-element.18), channel_id=1, source_target_pairs={{0,3},{1,2},{2,1},{3,0},{4,7},{5,6},{6,5},{7,4},{8,11},{9,10},{10,... | collective-permute-start | bytes 98312 | tf_op jit(solution)/shard_map/ppermute | solution.py:456

commit v14 on v11

--- a/solution.py
+++ b/solution.py
@@ -274,7 +274,7 @@
 
 def sandwich_kernel(
     count, natoms, shares, neighbours_hbm, offsets_hbm, middle_planes,
-    near_even, near_odd, far_odd, far_even, kernel, derivs, *refs,
+    near_even, far_odd, far_even, near_odd, kernel, derivs, *refs,
 ):
     outs, own_blocks = refs[: shares - 1], refs[shares - 1]
     neighbours, offsets, planes, blocks, results, sems = refs[shares:]
@@ -290,7 +290,7 @@
     order = row_matrix(tiles, natoms)
     place, length = lax.axis_index("energy"), lax.axis_size("energy")
     for ref, reach, odd in (
-        (near_even, 1, 0), (near_odd, 1, 1), (far_odd, 2, 1), (far_even, 2, 0)
+        (near_even, 1, 0), (far_odd, 2, 1), (far_even, 2, 0), (near_odd, 1, 1)
     ):
         other = neighbour(place, reach, odd)
         exists = ((other >= 0) & (other < length)).astype(jnp.float32)
@@ -446,9 +446,9 @@
     shares = lax.axis_size("mom")
     remote = (
         exchanged(local, "energy", 1, 0),
-        exchanged(local, "energy", 1, 1),
         exchanged(local, "energy", 2, 1),
         exchanged(local, "energy", 2, 0),
+        exchanged(local, "energy", 1, 1),
     )
     kernel, derivs, planes = tables(local, gradient, coupling.reshape(-1, 1, coupling.shape[-1]))
     *terms, own_blocks = sandwich(remote, planes, kernel, derivs, neighbours.T, offsets, shares)

time: 26.3 us -> 24.3 us (0.924)
  starting transfers between devices: 13.5 us -> 11.5 us
    ppermute x4, starting transfers between devices: 11.5 us -> 9.58 us  [exchanged(): return lax.ppermute(array, axis, pairs)]
  transfers between devices with their start and end apart: 7 -> 7, of which waited for: 2 -> 2; matrix products, arithmetic and copies ran while one was open for 0% -> 0% of each run, Pallas kernels for 20% -> 22%
where the time goes in v14:
time: 24.3 us; the launch traced here: 24.1 us
  starting transfers between devices  11.5 us (47%)
  Pallas kernels  10.4 us (43%)
  waiting for transfers between devices  2.12 us (9%)
    ppermute x4, starting transfers between devices, exchanged(): return lax.ppermute(array, axis, pairs)  9.58 us
    pallas_call x1, Pallas kernels, sandwich(): pl.pallas_call(functools.partial(sandwich_kernel, count, natoms, shares),...  4.44 us
    pallas_call x1, Pallas kernels, tables(): pl.pallas_call(functools.partial(tables_kernel, natoms), out_shape=(jax.S...  4.33 us
    ppermute x3, waiting for transfers between devices, body(): lax.ppermute(term, 'mom', [(i, partner(i, step, shares)) for i in range(s...  2.11 us
    ppermute x3, starting transfers between devices, body(): lax.ppermute(term, 'mom', [(i, partner(i, step, shares)) for i in range(s...  1.93 us
    pallas_call x1, Pallas kernels, own_share(): pl.pallas_call(functools.partial(own_kernel, groups), out_shape=jax.Shape...  0.96 us
    pallas_call x1, Pallas kernels, combine(): pl.pallas_call(combine_kernel, out_shape=jax.ShapeDtypeStruct((count, sha...  0.69 us
  transfers between devices with their start and end apart: 7, of which 2 were waited for; matrix products, arithmetic and copies ran while one was open for 0% of the time, Pallas kernels for 22%

profile of v14, /device:TPU:0, one launch (start us, length us, event | category | flops | bytes accessed | tf_op | source)
XLA Modules:
  0.0 24.1 jit_solution(3756255540030202456)
XLA Ops:
  0.0 1.6 %collective-permute-start.3 = (bf16[2,16,2048]{2,1,0:T(8,128)(2,1)}, bf16[2,16,2048]{2,1,0:T(8,128)(2,1)S(1)}, u32[]{:S(2)}, u32[]{:S(2)}) collective-permute-start(bf16[2,16,2048]{2,1,0:T(8,128)(2,1)} %bitcast.4), channel_id=1, source_target_pairs={{0,0},{4,8},{8,4},{12,16},{16,12},{20,24},{24,20},{28,28},{1,1},{5... | collective-permute-start | bytes 393224 | tf_op jit(solution)/shard_map/ppermute | solution.py:440
  1.6 4.8 %collective-permute-start.2 = (bf16[2,16,2048]{2,1,0:T(8,128)(2,1)}, bf16[2,16,2048]{2,1,0:T(8,128)(2,1)S(1)}, u32[]{:S(2)}, u32[]{:S(2)}) collective-permute-start(bf16[2,16,2048]{2,1,0:T(8,128)(2,1)} %bitcast.5), channel_id=1, source_target_pairs={{0,8},{4,12},{8,0},{12,4},{16,24},{20,28},{24,16},{28,20},{1,9},{5... | collective-permute-start | bytes 393224 | tf_op jit(solution)/shard_map/ppermute | solution.py:440
  6.4 1.6 %collective-permute-start.1 = (bf16[2,16,2048]{2,1,0:T(8,128)(2,1)}, bf16[2,16,2048]{2,1,0:T(8,128)(2,1)S(1)}, u32[]{:S(2)}, u32[]{:S(2)}) collective-permute-start(bf16[2,16,2048]{2,1,0:T(8,128)(2,1)} %bitcast.6), channel_id=1, source_target_pairs={{0,0},{4,4},{8,16},{12,20},{16,8},{20,12},{24,24},{28,28},{1,1},{5... | collective-permute-start | bytes 393224 | tf_op jit(solution)/shard_map/ppermute | solution.py:440
  7.9 1.7 %collective-permute-start = (bf16[2,16,2048]{2,1,0:T(8,128)(2,1)}, bf16[2,16,2048]{2,1,0:T(8,128)(2,1)S(1)}, u32[]{:S(2)}, u32[]{:S(2)}) collective-permute-start(bf16[2,16,2048]{2,1,0:T(8,128)(2,1)} %bitcast.7), channel_id=1, source_target_pairs={{0,4},{4,0},{8,12},{12,8},{16,20},{20,16},{24,28},{28,24},{1,5},{5... | collective-permute-start | bytes 393224 | tf_op jit(solution)/shard_map/ppermute | solution.py:440
  9.6 4.3 %tables.1 = (bf16[80,96,256]{2,1,0:T(8,128)(2,1)S(1)}, bf16[80,96,128]{2,1,0:T(8,128)(2,1)S(1)}, bf16[2,256,128]{2,1,0:T(8,128)(2,1)S(1)}) custom-call(bf16[2,16,2048]{2,1,0:T(8,128)(2,1)} %bitcast.8, bf16[5,3,16,1024]{3,2,1,0:T(8,128)(2,1)} %gradient_hbm.1, f32[270,1,16]{2,1,0:T(1,128)} %bitcast.3), custom_call_target="tpu_custom_call" | custom-call | flops 200000000 | bytes 6000000 | tf_op jit(solution)/shard_map/tables/pallas_call | solution.py:171
  13.9 0.0 collective-permute-done.3.near_odd
  13.9 0.0 collective-permute-done.2.far_even
  13.9 0.0 collective-permute-done.1.far_odd
  14.0 0.0 collective-permute-done.near_even
  14.0 4.4 %sandwich.1 = (bf16[128,128]{1,0:T(8,128)(2,1)S(1)}, bf16[128,128]{1,0:T(8,128)(2,1)S(1)}, bf16[128,128]{1,0:T(8,128)(2,1)S(1)}, bf16[20,128,256]{2,1,0:T(8,128)(2,1)S(1)}) custom-call(s32[5,16]{1,0:T(8,128)} %bitcast.9, s32[3]{0:T(128)} %offsets_hbm.1, bf16[2,256,128]{2,1,0:T(8,128)(2,1)S(1)} %get-tuple-element.12.middle_planes, ...), custom_call_target="tpu_custom_call" | custom-call | flops 800000000 | bytes 7000000 | tf_op jit(solution)/shard_map/sandwich/pallas_call | solution.py:354
  18.4 0.1 collective-permute-start.4
  18.5 1.6 %collective-permute-start.5 = (bf16[128,128]{1,0:T(8,128)(2,1)S(1)}, bf16[128,128]{1,0:T(8,128)(2,1)S(1)}, u32[]{:S(2)}, u32[]{:S(2)}) collective-permute-start(bf16[128,128]{1,0:T(8,128)(2,1)S(1)} %get-tuple-element.17), channel_id=1, source_target_pairs={{0,2},{1,3},{2,0},{3,1},{4,6},{5,7},{6,4},{7,5},{8,10},{9,11},{10,... | collective-permute-start | bytes 98312 | tf_op jit(solution)/shard_map/ppermute | solution.py:456
  20.1 0.3 %collective-permute-start.6 = (bf16[128,128]{1,0:T(8,128)(2,1)S(1)}, bf16[128,128]{1,0:T(8,128)(2,1)S(1)}, u32[]{:S(2)}, u32[]{:S(2)}) collective-permute-start(bf16[128,128]{1,0:T(8,128)(2,1)S(1)} %get-tuple-element.18), channel_id=1, source_target_pairs={{0,3},{1,2},{2,1},{3,0},{4,7},{5,6},{6,5},{7,4},{8,11},{9,10},{10,... | collective-permute-start | bytes 98312 | tf_op jit(solution)/shard_map/ppermute | solution.py:456
  20.3 1.0 %own_share.1.own = f32[128,128]{1,0:T(8,128)S(1)} custom-call(bf16[20,128,256]{2,1,0:T(8,128)(2,1)S(1)} %get-tuple-element.15.blocks, bf16[80,96,256]{2,1,0:T(8,128)(2,1)S(1)} %get-tuple-element.13.kernel, bf16[80,96,128]{2,1,0:T(8,128)(2,1)S(1)} %get-tuple-element.14.derivs), custom_call_target="tpu_custom_call" | custom-call | flops 200000000 | bytes 2000000 | tf_op jit(solution)/shard_map/own_share/pallas_call | solution.py:392
  21.3 0.0 collective-permute-done.4.refs_0_
  21.3 1.2 %collective-permute-done.5.refs_1_ = bf16[128,128]{1,0:T(8,128)(2,1)S(1)} collective-permute-done((bf16[128,128]{1,0:T(8,128)(2,1)S(1)}, bf16[128,128]{1,0:T(8,128)(2,1)S(1)}, u32[]{:S(2)}, u32[]{:S(2)}) %collective-permute-start.5) | collective-permute-done | bytes 32800 | tf_op jit(solution)/shard_map/ppermute | solution.py:456
  22.5 1.0 %collective-permute-done.6.refs_2_ = bf16[128,128]{1,0:T(8,128)(2,1)S(1)} collective-permute-done((bf16[128,128]{1,0:T(8,128)(2,1)S(1)}, bf16[128,128]{1,0:T(8,128)(2,1)S(1)}, u32[]{:S(2)}, u32[]{:S(2)}) %collective-permute-start.6) | collective-permute-done | bytes 32800 | tf_op jit(solution)/shard_map/ppermute | solution.py:456
  23.4 0.7 %combine.1 = f32[2,4,2048]{2,1,0:T(4,128)} custom-call(f32[128,128]{1,0:T(8,128)S(1)} %own_share.1.own, bf16[128,128]{1,0:T(8,128)(2,1)S(1)} %collective-permute-done.4.refs_0_, bf16[128,128]{1,0:T(8,128)(2,1)S(1)} %collective-permute-done.5.refs_1_, bf16[128,128]{1,0:T(8,128)(2,1)S(1)} %collective-permute-done.6.refs_2_), custom_call_target="tpu_custom_call" | custom-call | tf_op jit(solution)/shard_map/combine/pallas_call | solution.py:421
Async XLA Ops:
  0.0 13.9 %collective-permute-start.3 = (bf16[2,16,2048]{2,1,0:T(8,128)(2,1)}, bf16[2,16,2048]{2,1,0:T(8,128)(2,1)S(1)}, u32[]{:S(2)}, u32[]{:S(2)}) collective-permute-start(bf16[2,16,2048]{2,1,0:T(8,128)(2,1)} %bitcast.4), channel_id=1, source_target_pairs={{0,0},{4,8},{8,4},{12,16},{16,12},{20,24},{24,20},{28,28},{1,1},{5... | collective-permute-start | bytes 393224 | tf_op jit(solution)/shard_map/ppermute | solution.py:440
  1.6 12.4 %collective-permute-start.2 = (bf16[2,16,2048]{2,1,0:T(8,128)(2,1)}, bf16[2,16,2048]{2,1,0:T(8,128)(2,1)S(1)}, u32[]{:S(2)}, u32[]{:S(2)}) collective-permute-start(bf16[2,16,2048]{2,1,0:T(8,128)(2,1)} %bitcast.5), channel_id=1, source_target_pairs={{0,8},{4,12},{8,0},{12,4},{16,24},{20,28},{24,16},{28,20},{1,9},{5... | collective-permute-start | bytes 393224 | tf_op jit(solution)/shard_map/ppermute | solution.py:440
  6.4 7.6 %collective-permute-start.1 = (bf16[2,16,2048]{2,1,0:T(8,128)(2,1)}, bf16[2,16,2048]{2,1,0:T(8,128)(2,1)S(1)}, u32[]{:S(2)}, u32[]{:S(2)}) collective-permute-start(bf16[2,16,2048]{2,1,0:T(8,128)(2,1)} %bitcast.6), channel_id=1, source_target_pairs={{0,0},{4,4},{8,16},{12,20},{16,8},{20,12},{24,24},{28,28},{1,1},{5... | collective-permute-start | bytes 393224 | tf_op jit(solution)/shard_map/ppermute | solution.py:440
  7.9 6.0 %collective-permute-start = (bf16[2,16,2048]{2,1,0:T(8,128)(2,1)}, bf16[2,16,2048]{2,1,0:T(8,128)(2,1)S(1)}, u32[]{:S(2)}, u32[]{:S(2)}) collective-permute-start(bf16[2,16,2048]{2,1,0:T(8,128)(2,1)} %bitcast.7), channel_id=1, source_target_pairs={{0,4},{4,0},{8,12},{12,8},{16,20},{20,16},{24,28},{28,24},{1,5},{5... | collective-permute-start | bytes 393224 | tf_op jit(solution)/shard_map/ppermute | solution.py:440
  18.4 2.9 %collective-permute-start.4 = (bf16[128,128]{1,0:T(8,128)(2,1)S(1)}, bf16[128,128]{1,0:T(8,128)(2,1)S(1)}, u32[]{:S(2)}, u32[]{:S(2)}) collective-permute-start(bf16[128,128]{1,0:T(8,128)(2,1)S(1)} %get-tuple-element.16), channel_id=1, source_target_pairs={{0,1},{1,0},{2,3},{3,2},{4,5},{5,4},{6,7},{7,6},{8,9},{9,8},{10,11... | collective-permute-start | bytes 98312 | tf_op jit(solution)/shard_map/ppermute | solution.py:456
  18.5 4.0 %collective-permute-start.5 = (bf16[128,128]{1,0:T(8,128)(2,1)S(1)}, bf16[128,128]{1,0:T(8,128)(2,1)S(1)}, u32[]{:S(2)}, u32[]{:S(2)}) collective-permute-start(bf16[128,128]{1,0:T(8,128)(2,1)S(1)} %get-tuple-element.17), channel_id=1, source_target_pairs={{0,2},{1,3},{2,0},{3,1},{4,6},{5,7},{6,4},{7,5},{8,10},{9,11},{10,... | collective-permute-start | bytes 98312 | tf_op jit(solution)/shard_map/ppermute | solution.py:456
  20.1 3.3 %collective-permute-start.6 = (bf16[128,128]{1,0:T(8,128)(2,1)S(1)}, bf16[128,128]{1,0:T(8,128)(2,1)S(1)}, u32[]{:S(2)}, u32[]{:S(2)}) collective-permute-start(bf16[128,128]{1,0:T(8,128)(2,1)S(1)} %get-tuple-element.18), channel_id=1, source_target_pairs={{0,3},{1,2},{2,1},{3,0},{4,7},{5,6},{6,5},{7,4},{8,11},{9,10},{10,... | collective-permute-start | bytes 98312 | tf_op jit(solution)/shard_map/ppermute | solution.py:456

commit v15 on v14

--- a/solution.py
+++ b/solution.py
@@ -276,8 +276,10 @@
     count, natoms, shares, neighbours_hbm, offsets_hbm, middle_planes,
     near_even, far_odd, far_even, near_odd, kernel, derivs, *refs,
 ):
-    outs, own_blocks = refs[: shares - 1], refs[shares - 1]
-    neighbours, offsets, planes, blocks, results, sems = refs[shares:]
+    early = 1
+    late = shares - early
+    outs, late_blocks = refs[:late], refs[late]
+    neighbours, offsets, planes, blocks, results, sems = refs[late + 1 :]
     copies = [
         pltpu.make_async_copy(neighbours_hbm, neighbours, sems.at[0]),
         pltpu.make_async_copy(offsets_hbm, offsets, sems.at[1]),
@@ -329,9 +331,11 @@
 
     me = lax.axis_index("mom")
     share = natoms // shares
-    for k in range(share):
-        for slot in range(NB):
-            own_blocks[k * NB + slot] = blocks[neighbours[slot, me * share + k]]
+    for step in range(early):
+        first = partner(me, step, shares) * share
+        for k in range(share):
+            for slot in range(NB):
+                late_blocks[(step * share + k) * NB + slot] = blocks[neighbours[slot, first + k]]
 
     def one_share(step, carry):
         first = partner(me, step, shares) * share
@@ -341,9 +345,9 @@
         ).astype(jnp.bfloat16)
         return carry
 
-    lax.fori_loop(1, shares, one_share, 0)
-    for step in range(1, shares):
-        outs[step - 1][...] = results[step]
+    lax.fori_loop(early, shares, one_share, 0)
+    for step in range(early, shares):
+        outs[step - early][...] = results[step]
 
 
 def sandwich(window, middle_planes, kernel, derivs, neighbours, offsets, shares):
@@ -351,13 +355,15 @@
     groups = 2 * count
     share = natoms // shares
     rows = share * groups * HI
+    early = 1
+    late = shares - early
     return pl.pallas_call(
         functools.partial(sandwich_kernel, count, natoms, shares),
-        out_shape=(jax.ShapeDtypeStruct((rows, LANES), jnp.bfloat16),) * (shares - 1)
-        + (jax.ShapeDtypeStruct((share * NB, groups * NO, 2 * LANES), jnp.bfloat16),),
+        out_shape=(jax.ShapeDtypeStruct((rows, LANES), jnp.bfloat16),) * late
+        + (jax.ShapeDtypeStruct((early * share * NB, groups * NO, 2 * LANES), jnp.bfloat16),),
         in_specs=[pl.BlockSpec(memory_space=pltpu.HBM)] * 2
         + [pl.BlockSpec(memory_space=pltpu.VMEM)] * 7,
-        out_specs=[pl.BlockSpec(memory_space=pltpu.VMEM)] * shares,
+        out_specs=[pl.BlockSpec(memory_space=pltpu.VMEM)] * (late + 1),
         scratch_shapes=[
             pltpu.SMEM(neighbours.shape, jnp.int32),
             pltpu.SMEM(offsets.shape, jnp.int32),
@@ -377,28 +383,32 @@
     )
 
 
-def own_kernel(groups, blocks, kernel, derivs, out):
-    share = blocks.shape[0] // NB
-    first = lax.axis_index("mom") * share
-    out[...] = share_terms(
-        [first + k for k in range(share)], groups,
-        lambda k, slot: blocks[k * NB + slot], kernel, derivs,
-    )
-
-
-def own_share(blocks, kernel, derivs):
-    share = blocks.shape[0] // NB
+def chip_kernel(groups, shares, blocks, kernel, derivs, own, *outs):
+    me = lax.axis_index("mom")
+    share = blocks.shape[0] // (NB * (1 + len(outs)))
+    for step, out in enumerate((own, *outs)):
+        first = partner(me, step, shares) * share
+        out[...] = share_terms(
+            [first + k for k in range(share)], groups,
+            lambda k, slot: blocks[(step * share + k) * NB + slot], kernel, derivs,
+        ).astype(out.dtype)
+
+
+def chip_shares(blocks, kernel, derivs, shares):
+    early = 1
     groups = blocks.shape[1] // NO
+    rows = blocks.shape[0] // (NB * early) * groups * HI
     return pl.pallas_call(
-        functools.partial(own_kernel, groups),
-        out_shape=jax.ShapeDtypeStruct((share * groups * HI, LANES), jnp.float32),
+        functools.partial(chip_kernel, groups, shares),
+        out_shape=(jax.ShapeDtypeStruct((rows, LANES), jnp.float32),)
+        + (jax.ShapeDtypeStruct((rows, LANES), jnp.bfloat16),) * (early - 1),
         in_specs=[pl.BlockSpec(memory_space=pltpu.VMEM)] * 3,
-        out_specs=pl.BlockSpec(memory_space=pltpu.VMEM),
+        out_specs=[pl.BlockSpec(memory_space=pltpu.VMEM)] * early,
         compiler_params=pltpu.CompilerParams(vmem_limit_bytes=VMEM_LIMIT),
         cost_estimate=pl.CostEstimate(
-            flops=200_000_000, bytes_accessed=2_000_000, transcendentals=0
+            flops=400_000_000, bytes_accessed=4_000_000, transcendentals=0
         ),
-        name="own_share",
+        name="chip_shares",
     )(blocks, kernel, derivs)
 
 
@@ -433,11 +443,18 @@
     return ((index + odd * reach) ^ reach) - odd * reach
 
 
-def exchanged(array, axis, reach, odd):
-    length = lax.axis_size(axis)
-    others = [neighbour(i, reach, odd) for i in range(length)]
-    pairs = [(i, other if 0 <= other < length else i) for i, other in enumerate(others)]
-    return lax.ppermute(array, axis, pairs)
+def exchanged(array, reach, odd):
+    energies, momenta = lax.axis_size("energy"), lax.axis_size("mom")
+    pairs = []
+    for i in range(energies):
+        other = neighbour(i, reach, odd)
+        for k in range(momenta):
+            if 0 <= other < energies:
+                target = other * momenta + k
+            else:
+                target = i * momenta + (k ^ 1 if momenta & 1 == 0 else k)
+            pairs.append((i * momenta + k, target))
+    return lax.ppermute(array, ("energy", "mom"), pairs)
 
 
 def body(green, coupling, gradient, neighbours, offsets):
@@ -445,18 +462,21 @@
     count, natoms, _ = local.shape
     shares = lax.axis_size("mom")
     remote = (
-        exchanged(local, "energy", 1, 0),
-        exchanged(local, "energy", 2, 1),
-        exchanged(local, "energy", 2, 0),
-        exchanged(local, "energy", 1, 1),
+        exchanged(local, 1, 0),
+        exchanged(local, 2, 1),
+        exchanged(local, 2, 0),
+        exchanged(local, 1, 1),
     )
     kernel, derivs, planes = tables(local, gradient, coupling.reshape(-1, 1, coupling.shape[-1]))
-    *terms, own_blocks = sandwich(remote, planes, kernel, derivs, neighbours.T, offsets, shares)
-    parts = [
-        lax.ppermute(term, "mom", [(i, partner(i, step, shares)) for i in range(shares)])
-        for step, term in enumerate(terms, 1)
-    ]
-    own = own_share(own_blocks, kernel, derivs)
+    *late, blocks = sandwich(remote, planes, kernel, derivs, neighbours.T, offsets, shares)
+
+    def sent(term, step):
+        pairs = [(i, partner(i, step, shares)) for i in range(shares)]
+        return lax.ppermute(term, "mom", pairs)
+
+    steps = [*range(shares // 2, shares), *range(1, shares // 2)]
+    parts = [sent(late[step - 1], step) for step in steps]
+    (own,) = chip_shares(blocks, kernel, derivs, shares)
     return combine(own, parts, count, natoms // shares)
 
 

time: 24.3 us -> 21.2 us (0.87)
  starting transfers between devices: 11.5 us -> 8.27 us
    ppermute x7, starting transfers between devices: 11.5 us -> 8.27 us  [the longest x4 6.07 us: exchanged(): return lax.ppermute(array, ('energy', 'mom'), pairs)]
  transfers between devices with their start and end apart: 7 -> 7, of which waited for: 2 -> 3; matrix products, arithmetic and copies ran while one was open for 0% -> 0% of each run, Pallas kernels for 22% -> 25%
where the time goes in v15:
time: 21.2 us; the launch traced here: 21 us
  Pallas kernels  10.4 us (49%)
  starting transfers between devices  8.27 us (39%)
  waiting for transfers between devices  2.28 us (11%)
    ppermute x4, starting transfers between devices, exchanged(): return lax.ppermute(array, ('energy', 'mom'), pairs)  6.07 us
    pallas_call x1, Pallas kernels, sandwich(): pl.pallas_call(functools.partial(sandwich_kernel, count, natoms, shares),...  4.44 us
    pallas_call x1, Pallas kernels, tables(): pl.pallas_call(functools.partial(tables_kernel, natoms), out_shape=(jax.S...  4.33 us
    ppermute x3, starting transfers between devices, sent(): return lax.ppermute(term, 'mom', pairs)  2.21 us
    ppermute x3, waiting for transfers between devices, sent(): return lax.ppermute(term, 'mom', pairs)  2.05 us
    pallas_call x1, Pallas kernels, chip_shares(): pl.pallas_call(functools.partial(chip_kernel, groups, shares), out_shape=...  0.96 us
    pallas_call x1, Pallas kernels, combine(): pl.pallas_call(combine_kernel, out_shape=jax.ShapeDtypeStruct((count, sha...  0.69 us
  transfers between devices with their start and end apart: 7, of which 3 were waited for; matrix products, arithmetic and copies ran while one was open for 0% of the time, Pallas kernels for 25%

profile of v15, /device:TPU:0, one launch (start us, length us, event | category | flops | bytes accessed | tf_op | source)
XLA Modules:
  0.0 21.0 jit_solution(2250136548218961742)
XLA Ops:
  0.0 0.5 %collective-permute-start.3 = (bf16[2,16,2048]{2,1,0:T(8,128)(2,1)}, bf16[2,16,2048]{2,1,0:T(8,128)(2,1)S(1)}, u32[]{:S(2)}, u32[]{:S(2)}) collective-permute-start(bf16[2,16,2048]{2,1,0:T(8,128)(2,1)} %bitcast.4), channel_id=1, source_target_pairs={{0,1},{1,0},{2,3},{3,2},{4,8},{5,9},{6,10},{7,11},{8,4},{9,5},{10,... | collective-permute-start | bytes 393224 | tf_op jit(solution)/shard_map/ppermute | solution.py:457
  0.5 3.9 %collective-permute-start.2 = (bf16[2,16,2048]{2,1,0:T(8,128)(2,1)}, bf16[2,16,2048]{2,1,0:T(8,128)(2,1)S(1)}, u32[]{:S(2)}, u32[]{:S(2)}) collective-permute-start(bf16[2,16,2048]{2,1,0:T(8,128)(2,1)} %bitcast.5), channel_id=1, source_target_pairs={{0,8},{1,9},{2,10},{3,11},{4,12},{5,13},{6,14},{7,15},{8,0},{9,1},... | collective-permute-start | bytes 393224 | tf_op jit(solution)/shard_map/ppermute | solution.py:457
  4.4 0.0 collective-permute-start.1
  4.4 1.7 %collective-permute-start = (bf16[2,16,2048]{2,1,0:T(8,128)(2,1)}, bf16[2,16,2048]{2,1,0:T(8,128)(2,1)S(1)}, u32[]{:S(2)}, u32[]{:S(2)}) collective-permute-start(bf16[2,16,2048]{2,1,0:T(8,128)(2,1)} %bitcast.7), channel_id=1, source_target_pairs={{0,4},{1,5},{2,6},{3,7},{4,0},{5,1},{6,2},{7,3},{8,12},{9,13},{10,... | collective-permute-start | bytes 393224 | tf_op jit(solution)/shard_map/ppermute | solution.py:457
  6.1 4.3 %tables.1 = (bf16[80,96,256]{2,1,0:T(8,128)(2,1)S(1)}, bf16[80,96,128]{2,1,0:T(8,128)(2,1)S(1)}, bf16[2,256,128]{2,1,0:T(8,128)(2,1)S(1)}) custom-call(bf16[2,16,2048]{2,1,0:T(8,128)(2,1)} %bitcast.8, bf16[5,3,16,1024]{3,2,1,0:T(8,128)(2,1)} %gradient_hbm.1, f32[270,1,16]{2,1,0:T(1,128)} %bitcast.3), custom_call_target="tpu_custom_call" | custom-call | flops 200000000 | bytes 6000000 | tf_op jit(solution)/shard_map/tables/pallas_call | solution.py:171
  10.4 0.0 collective-permute-done.3.near_odd
  10.4 0.2 %collective-permute-done.2.far_even = bf16[2,16,2048]{2,1,0:T(8,128)(2,1)S(1)} collective-permute-done((bf16[2,16,2048]{2,1,0:T(8,128)(2,1)}, bf16[2,16,2048]{2,1,0:T(8,128)(2,1)S(1)}, u32[]{:S(2)}, u32[]{:S(2)}) %collective-permute-start.2) | collective-permute-done | bytes 131104 | tf_op jit(solution)/shard_map/ppermute | solution.py:457
  10.6 0.0 collective-permute-done.1.far_odd
  10.6 0.0 collective-permute-done.near_even
  10.6 4.4 %sandwich.1 = (bf16[128,128]{1,0:T(8,128)(2,1)S(1)}, bf16[128,128]{1,0:T(8,128)(2,1)S(1)}, bf16[128,128]{1,0:T(8,128)(2,1)S(1)}, bf16[20,128,256]{2,1,0:T(8,128)(2,1)S(1)}) custom-call(s32[5,16]{1,0:T(8,128)} %bitcast.9, s32[3]{0:T(128)} %offsets_hbm.1, bf16[2,256,128]{2,1,0:T(8,128)(2,1)S(1)} %get-tuple-element.12.middle_planes, ...), custom_call_target="tpu_custom_call" | custom-call | flops 800000000 | bytes 7000000 | tf_op jit(solution)/shard_map/sandwich/pallas_call | solution.py:360
  15.1 1.6 %collective-permute-start.4 = (bf16[128,128]{1,0:T(8,128)(2,1)S(1)}, bf16[128,128]{1,0:T(8,128)(2,1)S(1)}, u32[]{:S(2)}, u32[]{:S(2)}) collective-permute-start(bf16[128,128]{1,0:T(8,128)(2,1)S(1)} %get-tuple-element.16), channel_id=1, source_target_pairs={{0,2},{1,3},{2,0},{3,1},{4,6},{5,7},{6,4},{7,5},{8,10},{9,11},{10,... | collective-permute-start | bytes 98312 | tf_op jit(solution)/shard_map/ppermute | solution.py:475
  16.7 0.0 collective-permute-start.5
  16.7 0.6 %collective-permute-start.6 = (bf16[128,128]{1,0:T(8,128)(2,1)S(1)}, bf16[128,128]{1,0:T(8,128)(2,1)S(1)}, u32[]{:S(2)}, u32[]{:S(2)}) collective-permute-start(bf16[128,128]{1,0:T(8,128)(2,1)S(1)} %get-tuple-element.18), channel_id=1, source_target_pairs={{0,1},{1,0},{2,3},{3,2},{4,5},{5,4},{6,7},{7,6},{8,9},{9,8},{10,11... | collective-permute-start | bytes 98312 | tf_op jit(solution)/shard_map/ppermute | solution.py:475
  17.3 1.0 %chip_shares.1.own = f32[128,128]{1,0:T(8,128)S(1)} custom-call(bf16[20,128,256]{2,1,0:T(8,128)(2,1)S(1)} %get-tuple-element.15.blocks, bf16[80,96,256]{2,1,0:T(8,128)(2,1)S(1)} %get-tuple-element.13.kernel, bf16[80,96,128]{2,1,0:T(8,128)(2,1)S(1)} %get-tuple-element.14.derivs), custom_call_target="tpu_custom_call" | custom-call | flops 400000000 | bytes 4000000 | tf_op jit(solution)/shard_map/chip_shares/pallas_call | solution.py:401
  18.3 0.8 %collective-permute-done.4.refs_0_ = bf16[128,128]{1,0:T(8,128)(2,1)S(1)} collective-permute-done((bf16[128,128]{1,0:T(8,128)(2,1)S(1)}, bf16[128,128]{1,0:T(8,128)(2,1)S(1)}, u32[]{:S(2)}, u32[]{:S(2)}) %collective-permute-start.4) | collective-permute-done | bytes 32800 | tf_op jit(solution)/shard_map/ppermute | solution.py:475
  19.1 1.2 %collective-permute-done.5.refs_1_ = bf16[128,128]{1,0:T(8,128)(2,1)S(1)} collective-permute-done((bf16[128,128]{1,0:T(8,128)(2,1)S(1)}, bf16[128,128]{1,0:T(8,128)(2,1)S(1)}, u32[]{:S(2)}, u32[]{:S(2)}) %collective-permute-start.5) | collective-permute-done | bytes 32800 | tf_op jit(solution)/shard_map/ppermute | solution.py:475
  20.3 0.0 collective-permute-done.6.refs_2_
  20.3 0.7 %combine.1 = f32[2,4,2048]{2,1,0:T(4,128)} custom-call(f32[128,128]{1,0:T(8,128)S(1)} %chip_shares.1.own, bf16[128,128]{1,0:T(8,128)(2,1)S(1)} %collective-permute-done.4.refs_0_, bf16[128,128]{1,0:T(8,128)(2,1)S(1)} %collective-permute-done.5.refs_1_, bf16[128,128]{1,0:T(8,128)(2,1)S(1)} %collective-permute-done.6.refs_2_), custom_call_target="tpu_custom_call" | custom-call | tf_op jit(solution)/shard_map/combine/pallas_call | solution.py:431
Async XLA Ops:
  0.0 10.4 %collective-permute-start.3 = (bf16[2,16,2048]{2,1,0:T(8,128)(2,1)}, bf16[2,16,2048]{2,1,0:T(8,128)(2,1)S(1)}, u32[]{:S(2)}, u32[]{:S(2)}) collective-permute-start(bf16[2,16,2048]{2,1,0:T(8,128)(2,1)} %bitcast.4), channel_id=1, source_target_pairs={{0,1},{1,0},{2,3},{3,2},{4,8},{5,9},{6,10},{7,11},{8,4},{9,5},{10,... | collective-permute-start | bytes 393224 | tf_op jit(solution)/shard_map/ppermute | solution.py:457
  0.5 10.2 %collective-permute-start.2 = (bf16[2,16,2048]{2,1,0:T(8,128)(2,1)}, bf16[2,16,2048]{2,1,0:T(8,128)(2,1)S(1)}, u32[]{:S(2)}, u32[]{:S(2)}) collective-permute-start(bf16[2,16,2048]{2,1,0:T(8,128)(2,1)} %bitcast.5), channel_id=1, source_target_pairs={{0,8},{1,9},{2,10},{3,11},{4,12},{5,13},{6,14},{7,15},{8,0},{9,1},... | collective-permute-start | bytes 393224 | tf_op jit(solution)/shard_map/ppermute | solution.py:457
  4.4 6.2 %collective-permute-start.1 = (bf16[2,16,2048]{2,1,0:T(8,128)(2,1)}, bf16[2,16,2048]{2,1,0:T(8,128)(2,1)S(1)}, u32[]{:S(2)}, u32[]{:S(2)}) collective-permute-start(bf16[2,16,2048]{2,1,0:T(8,128)(2,1)} %bitcast.6), channel_id=1, source_target_pairs={{0,1},{1,0},{2,3},{3,2},{4,5},{5,4},{6,7},{7,6},{8,16},{9,17},{10,... | collective-permute-start | bytes 393224 | tf_op jit(solution)/shard_map/ppermute | solution.py:457
  4.4 6.2 %collective-permute-start = (bf16[2,16,2048]{2,1,0:T(8,128)(2,1)}, bf16[2,16,2048]{2,1,0:T(8,128)(2,1)S(1)}, u32[]{:S(2)}, u32[]{:S(2)}) collective-permute-start(bf16[2,16,2048]{2,1,0:T(8,128)(2,1)} %bitcast.7), channel_id=1, source_target_pairs={{0,4},{1,5},{2,6},{3,7},{4,0},{5,1},{6,2},{7,3},{8,12},{9,13},{10,... | collective-permute-start | bytes 393224 | tf_op jit(solution)/shard_map/ppermute | solution.py:457
  15.1 4.0 %collective-permute-start.4 = (bf16[128,128]{1,0:T(8,128)(2,1)S(1)}, bf16[128,128]{1,0:T(8,128)(2,1)S(1)}, u32[]{:S(2)}, u32[]{:S(2)}) collective-permute-start(bf16[128,128]{1,0:T(8,128)(2,1)S(1)} %get-tuple-element.16), channel_id=1, source_target_pairs={{0,2},{1,3},{2,0},{3,1},{4,6},{5,7},{6,4},{7,5},{8,10},{9,11},{10,... | collective-permute-start | bytes 98312 | tf_op jit(solution)/shard_map/ppermute | solution.py:475
  16.7 3.6 %collective-permute-start.5 = (bf16[128,128]{1,0:T(8,128)(2,1)S(1)}, bf16[128,128]{1,0:T(8,128)(2,1)S(1)}, u32[]{:S(2)}, u32[]{:S(2)}) collective-permute-start(bf16[128,128]{1,0:T(8,128)(2,1)S(1)} %get-tuple-element.17), channel_id=1, source_target_pairs={{0,3},{1,2},{2,1},{3,0},{4,7},{5,6},{6,5},{7,4},{8,11},{9,10},{10,... | collective-permute-start | bytes 98312 | tf_op jit(solution)/shard_map/ppermute | solution.py:475
  16.7 3.6 %collective-permute-start.6 = (bf16[128,128]{1,0:T(8,128)(2,1)S(1)}, bf16[128,128]{1,0:T(8,128)(2,1)S(1)}, u32[]{:S(2)}, u32[]{:S(2)}) collective-permute-start(bf16[128,128]{1,0:T(8,128)(2,1)S(1)} %get-tuple-element.18), channel_id=1, source_target_pairs={{0,1},{1,0},{2,3},{3,2},{4,5},{5,4},{6,7},{7,6},{8,9},{9,8},{10,11... | collective-permute-start | bytes 98312 | tf_op jit(solution)/shard_map/ppermute | solution.py:475

commit v16 on v15

--- a/solution.py
+++ b/solution.py
@@ -274,7 +274,7 @@
 
 def sandwich_kernel(
     count, natoms, shares, neighbours_hbm, offsets_hbm, middle_planes,
-    near_even, far_odd, far_even, near_odd, kernel, derivs, *refs,
+    far_odd, far_even, near_even, near_odd, kernel, derivs, *refs,
 ):
     early = 1
     late = shares - early
@@ -292,7 +292,7 @@
     order = row_matrix(tiles, natoms)
     place, length = lax.axis_index("energy"), lax.axis_size("energy")
     for ref, reach, odd in (
-        (near_even, 1, 0), (far_odd, 2, 1), (far_even, 2, 0), (near_odd, 1, 1)
+        (far_odd, 2, 1), (far_even, 2, 0), (near_even, 1, 0), (near_odd, 1, 1)
     ):
         other = neighbour(place, reach, odd)
         exists = ((other >= 0) & (other < length)).astype(jnp.float32)
@@ -462,9 +462,9 @@
     count, natoms, _ = local.shape
     shares = lax.axis_size("mom")
     remote = (
-        exchanged(local, 1, 0),
         exchanged(local, 2, 1),
         exchanged(local, 2, 0),
+        exchanged(local, 1, 0),
         exchanged(local, 1, 1),
     )
     kernel, derivs, planes = tables(local, gradient, coupling.reshape(-1, 1, coupling.shape[-1]))
@@ -474,8 +474,7 @@
         pairs = [(i, partner(i, step, shares)) for i in range(shares)]
         return lax.ppermute(term, "mom", pairs)
 
-    steps = [*range(shares // 2, shares), *range(1, shares // 2)]
-    parts = [sent(late[step - 1], step) for step in steps]
+    parts = [sent(term, step) for step, term in enumerate(late, 1)]
     (own,) = chip_shares(blocks, kernel, derivs, shares)
     return combine(own, parts, count, natoms // shares)
 

time: 21.2 us -> 21.6 us (1.019)
  waiting for transfers between devices: 2.28 us -> 2.82 us
  starting transfers between devices: 8.27 us -> 8.01 us
    ppermute x3, waiting for transfers between devices: 2.05 us -> 2.61 us  [sent(): return lax.ppermute(term, 'mom', pairs)]
    ppermute x3, starting transfers between devices: 2.21 us -> 1.94 us  [sent(): return lax.ppermute(term, 'mom', pairs)]
where the time goes in v16:
time: 21.6 us; the launch traced here: 21.4 us
  Pallas kernels  10.5 us (49%)
  starting transfers between devices  8.01 us (37%)
  waiting for transfers between devices  2.82 us (13%)
    ppermute x4, starting transfers between devices, exchanged(): return lax.ppermute(array, ('energy', 'mom'), pairs)  6.07 us
    pallas_call x1, Pallas kernels, sandwich(): pl.pallas_call(functools.partial(sandwich_kernel, count, natoms, shares),...  4.56 us
    pallas_call x1, Pallas kernels, tables(): pl.pallas_call(functools.partial(tables_kernel, natoms), out_shape=(jax.S...  4.33 us
    ppermute x3, waiting for transfers between devices, sent(): return lax.ppermute(term, 'mom', pairs)  2.61 us
    ppermute x3, starting transfers between devices, sent(): return lax.ppermute(term, 'mom', pairs)  1.94 us
    pallas_call x1, Pallas kernels, chip_shares(): pl.pallas_call(functools.partial(chip_kernel, groups, shares), out_shape=...  0.96 us
    pallas_call x1, Pallas kernels, combine(): pl.pallas_call(combine_kernel, out_shape=jax.ShapeDtypeStruct((count, sha...  0.69 us
  transfers between devices with their start and end apart: 7, of which 3 were waited for; matrix products, arithmetic and copies ran while one was open for 0% of the time, Pallas kernels for 25%

profile of v16, /device:TPU:0, one launch (start us, length us, event | category | flops | bytes accessed | tf_op | source)
XLA Modules:
  0.0 21.4 jit_solution(8549377207773931854)
XLA Ops:
  0.0 0.5 %collective-permute-start.3 = (bf16[2,16,2048]{2,1,0:T(8,128)(2,1)}, bf16[2,16,2048]{2,1,0:T(8,128)(2,1)S(1)}, u32[]{:S(2)}, u32[]{:S(2)}) collective-permute-start(bf16[2,16,2048]{2,1,0:T(8,128)(2,1)} %bitcast.4), channel_id=1, source_target_pairs={{0,1},{1,0},{2,3},{3,2},{4,8},{5,9},{6,10},{7,11},{8,4},{9,5},{10,... | collective-permute-start | bytes 393224 | tf_op jit(solution)/shard_map/ppermute | solution.py:457
  0.5 4.0 %collective-permute-start.2 = (bf16[2,16,2048]{2,1,0:T(8,128)(2,1)}, bf16[2,16,2048]{2,1,0:T(8,128)(2,1)S(1)}, u32[]{:S(2)}, u32[]{:S(2)}) collective-permute-start(bf16[2,16,2048]{2,1,0:T(8,128)(2,1)} %bitcast.5), channel_id=1, source_target_pairs={{0,4},{1,5},{2,6},{3,7},{4,0},{5,1},{6,2},{7,3},{8,12},{9,13},{10,... | collective-permute-start | bytes 393224 | tf_op jit(solution)/shard_map/ppermute | solution.py:457
  4.5 1.6 %collective-permute-start.1 = (bf16[2,16,2048]{2,1,0:T(8,128)(2,1)}, bf16[2,16,2048]{2,1,0:T(8,128)(2,1)S(1)}, u32[]{:S(2)}, u32[]{:S(2)}) collective-permute-start(bf16[2,16,2048]{2,1,0:T(8,128)(2,1)} %bitcast.6), channel_id=1, source_target_pairs={{0,8},{1,9},{2,10},{3,11},{4,12},{5,13},{6,14},{7,15},{8,0},{9,1},... | collective-permute-start | bytes 393224 | tf_op jit(solution)/shard_map/ppermute | solution.py:457
  6.1 0.0 collective-permute-start
  6.1 4.3 %tables.1 = (bf16[80,96,256]{2,1,0:T(8,128)(2,1)S(1)}, bf16[80,96,128]{2,1,0:T(8,128)(2,1)S(1)}, bf16[2,256,128]{2,1,0:T(8,128)(2,1)S(1)}) custom-call(bf16[2,16,2048]{2,1,0:T(8,128)(2,1)} %bitcast.8, bf16[5,3,16,1024]{3,2,1,0:T(8,128)(2,1)} %gradient_hbm.1, f32[270,1,16]{2,1,0:T(1,128)} %bitcast.3), custom_call_target="tpu_custom_call" | custom-call | flops 200000000 | bytes 6000000 | tf_op jit(solution)/shard_map/tables/pallas_call | solution.py:171
  10.4 0.0 collective-permute-done.3.near_odd
  10.4 0.0 collective-permute-done.2.near_even
  10.4 0.2 collective-permute-done.1.far_even
  10.6 0.0 collective-permute-done.far_odd
  10.6 4.6 %sandwich.1 = (bf16[128,128]{1,0:T(8,128)(2,1)S(1)}, bf16[128,128]{1,0:T(8,128)(2,1)S(1)}, bf16[128,128]{1,0:T(8,128)(2,1)S(1)}, bf16[20,128,256]{2,1,0:T(8,128)(2,1)S(1)}) custom-call(s32[5,16]{1,0:T(8,128)} %bitcast.9, s32[3]{0:T(128)} %offsets_hbm.1, bf16[2,256,128]{2,1,0:T(8,128)(2,1)S(1)} %get-tuple-element.12.middle_planes, ...), custom_call_target="tpu_custom_call" | custom-call | flops 800000000 | bytes 7000000 | tf_op jit(solution)/shard_map/sandwich/pallas_call | solution.py:360
  15.2 0.4 %collective-permute-start.4 = (bf16[128,128]{1,0:T(8,128)(2,1)S(1)}, bf16[128,128]{1,0:T(8,128)(2,1)S(1)}, u32[]{:S(2)}, u32[]{:S(2)}) collective-permute-start(bf16[128,128]{1,0:T(8,128)(2,1)S(1)} %get-tuple-element.16), channel_id=1, source_target_pairs={{0,1},{1,0},{2,3},{3,2},{4,5},{5,4},{6,7},{7,6},{8,9},{9,8},{10,11... | collective-permute-start | bytes 98312 | tf_op jit(solution)/shard_map/ppermute | solution.py:475
  15.6 1.5 %collective-permute-start.5 = (bf16[128,128]{1,0:T(8,128)(2,1)S(1)}, bf16[128,128]{1,0:T(8,128)(2,1)S(1)}, u32[]{:S(2)}, u32[]{:S(2)}) collective-permute-start(bf16[128,128]{1,0:T(8,128)(2,1)S(1)} %get-tuple-element.17), channel_id=1, source_target_pairs={{0,2},{1,3},{2,0},{3,1},{4,6},{5,7},{6,4},{7,5},{8,10},{9,11},{10,... | collective-permute-start | bytes 98312 | tf_op jit(solution)/shard_map/ppermute | solution.py:475
  17.1 0.0 collective-permute-start.6
  17.1 1.0 %chip_shares.1.own = f32[128,128]{1,0:T(8,128)S(1)} custom-call(bf16[20,128,256]{2,1,0:T(8,128)(2,1)S(1)} %get-tuple-element.15.blocks, bf16[80,96,256]{2,1,0:T(8,128)(2,1)S(1)} %get-tuple-element.13.kernel, bf16[80,96,128]{2,1,0:T(8,128)(2,1)S(1)} %get-tuple-element.14.derivs), custom_call_target="tpu_custom_call" | custom-call | flops 400000000 | bytes 4000000 | tf_op jit(solution)/shard_map/chip_shares/pallas_call | solution.py:401
  18.1 0.0 collective-permute-done.4.refs_0_
  18.1 1.4 %collective-permute-done.5.refs_1_ = bf16[128,128]{1,0:T(8,128)(2,1)S(1)} collective-permute-done((bf16[128,128]{1,0:T(8,128)(2,1)S(1)}, bf16[128,128]{1,0:T(8,128)(2,1)S(1)}, u32[]{:S(2)}, u32[]{:S(2)}) %collective-permute-start.5) | collective-permute-done | bytes 32800 | tf_op jit(solution)/shard_map/ppermute | solution.py:475
  19.5 1.2 %collective-permute-done.6.refs_2_ = bf16[128,128]{1,0:T(8,128)(2,1)S(1)} collective-permute-done((bf16[128,128]{1,0:T(8,128)(2,1)S(1)}, bf16[128,128]{1,0:T(8,128)(2,1)S(1)}, u32[]{:S(2)}, u32[]{:S(2)}) %collective-permute-start.6) | collective-permute-done | bytes 32800 | tf_op jit(solution)/shard_map/ppermute | solution.py:475
  20.7 0.7 %combine.1 = f32[2,4,2048]{2,1,0:T(4,128)} custom-call(f32[128,128]{1,0:T(8,128)S(1)} %chip_shares.1.own, bf16[128,128]{1,0:T(8,128)(2,1)S(1)} %collective-permute-done.4.refs_0_, bf16[128,128]{1,0:T(8,128)(2,1)S(1)} %collective-permute-done.5.refs_1_, bf16[128,128]{1,0:T(8,128)(2,1)S(1)} %collective-permute-done.6.refs_2_), custom_call_target="tpu_custom_call" | custom-call | tf_op jit(solution)/shard_map/combine/pallas_call | solution.py:431
Async XLA Ops:
  0.0 10.4 %collective-permute-start.3 = (bf16[2,16,2048]{2,1,0:T(8,128)(2,1)}, bf16[2,16,2048]{2,1,0:T(8,128)(2,1)S(1)}, u32[]{:S(2)}, u32[]{:S(2)}) collective-permute-start(bf16[2,16,2048]{2,1,0:T(8,128)(2,1)} %bitcast.4), channel_id=1, source_target_pairs={{0,1},{1,0},{2,3},{3,2},{4,8},{5,9},{6,10},{7,11},{8,4},{9,5},{10,... | collective-permute-start | bytes 393224 | tf_op jit(solution)/shard_map/ppermute | solution.py:457
  0.5 10.0 %collective-permute-start.2 = (bf16[2,16,2048]{2,1,0:T(8,128)(2,1)}, bf16[2,16,2048]{2,1,0:T(8,128)(2,1)S(1)}, u32[]{:S(2)}, u32[]{:S(2)}) collective-permute-start(bf16[2,16,2048]{2,1,0:T(8,128)(2,1)} %bitcast.5), channel_id=1, source_target_pairs={{0,4},{1,5},{2,6},{3,7},{4,0},{5,1},{6,2},{7,3},{8,12},{9,13},{10,... | collective-permute-start | bytes 393224 | tf_op jit(solution)/shard_map/ppermute | solution.py:457
  4.5 6.1 %collective-permute-start.1 = (bf16[2,16,2048]{2,1,0:T(8,128)(2,1)}, bf16[2,16,2048]{2,1,0:T(8,128)(2,1)S(1)}, u32[]{:S(2)}, u32[]{:S(2)}) collective-permute-start(bf16[2,16,2048]{2,1,0:T(8,128)(2,1)} %bitcast.6), channel_id=1, source_target_pairs={{0,8},{1,9},{2,10},{3,11},{4,12},{5,13},{6,14},{7,15},{8,0},{9,1},... | collective-permute-start | bytes 393224 | tf_op jit(solution)/shard_map/ppermute | solution.py:457
  6.1 4.6 %collective-permute-start = (bf16[2,16,2048]{2,1,0:T(8,128)(2,1)}, bf16[2,16,2048]{2,1,0:T(8,128)(2,1)S(1)}, u32[]{:S(2)}, u32[]{:S(2)}) collective-permute-start(bf16[2,16,2048]{2,1,0:T(8,128)(2,1)} %bitcast.7), channel_id=1, source_target_pairs={{0,1},{1,0},{2,3},{3,2},{4,5},{5,4},{6,7},{7,6},{8,16},{9,17},{10,... | collective-permute-start | bytes 393224 | tf_op jit(solution)/shard_map/ppermute | solution.py:457
  15.2 2.9 %collective-permute-start.4 = (bf16[128,128]{1,0:T(8,128)(2,1)S(1)}, bf16[128,128]{1,0:T(8,128)(2,1)S(1)}, u32[]{:S(2)}, u32[]{:S(2)}) collective-permute-start(bf16[128,128]{1,0:T(8,128)(2,1)S(1)} %get-tuple-element.16), channel_id=1, source_target_pairs={{0,1},{1,0},{2,3},{3,2},{4,5},{5,4},{6,7},{7,6},{8,9},{9,8},{10,11... | collective-permute-start | bytes 98312 | tf_op jit(solution)/shard_map/ppermute | solution.py:475
  15.6 3.9 %collective-permute-start.5 = (bf16[128,128]{1,0:T(8,128)(2,1)S(1)}, bf16[128,128]{1,0:T(8,128)(2,1)S(1)}, u32[]{:S(2)}, u32[]{:S(2)}) collective-permute-start(bf16[128,128]{1,0:T(8,128)(2,1)S(1)} %get-tuple-element.17), channel_id=1, source_target_pairs={{0,2},{1,3},{2,0},{3,1},{4,6},{5,7},{6,4},{7,5},{8,10},{9,11},{10,... | collective-permute-start | bytes 98312 | tf_op jit(solution)/shard_map/ppermute | solution.py:475
  17.1 3.6 %collective-permute-start.6 = (bf16[128,128]{1,0:T(8,128)(2,1)S(1)}, bf16[128,128]{1,0:T(8,128)(2,1)S(1)}, u32[]{:S(2)}, u32[]{:S(2)}) collective-permute-start(bf16[128,128]{1,0:T(8,128)(2,1)S(1)} %get-tuple-element.18), channel_id=1, source_target_pairs={{0,3},{1,2},{2,1},{3,0},{4,7},{5,6},{6,5},{7,4},{8,11},{9,10},{10,... | collective-permute-start | bytes 98312 | tf_op jit(solution)/shard_map/ppermute | solution.py:475

commit v17 on v15

--- a/solution.py
+++ b/solution.py
@@ -162,7 +162,7 @@
                 kernel_out[at, i * NO : (i + 1) * NO, half * LANES : (half + 1) * LANES] = total
         return carry
 
-    lax.fori_loop(0, natoms * NB, one_cell, 0, unroll=4)
+    lax.fori_loop(0, natoms * NB, one_cell, 0, unroll=16)
 
 
 def tables(local, gradient, coupling):

time: 21.2 us -> 21.1 us (level)
  no operation moved by 1% of the time
where the time goes in v17:
time: 21.1 us; the launch traced here: 20.9 us
  Pallas kernels  10.4 us (49%)
  starting transfers between devices  8.27 us (39%)
  waiting for transfers between devices  2.27 us (11%)
    ppermute x4, starting transfers between devices, exchanged(): return lax.ppermute(array, ('energy', 'mom'), pairs)  6.07 us
    pallas_call x1, Pallas kernels, sandwich(): pl.pallas_call(functools.partial(sandwich_kernel, count, natoms, shares),...  4.44 us
    pallas_call x1, Pallas kernels, tables(): pl.pallas_call(functools.partial(tables_kernel, natoms), out_shape=(jax.S...  4.28 us
    ppermute x3, starting transfers between devices, sent(): return lax.ppermute(term, 'mom', pairs)  2.21 us
    ppermute x3, waiting for transfers between devices, sent(): return lax.ppermute(term, 'mom', pairs)  2 us
    pallas_call x1, Pallas kernels, chip_shares(): pl.pallas_call(functools.partial(chip_kernel, groups, shares), out_shape=...  0.96 us
    pallas_call x1, Pallas kernels, combine(): pl.pallas_call(combine_kernel, out_shape=jax.ShapeDtypeStruct((count, sha...  0.69 us
  transfers between devices with their start and end apart: 7, of which 3 were waited for; matrix products, arithmetic and copies ran while one was open for 0% of the time, Pallas kernels for 25%

profile of v17, /device:TPU:0, one launch (start us, length us, event | category | flops | bytes accessed | tf_op | source)
XLA Modules:
  0.0 20.9 jit_solution(4585099938702964471)
XLA Ops:
  0.0 0.5 %collective-permute-start.3 = (bf16[2,16,2048]{2,1,0:T(8,128)(2,1)}, bf16[2,16,2048]{2,1,0:T(8,128)(2,1)S(1)}, u32[]{:S(2)}, u32[]{:S(2)}) collective-permute-start(bf16[2,16,2048]{2,1,0:T(8,128)(2,1)} %bitcast.4), channel_id=1, source_target_pairs={{0,1},{1,0},{2,3},{3,2},{4,8},{5,9},{6,10},{7,11},{8,4},{9,5},{10,... | collective-permute-start | bytes 393224 | tf_op jit(solution)/shard_map/ppermute | solution.py:457
  0.5 3.9 %collective-permute-start.2 = (bf16[2,16,2048]{2,1,0:T(8,128)(2,1)}, bf16[2,16,2048]{2,1,0:T(8,128)(2,1)S(1)}, u32[]{:S(2)}, u32[]{:S(2)}) collective-permute-start(bf16[2,16,2048]{2,1,0:T(8,128)(2,1)} %bitcast.5), channel_id=1, source_target_pairs={{0,8},{1,9},{2,10},{3,11},{4,12},{5,13},{6,14},{7,15},{8,0},{9,1},... | collective-permute-start | bytes 393224 | tf_op jit(solution)/shard_map/ppermute | solution.py:457
  4.4 0.0 collective-permute-start.1
  4.4 1.7 %collective-permute-start = (bf16[2,16,2048]{2,1,0:T(8,128)(2,1)}, bf16[2,16,2048]{2,1,0:T(8,128)(2,1)S(1)}, u32[]{:S(2)}, u32[]{:S(2)}) collective-permute-start(bf16[2,16,2048]{2,1,0:T(8,128)(2,1)} %bitcast.7), channel_id=1, source_target_pairs={{0,4},{1,5},{2,6},{3,7},{4,0},{5,1},{6,2},{7,3},{8,12},{9,13},{10,... | collective-permute-start | bytes 393224 | tf_op jit(solution)/shard_map/ppermute | solution.py:457
  6.1 4.3 %tables.1 = (bf16[80,96,256]{2,1,0:T(8,128)(2,1)S(1)}, bf16[80,96,128]{2,1,0:T(8,128)(2,1)S(1)}, bf16[2,256,128]{2,1,0:T(8,128)(2,1)S(1)}) custom-call(bf16[2,16,2048]{2,1,0:T(8,128)(2,1)} %bitcast.8, bf16[5,3,16,1024]{3,2,1,0:T(8,128)(2,1)} %gradient_hbm.1, f32[270,1,16]{2,1,0:T(1,128)} %bitcast.3), custom_call_target="tpu_custom_call" | custom-call | flops 200000000 | bytes 6000000 | tf_op jit(solution)/shard_map/tables/pallas_call | solution.py:171
  10.4 0.0 collective-permute-done.3.near_odd
  10.4 0.3 %collective-permute-done.2.far_even = bf16[2,16,2048]{2,1,0:T(8,128)(2,1)S(1)} collective-permute-done((bf16[2,16,2048]{2,1,0:T(8,128)(2,1)}, bf16[2,16,2048]{2,1,0:T(8,128)(2,1)S(1)}, u32[]{:S(2)}, u32[]{:S(2)}) %collective-permute-start.2) | collective-permute-done | bytes 131104 | tf_op jit(solution)/shard_map/ppermute | solution.py:457
  10.6 0.0 collective-permute-done.1.far_odd
  10.6 0.0 collective-permute-done.near_even
  10.6 4.4 %sandwich.1 = (bf16[128,128]{1,0:T(8,128)(2,1)S(1)}, bf16[128,128]{1,0:T(8,128)(2,1)S(1)}, bf16[128,128]{1,0:T(8,128)(2,1)S(1)}, bf16[20,128,256]{2,1,0:T(8,128)(2,1)S(1)}) custom-call(s32[5,16]{1,0:T(8,128)} %bitcast.9, s32[3]{0:T(128)} %offsets_hbm.1, bf16[2,256,128]{2,1,0:T(8,128)(2,1)S(1)} %get-tuple-element.12.middle_planes, ...), custom_call_target="tpu_custom_call" | custom-call | flops 800000000 | bytes 7000000 | tf_op jit(solution)/shard_map/sandwich/pallas_call | solution.py:360
  15.1 1.6 %collective-permute-start.4 = (bf16[128,128]{1,0:T(8,128)(2,1)S(1)}, bf16[128,128]{1,0:T(8,128)(2,1)S(1)}, u32[]{:S(2)}, u32[]{:S(2)}) collective-permute-start(bf16[128,128]{1,0:T(8,128)(2,1)S(1)} %get-tuple-element.16), channel_id=1, source_target_pairs={{0,2},{1,3},{2,0},{3,1},{4,6},{5,7},{6,4},{7,5},{8,10},{9,11},{10,... | collective-permute-start | bytes 98312 | tf_op jit(solution)/shard_map/ppermute | solution.py:475
  16.7 0.0 collective-permute-start.5
  16.7 0.6 %collective-permute-start.6 = (bf16[128,128]{1,0:T(8,128)(2,1)S(1)}, bf16[128,128]{1,0:T(8,128)(2,1)S(1)}, u32[]{:S(2)}, u32[]{:S(2)}) collective-permute-start(bf16[128,128]{1,0:T(8,128)(2,1)S(1)} %get-tuple-element.18), channel_id=1, source_target_pairs={{0,1},{1,0},{2,3},{3,2},{4,5},{5,4},{6,7},{7,6},{8,9},{9,8},{10,11... | collective-permute-start | bytes 98312 | tf_op jit(solution)/shard_map/ppermute | solution.py:475
  17.3 1.0 %chip_shares.1.own = f32[128,128]{1,0:T(8,128)S(1)} custom-call(bf16[20,128,256]{2,1,0:T(8,128)(2,1)S(1)} %get-tuple-element.15.blocks, bf16[80,96,256]{2,1,0:T(8,128)(2,1)S(1)} %get-tuple-element.13.kernel, bf16[80,96,128]{2,1,0:T(8,128)(2,1)S(1)} %get-tuple-element.14.derivs), custom_call_target="tpu_custom_call" | custom-call | flops 400000000 | bytes 4000000 | tf_op jit(solution)/shard_map/chip_shares/pallas_call | solution.py:401
  18.3 0.8 %collective-permute-done.4.refs_0_ = bf16[128,128]{1,0:T(8,128)(2,1)S(1)} collective-permute-done((bf16[128,128]{1,0:T(8,128)(2,1)S(1)}, bf16[128,128]{1,0:T(8,128)(2,1)S(1)}, u32[]{:S(2)}, u32[]{:S(2)}) %collective-permute-start.4) | collective-permute-done | bytes 32800 | tf_op jit(solution)/shard_map/ppermute | solution.py:475
  19.1 1.2 %collective-permute-done.5.refs_1_ = bf16[128,128]{1,0:T(8,128)(2,1)S(1)} collective-permute-done((bf16[128,128]{1,0:T(8,128)(2,1)S(1)}, bf16[128,128]{1,0:T(8,128)(2,1)S(1)}, u32[]{:S(2)}, u32[]{:S(2)}) %collective-permute-start.5) | collective-permute-done | bytes 32800 | tf_op jit(solution)/shard_map/ppermute | solution.py:475
  20.2 0.0 collective-permute-done.6.refs_2_
  20.3 0.7 %combine.1 = f32[2,4,2048]{2,1,0:T(4,128)} custom-call(f32[128,128]{1,0:T(8,128)S(1)} %chip_shares.1.own, bf16[128,128]{1,0:T(8,128)(2,1)S(1)} %collective-permute-done.4.refs_0_, bf16[128,128]{1,0:T(8,128)(2,1)S(1)} %collective-permute-done.5.refs_1_, bf16[128,128]{1,0:T(8,128)(2,1)S(1)} %collective-permute-done.6.refs_2_), custom_call_target="tpu_custom_call" | custom-call | tf_op jit(solution)/shard_map/combine/pallas_call | solution.py:431
Async XLA Ops:
  0.0 10.4 %collective-permute-start.3 = (bf16[2,16,2048]{2,1,0:T(8,128)(2,1)}, bf16[2,16,2048]{2,1,0:T(8,128)(2,1)S(1)}, u32[]{:S(2)}, u32[]{:S(2)}) collective-permute-start(bf16[2,16,2048]{2,1,0:T(8,128)(2,1)} %bitcast.4), channel_id=1, source_target_pairs={{0,1},{1,0},{2,3},{3,2},{4,8},{5,9},{6,10},{7,11},{8,4},{9,5},{10,... | collective-permute-start | bytes 393224 | tf_op jit(solution)/shard_map/ppermute | solution.py:457
  0.5 10.2 %collective-permute-start.2 = (bf16[2,16,2048]{2,1,0:T(8,128)(2,1)}, bf16[2,16,2048]{2,1,0:T(8,128)(2,1)S(1)}, u32[]{:S(2)}, u32[]{:S(2)}) collective-permute-start(bf16[2,16,2048]{2,1,0:T(8,128)(2,1)} %bitcast.5), channel_id=1, source_target_pairs={{0,8},{1,9},{2,10},{3,11},{4,12},{5,13},{6,14},{7,15},{8,0},{9,1},... | collective-permute-start | bytes 393224 | tf_op jit(solution)/shard_map/ppermute | solution.py:457
  4.4 6.2 %collective-permute-start.1 = (bf16[2,16,2048]{2,1,0:T(8,128)(2,1)}, bf16[2,16,2048]{2,1,0:T(8,128)(2,1)S(1)}, u32[]{:S(2)}, u32[]{:S(2)}) collective-permute-start(bf16[2,16,2048]{2,1,0:T(8,128)(2,1)} %bitcast.6), channel_id=1, source_target_pairs={{0,1},{1,0},{2,3},{3,2},{4,5},{5,4},{6,7},{7,6},{8,16},{9,17},{10,... | collective-permute-start | bytes 393224 | tf_op jit(solution)/shard_map/ppermute | solution.py:457
  4.4 6.2 %collective-permute-start = (bf16[2,16,2048]{2,1,0:T(8,128)(2,1)}, bf16[2,16,2048]{2,1,0:T(8,128)(2,1)S(1)}, u32[]{:S(2)}, u32[]{:S(2)}) collective-permute-start(bf16[2,16,2048]{2,1,0:T(8,128)(2,1)} %bitcast.7), channel_id=1, source_target_pairs={{0,4},{1,5},{2,6},{3,7},{4,0},{5,1},{6,2},{7,3},{8,12},{9,13},{10,... | collective-permute-start | bytes 393224 | tf_op jit(solution)/shard_map/ppermute | solution.py:457
  15.1 4.0 %collective-permute-start.4 = (bf16[128,128]{1,0:T(8,128)(2,1)S(1)}, bf16[128,128]{1,0:T(8,128)(2,1)S(1)}, u32[]{:S(2)}, u32[]{:S(2)}) collective-permute-start(bf16[128,128]{1,0:T(8,128)(2,1)S(1)} %get-tuple-element.16), channel_id=1, source_target_pairs={{0,2},{1,3},{2,0},{3,1},{4,6},{5,7},{6,4},{7,5},{8,10},{9,11},{10,... | collective-permute-start | bytes 98312 | tf_op jit(solution)/shard_map/ppermute | solution.py:475
  16.7 3.6 %collective-permute-start.5 = (bf16[128,128]{1,0:T(8,128)(2,1)S(1)}, bf16[128,128]{1,0:T(8,128)(2,1)S(1)}, u32[]{:S(2)}, u32[]{:S(2)}) collective-permute-start(bf16[128,128]{1,0:T(8,128)(2,1)S(1)} %get-tuple-element.17), channel_id=1, source_target_pairs={{0,3},{1,2},{2,1},{3,0},{4,7},{5,6},{6,5},{7,4},{8,11},{9,10},{10,... | collective-permute-start | bytes 98312 | tf_op jit(solution)/shard_map/ppermute | solution.py:475
  16.7 3.6 %collective-permute-start.6 = (bf16[128,128]{1,0:T(8,128)(2,1)S(1)}, bf16[128,128]{1,0:T(8,128)(2,1)S(1)}, u32[]{:S(2)}, u32[]{:S(2)}) collective-permute-start(bf16[128,128]{1,0:T(8,128)(2,1)S(1)} %get-tuple-element.18), channel_id=1, source_target_pairs={{0,1},{1,0},{2,3},{3,2},{4,5},{5,4},{6,7},{7,6},{8,9},{9,8},{10,11... | collective-permute-start | bytes 98312 | tf_op jit(solution)/shard_map/ppermute | solution.py:475

commit v18 on v15

--- a/solution.py
+++ b/solution.py
@@ -113,7 +113,8 @@
     for s in range(1, NS):
         chosen = chosen | (lane == s * cells)
 
-    copies[0].wait()
+    for copy in copies:
+        copy.wait()
     table = jnp.transpose(coupling[...])
     table = jnp.concatenate(
         [table, jnp.zeros((natoms, width - NS * cells), jnp.float32)], axis=1
@@ -129,7 +130,6 @@
                 at * depth : (at + 1) * depth, half * LANES : (half + 1) * LANES
             ]
 
-    copies[1].wait()
     flats = [stack_tiles(gradient[slot, j]) for slot in range(NB) for j in range(ND)]
     ordered = dot(order, jnp.concatenate(flats, axis=1)).astype(jnp.bfloat16)
     stacked = [ordered[:, at : at + LANES] for at in range(0, NB * ND * LANES, LANES)]
@@ -146,7 +146,6 @@
                     axis=0,
                 ).astype(jnp.bfloat16)
 
-    copies[2].wait()
     make_planes(local, planes_out, 0, row_matrix(2 * tiles, natoms))
 
     def one_cell(at, carry):

time: 21.2 us -> 20.9 us (0.986)
  Pallas kernels: 10.4 us -> 10.1 us
    ppermute x4, waiting for transfers between devices: 0.22 us -> 0.58 us  [exchanged(): return lax.ppermute(array, ('energy', 'mom'), pairs)]
    pallas_call x1, Pallas kernels: 4.33 us -> 3.97 us  [tables(): pl.pallas_call(functools.partial(tables_kernel, natoms), out_shape=(jax.S...]
    ppermute x3, waiting for transfers between devices: 2.05 us -> 1.76 us  [sent(): return lax.ppermute(term, 'mom', pairs)]
  transfers between devices with their start and end apart: 7 -> 7, of which waited for: 3 -> 3; matrix products, arithmetic and copies ran while one was open for 0% -> 0% of each run, Pallas kernels for 25% -> 24%
where the time goes in v18:
time: 20.9 us; the launch traced here: 20.7 us
  Pallas kernels  10.1 us (48%)
  starting transfers between devices  8.27 us (40%)
  waiting for transfers between devices  2.34 us (11%)
    ppermute x4, starting transfers between devices, exchanged(): return lax.ppermute(array, ('energy', 'mom'), pairs)  6.07 us
    pallas_call x1, Pallas kernels, sandwich(): pl.pallas_call(functools.partial(sandwich_kernel, count, natoms, shares),...  4.44 us
    pallas_call x1, Pallas kernels, tables(): pl.pallas_call(functools.partial(tables_kernel, natoms), out_shape=(jax.S...  3.97 us
    ppermute x3, starting transfers between devices, sent(): return lax.ppermute(term, 'mom', pairs)  2.21 us
    ppermute x3, waiting for transfers between devices, sent(): return lax.ppermute(term, 'mom', pairs)  1.76 us
    pallas_call x1, Pallas kernels, chip_shares(): pl.pallas_call(functools.partial(chip_kernel, groups, shares), out_shape=...  0.96 us
    pallas_call x1, Pallas kernels, combine(): pl.pallas_call(combine_kernel, out_shape=jax.ShapeDtypeStruct((count, sha...  0.69 us
    ppermute x4, waiting for transfers between devices, exchanged(): return lax.ppermute(array, ('energy', 'mom'), pairs)  0.58 us
  transfers between devices with their start and end apart: 7, of which 3 were waited for; matrix products, arithmetic and copies ran while one was open for 0% of the time, Pallas kernels for 24%

profile of v18, /device:TPU:0, one launch (start us, length us, event | category | flops | bytes accessed | tf_op | source)
XLA Modules:
  0.0 20.7 jit_solution(2914924008242306806)
XLA Ops:
  0.0 0.5 %collective-permute-start.3 = (bf16[2,16,2048]{2,1,0:T(8,128)(2,1)}, bf16[2,16,2048]{2,1,0:T(8,128)(2,1)S(1)}, u32[]{:S(2)}, u32[]{:S(2)}) collective-permute-start(bf16[2,16,2048]{2,1,0:T(8,128)(2,1)} %bitcast.4), channel_id=1, source_target_pairs={{0,1},{1,0},{2,3},{3,2},{4,8},{5,9},{6,10},{7,11},{8,4},{9,5},{10,... | collective-permute-start | bytes 393224 | tf_op jit(solution)/shard_map/ppermute | solution.py:456
  0.5 3.9 %collective-permute-start.2 = (bf16[2,16,2048]{2,1,0:T(8,128)(2,1)}, bf16[2,16,2048]{2,1,0:T(8,128)(2,1)S(1)}, u32[]{:S(2)}, u32[]{:S(2)}) collective-permute-start(bf16[2,16,2048]{2,1,0:T(8,128)(2,1)} %bitcast.5), channel_id=1, source_target_pairs={{0,8},{1,9},{2,10},{3,11},{4,12},{5,13},{6,14},{7,15},{8,0},{9,1},... | collective-permute-start | bytes 393224 | tf_op jit(solution)/shard_map/ppermute | solution.py:456
  4.4 0.0 collective-permute-start.1
  4.4 1.7 %collective-permute-start = (bf16[2,16,2048]{2,1,0:T(8,128)(2,1)}, bf16[2,16,2048]{2,1,0:T(8,128)(2,1)S(1)}, u32[]{:S(2)}, u32[]{:S(2)}) collective-permute-start(bf16[2,16,2048]{2,1,0:T(8,128)(2,1)} %bitcast.7), channel_id=1, source_target_pairs={{0,4},{1,5},{2,6},{3,7},{4,0},{5,1},{6,2},{7,3},{8,12},{9,13},{10,... | collective-permute-start | bytes 393224 | tf_op jit(solution)/shard_map/ppermute | solution.py:456
  6.1 4.0 %tables.1 = (bf16[80,96,256]{2,1,0:T(8,128)(2,1)S(1)}, bf16[80,96,128]{2,1,0:T(8,128)(2,1)S(1)}, bf16[2,256,128]{2,1,0:T(8,128)(2,1)S(1)}) custom-call(bf16[2,16,2048]{2,1,0:T(8,128)(2,1)} %bitcast.8, bf16[5,3,16,1024]{3,2,1,0:T(8,128)(2,1)} %gradient_hbm.1, f32[270,1,16]{2,1,0:T(1,128)} %bitcast.3), custom_call_target="tpu_custom_call" | custom-call | flops 200000000 | bytes 6000000 | tf_op jit(solution)/shard_map/tables/pallas_call | solution.py:170
  10.0 0.0 collective-permute-done.3.near_odd
  10.1 0.6 %collective-permute-done.2.far_even = bf16[2,16,2048]{2,1,0:T(8,128)(2,1)S(1)} collective-permute-done((bf16[2,16,2048]{2,1,0:T(8,128)(2,1)}, bf16[2,16,2048]{2,1,0:T(8,128)(2,1)S(1)}, u32[]{:S(2)}, u32[]{:S(2)}) %collective-permute-start.2) | collective-permute-done | bytes 131104 | tf_op jit(solution)/shard_map/ppermute | solution.py:456
  10.6 0.0 collective-permute-done.1.far_odd
  10.6 0.0 collective-permute-done.near_even
  10.6 4.4 %sandwich.1 = (bf16[128,128]{1,0:T(8,128)(2,1)S(1)}, bf16[128,128]{1,0:T(8,128)(2,1)S(1)}, bf16[128,128]{1,0:T(8,128)(2,1)S(1)}, bf16[20,128,256]{2,1,0:T(8,128)(2,1)S(1)}) custom-call(s32[5,16]{1,0:T(8,128)} %bitcast.9, s32[3]{0:T(128)} %offsets_hbm.1, bf16[2,256,128]{2,1,0:T(8,128)(2,1)S(1)} %get-tuple-element.12.middle_planes, ...), custom_call_target="tpu_custom_call" | custom-call | flops 800000000 | bytes 7000000 | tf_op jit(solution)/shard_map/sandwich/pallas_call | solution.py:359
  15.1 1.6 %collective-permute-start.4 = (bf16[128,128]{1,0:T(8,128)(2,1)S(1)}, bf16[128,128]{1,0:T(8,128)(2,1)S(1)}, u32[]{:S(2)}, u32[]{:S(2)}) collective-permute-start(bf16[128,128]{1,0:T(8,128)(2,1)S(1)} %get-tuple-element.16), channel_id=1, source_target_pairs={{0,2},{1,3},{2,0},{3,1},{4,6},{5,7},{6,4},{7,5},{8,10},{9,11},{10,... | collective-permute-start | bytes 98312 | tf_op jit(solution)/shard_map/ppermute | solution.py:474
  16.7 0.0 collective-permute-start.5
  16.7 0.6 %collective-permute-start.6 = (bf16[128,128]{1,0:T(8,128)(2,1)S(1)}, bf16[128,128]{1,0:T(8,128)(2,1)S(1)}, u32[]{:S(2)}, u32[]{:S(2)}) collective-permute-start(bf16[128,128]{1,0:T(8,128)(2,1)S(1)} %get-tuple-element.18), channel_id=1, source_target_pairs={{0,1},{1,0},{2,3},{3,2},{4,5},{5,4},{6,7},{7,6},{8,9},{9,8},{10,11... | collective-permute-start | bytes 98312 | tf_op jit(solution)/shard_map/ppermute | solution.py:474
  17.3 1.0 %chip_shares.1.own = f32[128,128]{1,0:T(8,128)S(1)} custom-call(bf16[20,128,256]{2,1,0:T(8,128)(2,1)S(1)} %get-tuple-element.15.blocks, bf16[80,96,256]{2,1,0:T(8,128)(2,1)S(1)} %get-tuple-element.13.kernel, bf16[80,96,128]{2,1,0:T(8,128)(2,1)S(1)} %get-tuple-element.14.derivs), custom_call_target="tpu_custom_call" | custom-call | flops 400000000 | bytes 4000000 | tf_op jit(solution)/shard_map/chip_shares/pallas_call | solution.py:400
  18.3 0.8 %collective-permute-done.4.refs_0_ = bf16[128,128]{1,0:T(8,128)(2,1)S(1)} collective-permute-done((bf16[128,128]{1,0:T(8,128)(2,1)S(1)}, bf16[128,128]{1,0:T(8,128)(2,1)S(1)}, u32[]{:S(2)}, u32[]{:S(2)}) %collective-permute-start.4) | collective-permute-done | bytes 32800 | tf_op jit(solution)/shard_map/ppermute | solution.py:474
  19.1 0.9 %collective-permute-done.5.refs_1_ = bf16[128,128]{1,0:T(8,128)(2,1)S(1)} collective-permute-done((bf16[128,128]{1,0:T(8,128)(2,1)S(1)}, bf16[128,128]{1,0:T(8,128)(2,1)S(1)}, u32[]{:S(2)}, u32[]{:S(2)}) %collective-permute-start.5) | collective-permute-done | bytes 32800 | tf_op jit(solution)/shard_map/ppermute | solution.py:474
  20.0 0.0 collective-permute-done.6.refs_2_
  20.0 0.7 %combine.1 = f32[2,4,2048]{2,1,0:T(4,128)} custom-call(f32[128,128]{1,0:T(8,128)S(1)} %chip_shares.1.own, bf16[128,128]{1,0:T(8,128)(2,1)S(1)} %collective-permute-done.4.refs_0_, bf16[128,128]{1,0:T(8,128)(2,1)S(1)} %collective-permute-done.5.refs_1_, bf16[128,128]{1,0:T(8,128)(2,1)S(1)} %collective-permute-done.6.refs_2_), custom_call_target="tpu_custom_call" | custom-call | tf_op jit(solution)/shard_map/combine/pallas_call | solution.py:430
Async XLA Ops:
  0.0 10.0 %collective-permute-start.3 = (bf16[2,16,2048]{2,1,0:T(8,128)(2,1)}, bf16[2,16,2048]{2,1,0:T(8,128)(2,1)S(1)}, u32[]{:S(2)}, u32[]{:S(2)}) collective-permute-start(bf16[2,16,2048]{2,1,0:T(8,128)(2,1)} %bitcast.4), channel_id=1, source_target_pairs={{0,1},{1,0},{2,3},{3,2},{4,8},{5,9},{6,10},{7,11},{8,4},{9,5},{10,... | collective-permute-start | bytes 393224 | tf_op jit(solution)/shard_map/ppermute | solution.py:456
  0.5 10.2 %collective-permute-start.2 = (bf16[2,16,2048]{2,1,0:T(8,128)(2,1)}, bf16[2,16,2048]{2,1,0:T(8,128)(2,1)S(1)}, u32[]{:S(2)}, u32[]{:S(2)}) collective-permute-start(bf16[2,16,2048]{2,1,0:T(8,128)(2,1)} %bitcast.5), channel_id=1, source_target_pairs={{0,8},{1,9},{2,10},{3,11},{4,12},{5,13},{6,14},{7,15},{8,0},{9,1},... | collective-permute-start | bytes 393224 | tf_op jit(solution)/shard_map/ppermute | solution.py:456
  4.4 6.2 %collective-permute-start.1 = (bf16[2,16,2048]{2,1,0:T(8,128)(2,1)}, bf16[2,16,2048]{2,1,0:T(8,128)(2,1)S(1)}, u32[]{:S(2)}, u32[]{:S(2)}) collective-permute-start(bf16[2,16,2048]{2,1,0:T(8,128)(2,1)} %bitcast.6), channel_id=1, source_target_pairs={{0,1},{1,0},{2,3},{3,2},{4,5},{5,4},{6,7},{7,6},{8,16},{9,17},{10,... | collective-permute-start | bytes 393224 | tf_op jit(solution)/shard_map/ppermute | solution.py:456
  4.4 6.2 %collective-permute-start = (bf16[2,16,2048]{2,1,0:T(8,128)(2,1)}, bf16[2,16,2048]{2,1,0:T(8,128)(2,1)S(1)}, u32[]{:S(2)}, u32[]{:S(2)}) collective-permute-start(bf16[2,16,2048]{2,1,0:T(8,128)(2,1)} %bitcast.7), channel_id=1, source_target_pairs={{0,4},{1,5},{2,6},{3,7},{4,0},{5,1},{6,2},{7,3},{8,12},{9,13},{10,... | collective-permute-start | bytes 393224 | tf_op jit(solution)/shard_map/ppermute | solution.py:456
  15.1 4.0 %collective-permute-start.4 = (bf16[128,128]{1,0:T(8,128)(2,1)S(1)}, bf16[128,128]{1,0:T(8,128)(2,1)S(1)}, u32[]{:S(2)}, u32[]{:S(2)}) collective-permute-start(bf16[128,128]{1,0:T(8,128)(2,1)S(1)} %get-tuple-element.16), channel_id=1, source_target_pairs={{0,2},{1,3},{2,0},{3,1},{4,6},{5,7},{6,4},{7,5},{8,10},{9,11},{10,... | collective-permute-start | bytes 98312 | tf_op jit(solution)/shard_map/ppermute | solution.py:474
  16.7 3.3 %collective-permute-start.5 = (bf16[128,128]{1,0:T(8,128)(2,1)S(1)}, bf16[128,128]{1,0:T(8,128)(2,1)S(1)}, u32[]{:S(2)}, u32[]{:S(2)}) collective-permute-start(bf16[128,128]{1,0:T(8,128)(2,1)S(1)} %get-tuple-element.17), channel_id=1, source_target_pairs={{0,3},{1,2},{2,1},{3,0},{4,7},{5,6},{6,5},{7,4},{8,11},{9,10},{10,... | collective-permute-start | bytes 98312 | tf_op jit(solution)/shard_map/ppermute | solution.py:474
  16.7 3.3 %collective-permute-start.6 = (bf16[128,128]{1,0:T(8,128)(2,1)S(1)}, bf16[128,128]{1,0:T(8,128)(2,1)S(1)}, u32[]{:S(2)}, u32[]{:S(2)}) collective-permute-start(bf16[128,128]{1,0:T(8,128)(2,1)S(1)} %get-tuple-element.18), channel_id=1, source_target_pairs={{0,1},{1,0},{2,3},{3,2},{4,5},{5,4},{6,7},{7,6},{8,9},{9,8},{10,11... | collective-permute-start | bytes 98312 | tf_op jit(solution)/shard_map/ppermute | solution.py:474
